TPU v7x, 32 devices: a whole 2x2x4 slice. The times are simulated.
32 devices in a mesh: ctx: 4 (over y, x), fsdp: 8 (over z, core).
Axes of the slice: x: 2, y: 2, z: 4, core: 2. Of those that a mesh axis runs over, the one named last changes fastest.
Arguments:
- activations: bfloat16 [8, 1536, 768], P('fsdp', 'ctx'), may hold values from -6 to 6
- cotangent: bfloat16 [8, 1536, 768], P('fsdp', 'ctx'), may hold values from -6 to 6
- doc_start: int32 [8, 1536], P('fsdp', 'ctx'), may hold values from 0 to 1535, as said below
- deal: int32 [4], replicated, may hold values from 0 to 3, as said below
- attend_in: bfloat16 [2, 768, 2304], P(None, 'fsdp'), may hold values from -0.21875 to 0.21875
- query_bias: bfloat16 [2, 768], P(None, 'fsdp'), may hold values from -3 to 3
- value_bias: bfloat16 [2, 768], P(None, 'fsdp'), may hold values from -3 to 3
- attend_out: bfloat16 [2, 768, 768], P(None, 'fsdp'), may hold values from -1.25 to 1.25
- attend_bias: bfloat16 [2, 768], P(None, 'fsdp'), may hold values from -3 to 3
- first_gain: bfloat16 [2, 768], P(None, 'fsdp'), may hold values from 0.099609375 to 1.8984375
- first_shift: bfloat16 [2, 768], P(None, 'fsdp'), may hold values from -3 to 3
- expand_proj: bfloat16 [2, 768, 3072], P(None, 'fsdp'), may hold values from -0.21875 to 0.21875
- expand_bias: bfloat16 [2, 3072], P(None, 'fsdp'), may hold values from -3 to 3
- reduce_proj: bfloat16 [2, 3072, 768], P(None, 'fsdp'), may hold values from -0.109375 to 0.109375
- reduce_bias: bfloat16 [2, 768], P(None, 'fsdp'), may hold values from -3 to 3
- second_gain: bfloat16 [2, 768], P(None, 'fsdp'), may hold values from 0.099609375 to 1.8984375
- second_shift: bfloat16 [2, 768], P(None, 'fsdp'), may hold values from -3 to 3
Outputs:
- out_act: bfloat16 [8, 1536, 768], P('fsdp', 'ctx')
- in_grad: float32 [8, 1536, 768], P('fsdp', 'ctx')
- attend_in_grad: float32 [2, 768, 2304], P(None, 'fsdp')
- query_bias_grad: float32 [2, 768], P(None, 'fsdp')
- value_bias_grad: float32 [2, 768], P(None, 'fsdp')
- attend_out_grad: float32 [2, 768, 768], P(None, 'fsdp')
- attend_bias_grad: float32 [2, 768], P(None, 'fsdp')
- first_gain_grad: float32 [2, 768], P(None, 'fsdp')
- first_shift_grad: float32 [2, 768], P(None, 'fsdp')
- expand_proj_grad: float32 [2, 768, 3072], P(None, 'fsdp')
- expand_bias_grad: float32 [2, 3072], P(None, 'fsdp')
- reduce_proj_grad: float32 [2, 3072, 768], P(None, 'fsdp')
- reduce_bias_grad: float32 [2, 768], P(None, 'fsdp')
- second_gain_grad: float32 [2, 768], P(None, 'fsdp')
- second_shift_grad: float32 [2, 768], P(None, 'fsdp')
Inputs may be any that keep to these rules, and one draw needn't show every extreme that they name: `doc_start`: rows of one document share the position where it begins; each sequence's first document begins at 0 and covers its first half or more; the last position of a sequence is a document of its own. A permutation of 0 to 3; index c of ctx holds blocks deal[c] and 7 - deal[c].
All inputs are finite; a program needn't handle non-finite values.
Results may differ from a plain program's by a relative error of at most 0.022.
Values may be sent and summed in bfloat16 or wider, within the bound.
No kernel may reach another device: no remote copies, remote signals or barrier semaphores. Data moves between devices by JAX's collectives and lax.ppermute only.
A program may use at most 192 MiB of HBM per device.

v0:
```python
import functools

import jax
import jax.numpy as jnp
from jax import lax
from jax.experimental import pallas as pl
from jax.experimental.pallas import tpu as pltpu
from jax.sharding import PartitionSpec as P

HEADS = 12
HEAD_DIM = 64
LAYERS = 2
BLK = 192


norm_eps = 1e-05


def for_sending(x):
    return jax.tree.map(lambda a: a.astype(jnp.bfloat16) if a.dtype == jnp.float32 else a, x)


def layer_norm(values, gain, shift):
    centre = values - jnp.mean(values, axis=-1, keepdims=True)
    spread = jnp.mean(centre * centre, axis=-1, keepdims=True)
    return centre * lax.rsqrt(spread + norm_eps) * gain + shift


def gelu_exact(inputs):
    return 0.5 * inputs * (1.0 + jax.scipy.special.erf(inputs * 0.7071067811865476))


def key_positions(deal):
    pairs = deal.shape[0]
    offsets = jnp.arange(BLK, dtype=jnp.int32)
    first = deal[:, None] * BLK + offsets[None, :]
    second = (2 * pairs - 1 - deal)[:, None] * BLK + offsets[None, :]
    return jnp.concatenate([first, second], axis=1).reshape(-1)


def split_heads(matrix):
    return matrix.reshape(matrix.shape[0], HEADS, HEAD_DIM).transpose(1, 0, 2)


def join_heads(stacked):
    return stacked.transpose(1, 0, 2).reshape(stacked.shape[1], HEADS * HEAD_DIM)


def attend_forward(queries, keys_full, values_full, allowed):

    def one_head(items):
        head_q, head_k, head_v = items
        scores = jnp.einsum(
            "qd,kd->qk", head_q, head_k, preferred_element_type=jnp.float32
        ) * HEAD_DIM ** (-0.5)
        scores = jnp.where(allowed, scores, -1e30)
        top = jnp.max(scores, axis=-1, keepdims=True)
        weights = jnp.exp(scores - top)
        total = jnp.sum(weights, axis=-1, keepdims=True)
        probs = (weights / total).astype(jnp.bfloat16)
        output = jnp.einsum("qk,kd->qd", probs, head_v, preferred_element_type=jnp.float32)
        return (output, top[:, 0] + jnp.log(total[:, 0]))

    outputs, log_totals = lax.map(
        one_head, (split_heads(queries), split_heads(keys_full), split_heads(values_full))
    )
    return (join_heads(outputs), log_totals)


def attend_backward(queries, keys_full, values_full, log_totals, grad_context, allowed):

    def one_head(items):
        head_q, head_k, head_v, head_lse, head_grad = items
        scores = jnp.einsum(
            "qd,kd->qk", head_q, head_k, preferred_element_type=jnp.float32
        ) * HEAD_DIM ** (-0.5)
        scores = jnp.where(allowed, scores, -1e30)
        probs = jnp.exp(scores - head_lse[:, None])
        grad_probs = jnp.einsum("qd,kd->qk", head_grad, head_v, preferred_element_type=jnp.float32)
        inner_sum = jnp.sum(probs * grad_probs, axis=-1, keepdims=True)
        grad_scores = (probs * (grad_probs - inner_sum)).astype(jnp.bfloat16)
        grad_q = jnp.einsum(
            "qk,kd->qd", grad_scores, head_k, preferred_element_type=jnp.float32
        ) * HEAD_DIM ** (-0.5)
        grad_k = jnp.einsum(
            "qk,qd->kd", grad_scores, head_q, preferred_element_type=jnp.float32
        ) * HEAD_DIM ** (-0.5)
        grad_v = jnp.einsum(
            "qk,qd->kd", probs.astype(jnp.bfloat16), head_grad, preferred_element_type=jnp.float32
        )
        return (grad_q, grad_k, grad_v)

    grads = lax.map(
        one_head,
        (
            split_heads(queries),
            split_heads(keys_full),
            split_heads(values_full),
            log_totals,
            split_heads(grad_context),
        ),
    )
    return (join_heads(grads[0]), join_heads(grads[1]), join_heads(grads[2]))


def forward_layer(hidden, weights, allowed):
    (
        attend_in,
        query_bias,
        value_bias,
        attend_out,
        attend_bias,
        first_gain,
        first_shift,
        expand_proj,
        expand_bias,
        reduce_proj,
        reduce_bias,
        second_gain,
        second_shift,
    ) = weights
    width = hidden.shape[1]
    low_hidden = hidden.astype(jnp.bfloat16)
    projected = jnp.dot(low_hidden, attend_in, preferred_element_type=jnp.float32)
    queries = (projected[:, :width] + query_bias.astype(jnp.float32)).astype(jnp.bfloat16)
    keys_own = projected[:, width : 2 * width].astype(jnp.bfloat16)
    values_own = (projected[:, 2 * width :] + value_bias.astype(jnp.float32)).astype(jnp.bfloat16)
    keys_full, values_full = (
        lax.all_gather(keys_own, "ctx", axis=0, tiled=True),
        lax.all_gather(values_own, "ctx", axis=0, tiled=True),
    )
    context, log_totals = attend_forward(queries, keys_full, values_full, allowed)
    low_context = context.astype(jnp.bfloat16)
    branch = jnp.dot(
        low_context, attend_out, preferred_element_type=jnp.float32
    ) + attend_bias.astype(jnp.float32)
    first_sum = hidden + branch
    normed = layer_norm(first_sum, first_gain.astype(jnp.float32), first_shift.astype(jnp.float32))
    low_normed = normed.astype(jnp.bfloat16)
    inner_pre = jnp.dot(
        low_normed, expand_proj, preferred_element_type=jnp.float32
    ) + expand_bias.astype(jnp.float32)
    active = gelu_exact(inner_pre).astype(jnp.bfloat16)
    output_branch = jnp.dot(
        active, reduce_proj, preferred_element_type=jnp.float32
    ) + reduce_bias.astype(jnp.float32)
    second_sum = normed + output_branch
    output = layer_norm(
        second_sum, second_gain.astype(jnp.float32), second_shift.astype(jnp.float32)
    )
    saved = (
        low_hidden,
        queries,
        keys_full,
        values_full,
        log_totals,
        low_context,
        first_sum,
        low_normed,
        inner_pre,
        active,
        second_sum,
    )
    return (output, saved)


def column_sum(matrix):
    return jnp.sum(matrix.astype(jnp.float32), axis=0)


def backward_layer(grad_hidden, weights, saved, allowed):
    (
        attend_in,
        query_bias,
        value_bias,
        attend_out,
        attend_bias,
        first_gain,
        first_shift,
        expand_proj,
        expand_bias,
        reduce_proj,
        reduce_bias,
        second_gain,
        second_shift,
    ) = weights
    (
        low_hidden,
        queries,
        keys_full,
        values_full,
        log_totals,
        low_context,
        first_sum,
        low_normed,
        inner_pre,
        active,
        second_sum,
    ) = saved
    width = low_hidden.shape[1]
    second_pull = jax.vjp(
        layer_norm, second_sum, second_gain.astype(jnp.float32), second_shift.astype(jnp.float32)
    )[1]
    grad_second_sum, grad_second_gain, grad_second_shift = second_pull(grad_hidden)
    grad_branch = grad_second_sum.astype(jnp.bfloat16)
    grad_reduce_bias = column_sum(grad_branch)
    grad_reduce = jnp.einsum("tf,td->fd", active, grad_branch, preferred_element_type=jnp.float32)
    grad_active = jnp.einsum(
        "td,fd->tf", grad_branch, reduce_proj, preferred_element_type=jnp.float32
    )
    gelu_pull = jax.vjp(gelu_exact, inner_pre)[1]
    grad_inner = gelu_pull(grad_active)[0].astype(jnp.bfloat16)
    grad_expand_bias = column_sum(grad_inner)
    grad_expand = jnp.einsum(
        "td,tf->df", low_normed, grad_inner, preferred_element_type=jnp.float32
    )
    grad_normed = grad_second_sum + jnp.einsum(
        "tf,df->td", grad_inner, expand_proj, preferred_element_type=jnp.float32
    )
    first_pull = jax.vjp(
        layer_norm, first_sum, first_gain.astype(jnp.float32), first_shift.astype(jnp.float32)
    )[1]
    grad_first_sum, grad_first_gain, grad_first_shift = first_pull(grad_normed)
    grad_attn = grad_first_sum.astype(jnp.bfloat16)
    grad_attend_bias = column_sum(grad_attn)
    grad_attend_out = jnp.einsum(
        "td,te->de", low_context, grad_attn, preferred_element_type=jnp.float32
    )
    grad_context = jnp.einsum(
        "te,de->td", grad_attn, attend_out, preferred_element_type=jnp.float32
    ).astype(jnp.bfloat16)
    grad_queries, grad_keys_full, grad_values_full = attend_backward(
        queries, keys_full, values_full, log_totals, grad_context, allowed
    )
    grad_keys, grad_values = (
        lax.psum_scatter(
            grad_keys_full.astype(jnp.bfloat16), "ctx", scatter_dimension=0, tiled=True
        ).astype(jnp.float32),
        lax.psum_scatter(
            grad_values_full.astype(jnp.bfloat16), "ctx", scatter_dimension=0, tiled=True
        ).astype(jnp.float32),
    )
    grad_proj = jnp.concatenate(
        [
            grad_queries.astype(jnp.bfloat16),
            grad_keys.astype(jnp.bfloat16),
            grad_values.astype(jnp.bfloat16),
        ],
        axis=1,
    )
    grad_query_bias = column_sum(grad_proj[:, :width])
    grad_value_bias = column_sum(grad_proj[:, 2 * width :])
    grad_attend_in = jnp.einsum(
        "td,te->de", low_hidden, grad_proj, preferred_element_type=jnp.float32
    )
    grad_input = grad_first_sum + jnp.einsum(
        "te,de->td", grad_proj, attend_in, preferred_element_type=jnp.float32
    )
    grads = (
        grad_attend_in,
        grad_query_bias,
        grad_value_bias,
        grad_attend_out,
        grad_attend_bias,
        grad_first_gain,
        grad_first_shift,
        grad_expand,
        grad_expand_bias,
        grad_reduce,
        grad_reduce_bias,
        grad_second_gain,
        grad_second_shift,
    )
    return (grad_input, grads)


def reduce_grads(grads):
    shards = (
        lax.psum_scatter(
            grads[0].astype(jnp.bfloat16), "fsdp", scatter_dimension=0, tiled=True
        ).astype(jnp.float32),
        lax.psum_scatter(
            grads[1].astype(jnp.bfloat16), "fsdp", scatter_dimension=0, tiled=True
        ).astype(jnp.float32),
        lax.psum_scatter(
            grads[2].astype(jnp.bfloat16), "fsdp", scatter_dimension=0, tiled=True
        ).astype(jnp.float32),
        lax.psum_scatter(
            grads[3].astype(jnp.bfloat16), "fsdp", scatter_dimension=0, tiled=True
        ).astype(jnp.float32),
        lax.psum_scatter(
            grads[4].astype(jnp.bfloat16), "fsdp", scatter_dimension=0, tiled=True
        ).astype(jnp.float32),
        lax.psum_scatter(
            grads[5].astype(jnp.bfloat16), "fsdp", scatter_dimension=0, tiled=True
        ).astype(jnp.float32),
        lax.psum_scatter(
            grads[6].astype(jnp.bfloat16), "fsdp", scatter_dimension=0, tiled=True
        ).astype(jnp.float32),
        lax.psum_scatter(
            grads[7].astype(jnp.bfloat16), "fsdp", scatter_dimension=0, tiled=True
        ).astype(jnp.float32),
        lax.psum_scatter(
            grads[8].astype(jnp.bfloat16), "fsdp", scatter_dimension=0, tiled=True
        ).astype(jnp.float32),
        lax.psum_scatter(
            grads[9].astype(jnp.bfloat16), "fsdp", scatter_dimension=0, tiled=True
        ).astype(jnp.float32),
        lax.psum_scatter(
            grads[10].astype(jnp.bfloat16), "fsdp", scatter_dimension=0, tiled=True
        ).astype(jnp.float32),
        lax.psum_scatter(
            grads[11].astype(jnp.bfloat16), "fsdp", scatter_dimension=0, tiled=True
        ).astype(jnp.float32),
        lax.psum_scatter(
            grads[12].astype(jnp.bfloat16), "fsdp", scatter_dimension=0, tiled=True
        ).astype(jnp.float32),
    )
    return (
        lax.psum(shards[0].astype(jnp.bfloat16), "ctx").astype(jnp.float32),
        lax.psum(shards[1].astype(jnp.bfloat16), "ctx").astype(jnp.float32),
        lax.psum(shards[2].astype(jnp.bfloat16), "ctx").astype(jnp.float32),
        lax.psum(shards[3].astype(jnp.bfloat16), "ctx").astype(jnp.float32),
        lax.psum(shards[4].astype(jnp.bfloat16), "ctx").astype(jnp.float32),
        lax.psum(shards[5].astype(jnp.bfloat16), "ctx").astype(jnp.float32),
        lax.psum(shards[6].astype(jnp.bfloat16), "ctx").astype(jnp.float32),
        lax.psum(shards[7].astype(jnp.bfloat16), "ctx").astype(jnp.float32),
        lax.psum(shards[8].astype(jnp.bfloat16), "ctx").astype(jnp.float32),
        lax.psum(shards[9].astype(jnp.bfloat16), "ctx").astype(jnp.float32),
        lax.psum(shards[10].astype(jnp.bfloat16), "ctx").astype(jnp.float32),
        lax.psum(shards[11].astype(jnp.bfloat16), "ctx").astype(jnp.float32),
        lax.psum(shards[12].astype(jnp.bfloat16), "ctx").astype(jnp.float32),
    )


def layer_slices(sharded, layer_index):
    return tuple((tensor[layer_index] for tensor in sharded))


def on_device_plain(
    activations,
    cotangent,
    doc_start,
    deal,
    attend_in,
    query_bias,
    value_bias,
    attend_out,
    attend_bias,
    first_gain,
    first_shift,
    expand_proj,
    expand_bias,
    reduce_proj,
    reduce_bias,
    second_gain,
    second_shift,
):
    sharded = (
        attend_in,
        query_bias,
        value_bias,
        attend_out,
        attend_bias,
        first_gain,
        first_shift,
        expand_proj,
        expand_bias,
        reduce_proj,
        reduce_bias,
        second_gain,
        second_shift,
    )
    row_count = activations.shape[1]
    positions = key_positions(deal)
    own_rank = lax.axis_index("ctx")
    own_positions = lax.dynamic_slice_in_dim(positions, own_rank * row_count, row_count)
    own_starts = doc_start[0]
    key_starts = lax.all_gather(own_starts, "ctx", axis=0, tiled=True)
    allowed = (positions[None, :] <= own_positions[:, None]) & (
        key_starts[None, :] == own_starts[:, None]
    )
    hidden = activations[0].astype(jnp.float32)
    kept_weights = []
    kept_saved = []
    for layer_index in range(LAYERS):
        weights = lax.all_gather(
            for_sending(layer_slices(sharded, layer_index)), "fsdp", axis=0, tiled=True
        )
        hidden, saved = forward_layer(hidden, weights, allowed)
        kept_weights.append(weights)
        kept_saved.append(saved)
    out_act = hidden.astype(jnp.bfloat16)[None]
    grad_hidden = cotangent[0].astype(jnp.float32)
    reduced = [None] * LAYERS
    for layer_index in reversed(range(LAYERS)):
        weights = lax.all_gather(
            for_sending(layer_slices(sharded, layer_index)), "fsdp", axis=0, tiled=True
        )
        grad_hidden, grads = backward_layer(grad_hidden, weights, kept_saved[layer_index], allowed)
        reduced[layer_index] = reduce_grads(grads)
    stacked = [
        jnp.stack([reduced[layer_index][member] for layer_index in range(LAYERS)])
        for member in range(13)
    ]
    return (
        out_act,
        grad_hidden[None],
        stacked[0],
        stacked[1],
        stacked[2],
        stacked[3],
        stacked[4],
        stacked[5],
        stacked[6],
        stacked[7],
        stacked[8],
        stacked[9],
        stacked[10],
        stacked[11],
        stacked[12],
    )


F32 = jnp.float32
BF = jnp.bfloat16
WIDTH = HEADS * HEAD_DIM
QB = 256
SCORE_SCALE = HEAD_DIM ** (-0.5) * 1.4426950408889634
NEG = -1e30
VMEM_LIMIT = 60 * 1024 * 1024


def mm_nn(a, b):
    return lax.dot_general(a, b, (((1,), (0,)), ((), ())), preferred_element_type=F32)


def mm_nt(a, b):
    return lax.dot_general(a, b, (((1,), (1,)), ((), ())), preferred_element_type=F32)


def mm_tn(a, b):
    return lax.dot_general(a, b, (((0,), (0,)), ((), ())), preferred_element_type=F32)


def call(kernel, outs, args, specs, scratch, name, flops, nbytes):
    return pl.pallas_call(
        kernel,
        out_shape=[jax.ShapeDtypeStruct(shape, dtype) for shape, dtype in outs],
        in_specs=[pl.BlockSpec(memory_space=space) for space in specs],
        out_specs=[pl.BlockSpec(memory_space=pltpu.VMEM) for _ in outs],
        scratch_shapes=scratch,
        compiler_params=pltpu.CompilerParams(vmem_limit_bytes=VMEM_LIMIT),
        cost_estimate=pl.CostEstimate(flops=flops if name in ("sums", "join") else 0, bytes_accessed=0, transcendentals=0),
        name=name,
    )(*args)


def block_of(block, blocks):
    half = 0 if 2 * block < blocks else 1
    return (block if half == 0 else blocks - 1 - block), half


CORE, SHARD, RANK, JMAP, INV, JMIN = 0, 1, 2, 6, 10, 14
SWAPPED = (0, 2, 1, 3)
WEIGHT = 10**11
VEC_AT = 640


def started_copies(sems, *pairs):
    copies = []
    for n, (src, dst) in enumerate(pairs):
        copy = pltpu.make_async_copy(src, dst, sems.at[n])
        copy.start()
        copies.append(copy)
    return copies


def last_kernel(
    writer, places, meta, c0, c1, c2, c3, hid, cot, t, a, b, d, crossed,
    l_mine, l_other, hlow, gfs, dgg, gctx,
    xhat1, rstd1, gp, xhat2, rstd2, e_s, r_s, sems, wo_s, b_s, wo_sems, ctx, eb, eb_s,
):
    loads = (e_s, r_s, sems, wo_s, b_s, wo_sems)
    mlp_fwd_kernel(
        writer, (None,) * 5 + tuple(places[:3]), meta, c0, c1, c2, c3, hid, t, a, b, d, crossed,
        xhat1, rstd1, gp, xhat2, rstd2, l_mine, l_other, hlow, *loads, ctx, eb, finish=False,
    )
    mlp_bwd_kernel(
        writer, places[3:], meta, xhat1, rstd1, xhat2, rstd2, gp, cot, t, a, b, d, crossed,
        gfs, dgg, gctx, *loads, eb_s, parts=1, loaded=True,
    )


class Writer:
    def __init__(self, sems):
        self.sems = sems
        self.copies = []

    def send(self, src, dst, *at):
        if dst is None:
            return
        if at:
            src, dst = src.at[at], dst.at[at]
        copy = pltpu.make_async_copy(src, dst, self.sems.at[len(self.copies)])
        copy.start()
        self.copies.append(copy)

    def finish(self):
        for copy in self.copies:
            copy.wait()


def writing(kernel, outs, copies):
    count = len(outs)

    def run(*refs, scratch, **keys):
        ins, places, rest = refs[: -count - scratch], refs[-count - scratch : -scratch], refs[-scratch:]
        buffers, sems, rest = rest[:count], rest[count], rest[count + 1 :]
        kernel(Writer(sems), places, *ins, *buffers, *rest, **keys)

    return run, [pltpu.VMEM(shape, dtype) for shape, dtype in outs] + [pltpu.SemaphoreType.DMA((copies,))]


def call_writing(kernel, outs, args, specs, scratch, name, copies, **keys):
    run, buffers = writing(kernel, outs, copies)
    scratch = buffers + scratch
    return pl.pallas_call(
        functools.partial(run, scratch=len(scratch), **keys),
        out_shape=[jax.ShapeDtypeStruct(shape, dtype) for shape, dtype in outs],
        in_specs=[pl.BlockSpec(memory_space=space) for space in specs],
        out_specs=[pl.BlockSpec(memory_space=pl.ANY) for _ in outs],
        scratch_shapes=scratch,
        compiler_params=pltpu.CompilerParams(vmem_limit_bytes=VMEM_LIMIT),
        cost_estimate=pl.CostEstimate(flops=0, bytes_accessed=0, transcendentals=0),
        name=name,
    )(*args)


def prep_kernel(
    expand, reduce, attend_in, attend_out, expand_bias, v0, v1, v2, v3, v4, v5, v6, v7,
    t0, d0, t1, d1,
):
    rank = lax.axis_index("ctx")
    cut = expand.shape[1]
    hw = WIDTH // 4
    for layer, (t, d) in enumerate(((t0, d0), (t1, d1))):
        bias = expand_bias[layer : layer + 1, :].astype(F32)
        rows = [v[layer : layer + 1, :].astype(F32) for v in (v0, v1, v2, v3, v4, v5, v6, v7)]
        rows += [bias[:, k * cut : (k + 1) * cut] for k in range(4)]
        rows.append(jnp.zeros((4, cut), F32))
        d[2 * cut :, :] = attend_out[layer]
        t[2 * cut :, 3 * hw :] = jnp.zeros((cut, WIDTH - 3 * hw), BF)
        t[2 * cut : 2 * cut + 16, VEC_AT : VEC_AT + cut] = jnp.concatenate(rows, axis=0).astype(BF)
        for k in range(4):

            @pl.when(rank == k)
            def _():
                for out, at in ((t, k), (d, k ^ 3)):
                    out[0:cut, :] = jnp.concatenate(
                        [
                            expand[layer, :, (2 * z + h) * 4 * cut + at * cut : (2 * z + h) * 4 * cut + (at + 1) * cut]
                            for h in range(2)
                            for z in range(4)
                        ],
                        axis=1,
                    )
                    out[cut : 2 * cut, :] = reduce[layer, at * cut : (at + 1) * cut, :]
                t[2 * cut :, 0 : 3 * hw] = jnp.concatenate(
                    [attend_in[layer, :, n * WIDTH + k * hw : n * WIDTH + (k + 1) * hw] for n in range(3)], axis=1
                )


def nothing_kernel(*refs):
    pass


def after(xs, *others):
    return pl.pallas_call(
        nothing_kernel,
        out_shape=[jax.ShapeDtypeStruct(x.shape, x.dtype) for x in xs],
        in_specs=[pl.BlockSpec(memory_space=pl.ANY)] * (len(xs) + len(others)),
        out_specs=[pl.BlockSpec(memory_space=pl.ANY)] * len(xs),
        input_output_aliases={n: n for n in range(len(xs))},
        cost_estimate=pl.CostEstimate(flops=WEIGHT, bytes_accessed=0, transcendentals=0),
        name="after",
    )(*xs, *others)


def pack_kernel(a, b, *rest):
    out, held, ins, outs = rest[-4:]
    coming = [pltpu.make_async_copy((a, b)[n // 4].at[n % 4], held.at[n // 4, n % 4], ins.at[n]) for n in range(8)]
    going = [pltpu.make_async_copy(held.at[n // 4, n % 4], out.at[n // 4, n % 4], outs.at[n]) for n in range(8)]
    for copy in coming:
        copy.start()
    for arrive, leave in zip(coming, going):
        arrive.wait()
        leave.start()
    for copy in going:
        copy.wait()


def pack(a, b, *others):
    shape = (2,) + a.shape
    return pl.pallas_call(
        pack_kernel,
        out_shape=jax.ShapeDtypeStruct(shape, a.dtype),
        in_specs=[pl.BlockSpec(memory_space=pl.ANY)] * (2 + len(others)),
        out_specs=pl.BlockSpec(memory_space=pl.ANY),
        scratch_shapes=[pltpu.VMEM(shape, a.dtype), pltpu.SemaphoreType.DMA((8,)), pltpu.SemaphoreType.DMA((8,))],
        cost_estimate=pl.CostEstimate(flops=0, bytes_accessed=0, transcendentals=0),
        name="pack",
    )(a, b, *others)


def half_kernel(meta, t, *rest):
    out, held, ins, outs = rest[-4:]
    coming = [pltpu.make_async_copy(t.at[z, meta[CORE], 0:2], held.at[z], ins.at[z]) for z in range(4)]
    going = [pltpu.make_async_copy(held.at[z], out.at[z], outs.at[z]) for z in range(4)]
    for copy in coming:
        copy.start()
    for arrive, leave in zip(coming, going):
        arrive.wait()
        leave.start()
    for copy in going:
        copy.wait()


def half_of(meta, t, *others):
    shape = (4, 2) + t.shape[3:]
    return pl.pallas_call(
        half_kernel,
        out_shape=jax.ShapeDtypeStruct(shape, t.dtype),
        in_specs=[pl.BlockSpec(memory_space=space) for space in [pltpu.SMEM] + [pl.ANY] * (1 + len(others))],
        out_specs=pl.BlockSpec(memory_space=pl.ANY),
        scratch_shapes=[pltpu.VMEM(shape, t.dtype), pltpu.SemaphoreType.DMA((4,)), pltpu.SemaphoreType.DMA((4,))],
        cost_estimate=pl.CostEstimate(flops=0, bytes_accessed=0, transcendentals=0),
        name="half",
    )(meta, t, *others)


def sums_kernel(*refs, layout, count, split):
    outs = refs[-len(layout) :]
    at = 0
    for out, parts in zip(outs, layout):
        lane = 0
        for n in parts:
            total = refs[at][...].astype(F32)
            for ref in refs[at + 1 : at + n]:
                total = total + ref[...].astype(F32)
            at += n
            if split:
                for k in range(len(outs)):
                    outs[k][...] = total[k].astype(BF)
            else:
                out[..., lane : lane + total.shape[-1]] = total.astype(BF)
            lane += total.shape[-1]
        if split:
            break


def sums(outputs, *others, split=0, weight=0):
    args = tuple(x for groups in outputs for group in groups for x in group)
    layout = tuple(tuple(len(group) for group in groups) for groups in outputs)
    if split:
        shapes = [(args[0].shape[1:], BF)] * split
        layout = layout * split
    else:
        shapes = [
            (groups[0][0].shape[:-1] + (sum(group[0].shape[-1] for group in groups),), BF) for groups in outputs
        ]
    return call(
        functools.partial(sums_kernel, layout=layout, count=len(args), split=split),
        shapes, args + others, [pltpu.VMEM] * len(args) + [pl.ANY] * len(others), [], "sums", weight, 0,
    )


def join_kernel(att, t, d, *rest):
    out = rest[-1]
    rows = att.shape[0]
    out[0:rows, 0 : att.shape[1]] = att[...]
    out[0:rows, att.shape[1] :] = jnp.zeros((rows, out.shape[1] - att.shape[1]), BF)
    for k in range(2):
        out[rows:, k * WIDTH : (k + 1) * WIDTH] = (t[k].astype(F32) + d[k].astype(F32)).astype(BF)


def merge_kernel(dwo, own, other, *rest):
    out = rest[-1]
    out[:, :, 0:WIDTH] = dwo[...]
    out[:, :, WIDTH:] = (own[...].astype(F32) + other[...].astype(F32)).astype(BF)


def vectors_of(shards, order):
    return jnp.concatenate([shards[f // 2, f % 2, :, 0:96] for f in order], axis=1).astype(F32)


NATURAL = tuple(range(8))
CORE_MAJOR = (0, 2, 4, 6, 1, 3, 5, 7)


def attn_fwd_kernel(
    meta, h0, h1, h2, h3, qrow, kcol, t, *rest, heads, tokens
):
    qkv, c0, c1, c2, c3, lse, q_s, k_s, vt_s, o_s, ctx, w_s, b_s, sems = rest[-14:]
    blocks = tokens // BLK
    hw = heads * HEAD_DIM
    copies = started_copies(
        sems, (t.at[:, :, 2, :, 0:VEC_AT], w_s), (t.at[:, :, 2, 0:16, VEC_AT : VEC_AT + 128], b_s)
    )
    for copy in copies:
        copy.wait()
    w = w_s[...].reshape(WIDTH, VEC_AT)[:, 0 : 3 * hw]
    vec = vectors_of(b_s, NATURAL)
    bias = jnp.zeros((1, 3 * hw), F32)
    for k in range(4):
        part = jnp.concatenate(
            [vec[6:7, k * hw : (k + 1) * hw], jnp.zeros((1, hw), F32), vec[7:8, k * hw : (k + 1) * hw]], axis=1
        )
        bias = jnp.where(meta[RANK] == k, part, bias)
    for j, piece in enumerate((h0, h1, h2, h3)):
        qkv[j] = (mm_nn(piece[...], w) + bias).astype(BF)
    for pair in range(blocks // 2):
        rows = []
        for block in (2 * pair, 2 * pair + 1):
            at, half = block_of(block, blocks)
            rows.append(qkv[meta[JMAP + at], half * BLK : (half + 1) * BLK, :])
        both = jnp.concatenate(rows, axis=0)
        lo, hi = 2 * pair * BLK, 2 * (pair + 1) * BLK
        for h in range(heads):
            q_s[h, lo:hi, :] = both[:, h * HEAD_DIM : (h + 1) * HEAD_DIM]
            k_s[h, lo:hi, :] = both[:, hw + h * HEAD_DIM : hw + (h + 1) * HEAD_DIM]
        vt_s[:, lo:hi] = both[:, 2 * hw :].T
    iota_k = lax.broadcasted_iota(jnp.int32, (QB, QB), 0)
    iota_q = lax.broadcasted_iota(jnp.int32, (QB, QB), 1)
    causal = iota_k <= iota_q
    head_rows = [slice(h * HEAD_DIM, (h + 1) * HEAD_DIM) for h in range(heads)]
    for i in range(tokens // QB):
        lo = i * QB
        starts_q = qrow[0:1, lo : lo + QB]

        def scores(at, diagonal):
            col = kcol[pl.ds(at, QB), :]
            allowed = jnp.concatenate([col, col], axis=1) == starts_q
            if diagonal:
                allowed = allowed & causal
            return [
                jnp.where(allowed, mm_nt(k_s[h, pl.ds(at, QB), :], q_s[h, lo : lo + QB, :]) * SCORE_SCALE, NEG)
                for h in range(heads)
            ]

        ss = scores(lo, True)
        tops = [jnp.max(s, axis=0, keepdims=True) for s in ss]
        ps = [jnp.exp2(s - top) for s, top in zip(ss, tops)]
        totals = [jnp.sum(p, axis=0, keepdims=True) for p in ps]
        outs = [mm_nn(vt_s[head_rows[h], lo : lo + QB], ps[h].astype(BF)) for h in range(heads)]

        def step(jb, carry):
            tops, totals, outs = carry
            at = pl.multiple_of(jb * QB, QB)
            ss = scores(at, False)
            new = [jnp.maximum(top, jnp.max(s, axis=0, keepdims=True)) for s, top in zip(ss, tops)]
            ps = [jnp.exp2(s - top) for s, top in zip(ss, new)]
            alphas = [jnp.exp2(top - n) for top, n in zip(tops, new)]
            totals = [
                total * alpha + jnp.sum(p, axis=0, keepdims=True) for total, alpha, p in zip(totals, alphas, ps)
            ]
            outs = [
                outs[h] * alphas[h] + mm_nn(vt_s[head_rows[h], pl.ds(at, QB)], ps[h].astype(BF)) for h in range(heads)
            ]
            return new, totals, outs

        if i > 0:
            tops, totals, outs = lax.fori_loop(meta[JMIN + i], i, step, (tops, totals, outs))
        for h in range(heads):
            o_s[head_rows[h], lo : lo + QB] = outs[h] / totals[h]
            lse[h : h + 1, lo : lo + QB] = tops[h] + jnp.log2(totals[h])
    for pair in range(blocks // 2):
        lo, hi = 2 * pair * BLK, 2 * (pair + 1) * BLK
        both = o_s[:, lo:hi].T.astype(BF)
        for n, block in enumerate((2 * pair, 2 * pair + 1)):
            at, half = block_of(block, blocks)
            ctx[meta[JMAP + at], :, half * hw : (half + 1) * hw] = both[n * BLK : (n + 1) * BLK, :]
    for j, out in enumerate((c0, c1, c2, c3)):
        out[...] = ctx[j]


def attn_bwd_kernel(
    meta, h0, h1, h2, h3, qrow, kcol, qkv, c0, c1, c2, c3, gctx, lse, t, *rest, heads, tokens
):
    (
        g_own, g_a, g_b, g_d, dw_own, dw_other, q_s, k_s, v_s, do_s, kt_s, delta_s, dk_s, dv_s, dqt_s, g_s, w_s, ctx, dw, sems,
    ) = rest[-20:]
    blocks = tokens // BLK
    hw = heads * HEAD_DIM
    scale = HEAD_DIM ** (-0.5)
    copies = started_copies(sems, (t.at[:, :, 2, :, 0:VEC_AT], w_s))
    for j, c in enumerate((c0, c1, c2, c3)):
        ctx[j] = c[...]
    for pair in range(blocks // 2):
        rows, grads, outs = [], [], []
        for block in (2 * pair, 2 * pair + 1):
            at, half = block_of(block, blocks)
            rows.append(qkv[meta[JMAP + at], half * BLK : (half + 1) * BLK, :])
            grads.append(gctx[meta[INV + at], :, half * hw : (half + 1) * hw])
            outs.append(ctx[meta[JMAP + at], :, half * hw : (half + 1) * hw])
        both = jnp.concatenate(rows, axis=0)
        grad = jnp.concatenate(grads, axis=0)
        out = jnp.concatenate(outs, axis=0)
        lo, hi = 2 * pair * BLK, 2 * (pair + 1) * BLK
        prod = (grad.astype(F32) * out.astype(F32)).T
        kt_s[:, lo:hi] = both[:, hw : 2 * hw].T
        for h in range(heads):
            c0, c1 = h * HEAD_DIM, (h + 1) * HEAD_DIM
            q_s[h, lo:hi, :] = both[:, c0:c1]
            k_s[h, lo:hi, :] = both[:, hw + c0 : hw + c1]
            v_s[h, lo:hi, :] = both[:, 2 * hw + c0 : 2 * hw + c1]
            do_s[h, lo:hi, :] = grad[:, c0:c1]
            delta_s[h : h + 1, lo:hi] = jnp.sum(prod[c0:c1, :], axis=0, keepdims=True)
    dk_s[...] = jnp.zeros_like(dk_s)
    dv_s[...] = jnp.zeros_like(dv_s)
    iota_k = lax.broadcasted_iota(jnp.int32, (QB, QB), 0)
    iota_q = lax.broadcasted_iota(jnp.int32, (QB, QB), 1)
    causal = iota_k <= iota_q
    head_rows = [slice(h * HEAD_DIM, (h + 1) * HEAD_DIM) for h in range(heads)]
    for i in range(tokens // QB):
        lo = i * QB
        starts_q = qrow[0:1, lo : lo + QB]

        def block(at, diagonal):
            col = kcol[pl.ds(at, QB), :]
            allowed = jnp.concatenate([col, col], axis=1) == starts_q
            if diagonal:
                allowed = allowed & causal
            dqs = []
            for h in range(heads):
                q, do = q_s[h, lo : lo + QB, :], do_s[h, lo : lo + QB, :]
                s = mm_nt(k_s[h, pl.ds(at, QB), :], q) * SCORE_SCALE
                p = jnp.exp2(jnp.where(allowed, s, NEG) - lse[h : h + 1, lo : lo + QB])
                dp = mm_nt(v_s[h, pl.ds(at, QB), :], do)
                ds = (p * (dp - delta_s[h : h + 1, lo : lo + QB])).astype(BF)
                dv_s[h, pl.ds(at, QB), :] += mm_nn(p.astype(BF), do)
                dk_s[h, pl.ds(at, QB), :] += mm_nn(ds, q)
                dqs.append(mm_nn(kt_s[head_rows[h], pl.ds(at, QB)], ds))
            return dqs

        dqs = block(lo, True)
        if i > 0:
            dqs = lax.fori_loop(
                meta[JMIN + i],
                i,
                lambda jb, acc: [x + y for x, y in zip(acc, block(pl.multiple_of(jb * QB, QB), False))],
                dqs,
            )
        for h in range(heads):
            dqt_s[head_rows[h], lo : lo + QB] = dqs[h] * scale
    for pair in range(blocks // 2):
        lo, hi = 2 * pair * BLK, 2 * (pair + 1) * BLK
        parts = [dqt_s[:, lo:hi].T.astype(BF)]
        parts += [(dk_s[h, lo:hi, :] * scale).astype(BF) for h in range(heads)]
        parts += [dv_s[h, lo:hi, :].astype(BF) for h in range(heads)]
        both = jnp.concatenate(parts, axis=1)
        for n, block_at in enumerate((2 * pair, 2 * pair + 1)):
            at, half = block_of(block_at, blocks)
            g_s[meta[JMAP + at], half * BLK : (half + 1) * BLK, :] = both[n * BLK : (n + 1) * BLK, :]
    for copy in copies:
        copy.wait()
    w = w_s[...].reshape(WIDTH, VEC_AT)[:, 0 : 3 * hw]
    total = None
    sums = None
    for j, piece in enumerate((h0, h1, h2, h3)):
        g = g_s[j]
        back = mm_nt(g, w)
        if j == 0:
            g_own[...] = back
        else:
            (g_a, g_b, g_d)[j - 1][...] = back.astype(BF)
        part = mm_tn(piece[...], g)
        col = jnp.sum(g.astype(F32), axis=0, keepdims=True)
        total = part if total is None else total + part
        sums = col if sums is None else sums + col
    shards, rows_out, cols = dw.shape
    rows = WIDTH // shards
    dw[:, 0:rows, :] = total.reshape(shards, rows, cols).astype(BF)
    dw[:, rows:, :] = jnp.broadcast_to(sums[None], (shards, rows_out - rows, cols)).astype(BF)
    for k in range(4):
        dw_own[k] = dw[2 * k + meta[CORE]]
        dw_other[k] = dw[2 * k + 1 - meta[CORE]]


def start_ffn_copies(core, t, a, b, d, crossed, e_s, r_s, sems):
    ca, cb = crossed.at[0], crossed.at[1]
    groups = []
    for p, parts in enumerate(((t,), (a, cb), (b, ca), (d,))):
        pairs = []
        if len(parts) == 1:
            pairs.append((parts[0].at[:, :, 0], e_s.at[p]))
            for h in range(2):
                pairs.append((parts[0].at[:, h, 1], r_s.at[p, h]))
        else:
            for src, parity in ((parts[0], core), (parts[1], 1 - core)):
                pairs.append((src.at[:, 0], e_s.at[p, :, parity]))
                pairs.append((src.at[:, 1], r_s.at[p, parity]))
        group = []
        for n, (src, dst) in enumerate(pairs):
            copy = pltpu.make_async_copy(src, dst, sems.at[p, n])
            copy.start()
            group.append(copy)
        groups.append(group)
    return groups


def ffn_scratch():
    return [
        pltpu.VMEM((4, 4, 2, 96, WIDTH), BF),
        pltpu.VMEM((4, 2, 4, 96, WIDTH), BF),
        pltpu.SemaphoreType.DMA((4, 4)),
        pltpu.VMEM((4, 2, 96, WIDTH), BF),
        pltpu.VMEM((4, 2, 16, 128), BF),
        pltpu.SemaphoreType.DMA((2,)),
    ]


def mlp_fwd_scratch(rows, hw):
    return ffn_scratch() + [pltpu.VMEM((4, rows, hw), BF), pltpu.VMEM((8, WIDTH), F32)]


def mlp_bwd_scratch():
    return ffn_scratch() + [pltpu.VMEM((8, WIDTH), F32)]


def wgrad_scratch():
    rows = 2 * BLK
    return [
        pltpu.VMEM((rows, 3 * WIDTH), BF),
        pltpu.VMEM((rows, 3 * WIDTH), BF),
        pltpu.VMEM((rows + 16, 6 * WIDTH), BF),
        pltpu.VMEM((rows + 16, 6 * WIDTH), BF),
        pltpu.SemaphoreType.DMA((16,)),
    ]


def attn_fwd_scratch(heads, tokens):
    hw = heads * HEAD_DIM
    return [
        pltpu.VMEM((heads, tokens, HEAD_DIM), BF),
        pltpu.VMEM((heads, tokens, HEAD_DIM), BF),
        pltpu.VMEM((hw, tokens), BF),
        pltpu.VMEM((hw, tokens), F32),
        pltpu.VMEM((4, BLK, 2 * hw), BF),
        pltpu.VMEM((4, 2, 96, VEC_AT), BF),
        pltpu.VMEM((4, 2, 16, 128), BF),
        pltpu.SemaphoreType.DMA((2,)),
    ]


def attn_bwd_scratch(heads, tokens):
    hw = heads * HEAD_DIM
    return [pltpu.VMEM((heads, tokens, HEAD_DIM), BF)] * 4 + [
        pltpu.VMEM((hw, tokens), BF),
        pltpu.VMEM((8, tokens), F32),
        pltpu.VMEM((heads, tokens, HEAD_DIM), F32),
        pltpu.VMEM((heads, tokens, HEAD_DIM), F32),
        pltpu.VMEM((hw, tokens), F32),
        pltpu.VMEM((4, tokens // 4, 3 * hw), BF),
        pltpu.VMEM((4, 2, 96, VEC_AT), BF),
        pltpu.VMEM((4, BLK, 2 * hw), BF),
        pltpu.VMEM((8, 112, 3 * hw), BF),
        pltpu.SemaphoreType.DMA((1,)),
    ]


def norm_parts(values):
    centre = values - jnp.mean(values, axis=-1, keepdims=True)
    spread = jnp.mean(centre * centre, axis=-1, keepdims=True)
    rstd = lax.rsqrt(spread + norm_eps)
    return centre * rstd, rstd


def shard_columns(x, parity):
    return jnp.concatenate([x[:, (2 * z + parity) * 96 : (2 * z + parity + 1) * 96] for z in range(4)], axis=1)


def mlp_fwd_kernel(
    writer, places, meta, c0, c1, c2, c3, hid, t, a, b, d, crossed,
    xhat1, rstd1, gp, xhat2, rstd2, l_mine, l_other, hlow, *rest, finish=True,
):
    hnext, (e_s, r_s, sems, wo_s, b_s, wo_sems, ctx, eb) = rest[:-8], rest[-8:]
    core = meta[CORE]
    xhat1_to, rstd1_to, gp_to, xhat2_to, rstd2_to, mine_to, other_to, hlow_to = places[:8]
    wo_copies = started_copies(
        wo_sems, (d.at[:, :, 2], wo_s), (t.at[:, :, 2, 0:16, VEC_AT : VEC_AT + 128], b_s)
    )
    copies = start_ffn_copies(core, t, a, b, d, crossed, e_s, r_s, sems)
    half_cols = WIDTH // 2
    hw = c0.shape[1] // 2
    for p, piece in enumerate((c0, c1, c2, c3)):
        for half in range(2):
            ctx[meta[RANK + p], half * BLK : (half + 1) * BLK, :] = piece[:, half * hw : (half + 1) * hw]

    def keep(parts, at):
        for parity in range(2):

            @pl.when(core == parity)
            def _():
                l_mine[:, at : at + half_cols] = parts[parity]

            @pl.when(core != parity)
            def _():
                l_other[:, at : at + half_cols] = parts[parity]

        for ref, to in ((l_mine, mine_to), (l_other, other_to)):
            writer.send(ref, to, slice(None), slice(at, at + half_cols))

    low = jnp.concatenate([ctx[rank] for rank in range(4)], axis=1)
    keep([shard_columns(low, parity) for parity in range(2)], half_cols)
    for copy in wo_copies:
        copy.wait()
    vec = vectors_of(b_s, NATURAL)
    eb[...] = vectors_of(b_s, CORE_MAJOR)[8:16, :]
    wo = wo_s[...].reshape(WIDTH, WIDTH)
    first_sum = hid[...].astype(F32) + (mm_nn(low, wo) + vec[0:1, :])
    x1, r1 = norm_parts(first_sum)
    xhat1[...] = x1
    rstd1[...] = r1
    writer.send(xhat1, xhat1_to)
    writer.send(rstd1, rstd1_to)
    normed = x1 * vec[1:2, :] + vec[2:3, :]
    lown = normed.astype(BF)
    keep([shard_columns(lown, parity) for parity in range(2)], 0)
    out = normed + vec[3:4, :]
    for p in range(4):
        for copy in copies[p]:
            copy.wait()
        bias = eb[pl.ds(meta[RANK + p], 1), :]
        u = mm_nn(lown, e_s[p].reshape(WIDTH, WIDTH)) + bias
        cdf = 0.5 * (1.0 + lax.erf(u * 0.7071067811865476))
        pdf = jnp.exp(-0.5 * u * u) * 0.3989422804014327
        low = (u * cdf).astype(BF)
        cut = slice(p * WIDTH, (p + 1) * WIDTH)
        gp[:, cut] = (cdf + u * pdf).astype(BF)
        writer.send(gp, gp_to, slice(None), cut)
        keep([low[:, :half_cols], low[:, half_cols:]], WIDTH + p * half_cols)
        out = out + mm_nn(low, r_s[p].reshape(WIDTH, WIDTH))
    x2, r2 = norm_parts(out)
    nxt = x2 * vec[4:5, :] + vec[5:6, :]
    hlow[...] = nxt.astype(BF)
    writer.send(hlow, hlow_to)
    xhat2[...] = x2
    writer.send(xhat2, xhat2_to)
    rstd2[...] = r2
    writer.send(rstd2, rstd2_to)
    if hnext:
        hnext[0][...] = nxt
        writer.send(hnext[0], places[8])
    if finish:
        writer.finish()


def norm_back(gy, gain, xhat, rstd):
    g = gy * gain
    return rstd * (g - jnp.mean(g, axis=-1, keepdims=True) - xhat * jnp.mean(g * xhat, axis=-1, keepdims=True))


def rows_sum(x):
    return jnp.sum(x, axis=0, keepdims=True)


def mlp_bwd_kernel(
    writer, places, meta, xhat1, rstd1, xhat2, rstd2, gp, *rest, parts, loaded=False
):
    t, a, b, d, crossed = rest[parts : parts + 5]
    gfs, dgg, gctx, e_s, r_s, sems, wo_s, b_s, wo_sems, eb_s = rest[-10:]
    rows = gfs.shape[0]
    core = meta[CORE]
    if loaded:
        copies, wo_copies = [[]] * 4, []
    else:
        copies = start_ffn_copies(core, t, a, b, d, crossed, e_s, r_s, sems)
        wo_copies = started_copies(
            wo_sems, (d.at[:, :, 2], wo_s), (t.at[:, :, 2, 0:16, VEC_AT : VEC_AT + 128], b_s)
        )
    grad = rest[0][...].astype(F32)
    for ref in rest[1:parts]:
        grad = grad + ref[...].astype(F32)
    x2 = xhat2[...]
    for copy in wo_copies:
        copy.wait()
    vec = vectors_of(b_s, NATURAL)
    gss = norm_back(grad, vec[4:5, :], x2, rstd2[...])
    low = gss.astype(BF)
    cut = slice(4 * WIDTH, 5 * WIDTH)
    dgg[0:rows, cut] = low
    writer.send(dgg.at[0:rows, cut], places[1].at[0:rows, cut])
    sums = [None] * 8
    sums[4] = rows_sum(grad * x2)
    sums[5] = rows_sum(grad)
    sums[3] = rows_sum(low.astype(F32))
    gn = gss
    eb_s[...] = jnp.zeros_like(eb_s)
    for p in range(4):
        for copy in copies[p]:
            copy.wait()
        ga = mm_nt(low, r_s[p].reshape(WIDTH, WIDTH))
        dip = (ga * gp[:, p * WIDTH : (p + 1) * WIDTH].astype(F32)).astype(BF)
        cut = slice(p * WIDTH, (p + 1) * WIDTH)
        dgg[0:rows, cut] = dip
        writer.send(dgg.at[0:rows, cut], places[1].at[0:rows, cut])
        eb_s[pl.ds(meta[RANK + p], 1), :] = rows_sum(dip.astype(F32))
        gn = gn + mm_nt(dip, e_s[p].reshape(WIDTH, WIDTH))
    x1 = xhat1[...]
    gf = norm_back(gn, vec[1:2, :], x1, rstd1[...])
    sums[1] = rows_sum(gn * x1)
    sums[2] = rows_sum(gn)
    lowa = gf.astype(BF)
    cut = slice(5 * WIDTH, 6 * WIDTH)
    dgg[0:rows, cut] = lowa
    writer.send(dgg.at[0:rows, cut], places[1].at[0:rows, cut])
    gfs[...] = gf
    writer.send(gfs, places[0])
    sums[0] = rows_sum(lowa.astype(F32))
    sums[6] = jnp.zeros_like(sums[0])
    sums[7] = sums[6]
    gc = mm_nt(lowa, wo_s[...].reshape(WIDTH, WIDTH)).astype(BF)
    hw = gctx.shape[2] // 2
    for rank in range(4):
        for half in range(2):
            gctx[rank, :, half * hw : (half + 1) * hw] = gc[half * BLK : (half + 1) * BLK, rank * hw : (rank + 1) * hw]
    writer.send(gctx, places[2])
    vecs = jnp.concatenate(sums, axis=0)
    ebs = jnp.concatenate([eb_s[:, (4 * (f % 2) + f // 2) * 96 : (4 * (f % 2) + f // 2 + 1) * 96] for f in range(8)], axis=1)
    dgg[rows:, 0:WIDTH] = jnp.concatenate([vecs, ebs], axis=0).astype(BF)
    dgg[rows:, WIDTH:] = jnp.zeros((16, 5 * WIDTH), BF)
    writer.send(dgg.at[rows:], places[1].at[rows:])
    writer.finish()


def wgrad_kernel(writer, places, meta, l_mine_from, l_other_from, dgg_from, dgg_other_from, *rest):
    t, a, b, dwo, d, l_mine, l_other, dgg, dgg_other, sems = rest[-10:]
    half = WIDTH // 2
    rows = l_mine.shape[0]

    def fetch(n, src, dst, at, width):
        copy = pltpu.make_async_copy(src.at[:, at : at + width], dst.at[:, at : at + width], sems.at[n])
        copy.start()
        return copy

    lefts = [fetch(n, src, dst, 0, WIDTH) for n, (src, dst) in enumerate(((l_mine_from, l_mine), (l_other_from, l_other)))]
    rights = {}
    for k in (3, 4, 1, 2, 0, 5):
        q = SWAPPED[k] if k < 4 else k
        rights[k] = [fetch(4 + k, dgg_from, dgg, k * WIDTH, WIDTH), fetch(10 + k, dgg_other_from, dgg_other, q * WIDTH, WIDTH)]
        if k == 3:
            acts = [
                fetch(2 + n, src, dst, WIDTH, 2 * WIDTH)
                for n, (src, dst) in enumerate(((l_mine_from, l_mine), (l_other_from, l_other)))
            ]

    def wait(copies):
        for copy in copies:
            copy.wait()

    def grad(left, left_other, right, right_other):
        return mm_nn(left, dgg[0:rows, right : right + WIDTH]) + mm_nn(
            left_other, dgg_other[0:rows, right_other : right_other + WIDTH]
        )

    def left(at, at_other):
        return l_mine[:, at : at + half].T, l_other[:, at_other : at_other + half].T

    wait(lefts)
    low = left(0, 0)
    for n, (p, out) in enumerate(((3, d), (1, a), (2, b), (0, t))):
        q = SWAPPED[p]
        wait(rights[p])
        out[:, 0] = grad(*low, p * WIDTH, q * WIDTH).reshape(4, 96, WIDTH).astype(BF)
        if n == 0:
            wait(acts)
            wait(rights[4])
        out[:, 1] = (
            grad(*left(WIDTH + p * half, WIDTH + q * half), 4 * WIDTH, 4 * WIDTH).reshape(4, 96, WIDTH).astype(BF)
        )
        writer.send(out, places[(4, 1, 2, 0)[n]])
    wait(rights[5])
    dwo[:, 0:96, :] = grad(*left(half, half), 5 * WIDTH, 5 * WIDTH).reshape(4, 96, WIDTH).astype(BF)
    vecs = dgg[rows:, 0:WIDTH].astype(F32) + dgg_other[rows:, 0:WIDTH].astype(F32)
    dwo[:, 96:, :] = jnp.zeros((4, 16, WIDTH), BF)
    for parity in range(2):

        @pl.when(meta[CORE] == parity)
        def _():
            for z in range(4):
                dwo[z, 96:, 0:96] = vecs[:, (2 * z + parity) * 96 : (2 * z + parity + 1) * 96].astype(BF)

    writer.send(dwo, places[3])
    writer.finish()


def place_kernel(
    meta, *rest, layer, last
):
    if last:
        parts = [((f.at[0], f.at[1]), a) for f, a in zip(rest[:4], rest[4:8])]
        small_in, rest = rest[8], rest[13:]
    else:
        parts = [((x.at[112:, 0:WIDTH], x.at[112:, WIDTH:]), x.at[0:112, :]) for x in rest[:4]]
        rest = rest[5:]
    e_hbm, r_hbm, i_hbm, o_hbm = rest[:4]
    smalls = rest[4:-10]
    e_s, i_s, b_s, e_out, r_out, i_out, o_out, small_s, eb_s, sems = rest[-10:]
    for p, (ffn, att) in enumerate(parts):
        rank = meta[RANK + p]
        r_out[pl.ds(pl.multiple_of(rank * 96, 96), 96), :] = ffn[1][...].astype(F32)
        e_s[rank] = ffn[0][...].astype(F32)
        i_s[rank] = att[0:96, WIDTH : WIDTH + 9 * HEAD_DIM].astype(F32)
        b_s[rank] = att[96:112, WIDTH : WIDTH + 9 * HEAD_DIM].astype(F32)
    copies = []

    def send(n, src, dst):
        copy = pltpu.make_async_copy(src, dst.at[layer], sems.at[n])
        copy.start()
        copies.append(copy)

    send(0, r_out, r_hbm)
    for f in range(8):
        at = (4 * (f % 2) + f // 2) * 96
        e_out[:, f * 384 : (f + 1) * 384] = jnp.concatenate([e_s[c, :, at : at + 96] for c in range(4)], axis=1)
    send(1, e_out, e_hbm)
    hw = WIDTH // 4
    for k in range(3):
        i_out[:, k * WIDTH : (k + 1) * WIDTH] = jnp.concatenate(
            [i_s[c, :, k * hw : (k + 1) * hw] for c in range(4)], axis=1
        )
    send(2, i_out, i_hbm)
    wo = [att[:, 0:WIDTH].astype(F32) for _, att in parts]
    total = (wo[0] + wo[1]) + (wo[2] + wo[3])
    o_out[...] = total[0:96, :]
    send(3, o_out, o_hbm)
    bias = b_s[lax.shift_right_logical(meta[SHARD], 1)]
    low_half = (meta[SHARD] & 1) == 0
    qb = jnp.where(low_half, bias[:, 0:96], bias[:, 96:192])
    vb = jnp.where(low_half, bias[:, 2 * hw : 2 * hw + 96], bias[:, 2 * hw + 96 : 3 * hw])
    rows = jnp.concatenate([total[96:102, 0:96], qb[0:1], vb[0:1], total[104:112, 0:96]], axis=0)
    if last:
        for n, ref in enumerate(smalls[:-1]):
            ref[...] = jnp.concatenate([rows[n : n + 1], small_in[n : n + 1, 0:96]], axis=0)
        smalls[-1][...] = jnp.concatenate(
            [
                jnp.concatenate([x[8 + c : 9 + c, 0:96] for c in range(4)], axis=1)
                for x in (rows, small_in[...])
            ],
            axis=0,
        )
    else:
        smalls[0][...] = rows
    for copy in copies:
        copy.wait()


def permutation(ctx, fsdp, move):
    return [
        (c * fsdp + f, move(c, f)[0] * fsdp + move(c, f)[1]) for c in range(ctx) for f in range(fsdp)
    ]


def add(*parts):
    total = parts[0].astype(F32)
    for part in parts[1:]:
        total = total + part.astype(F32)
    return total


def on_device_fast(
    activations, cotangent, doc_start, deal,
    attend_in, query_bias, value_bias, attend_out, attend_bias, first_gain, first_shift,
    expand_proj, expand_bias, reduce_proj, reduce_bias, second_gain, second_shift,
    *, ctx, fsdp,
):
    S = [pltpu.SMEM]
    V = [pltpu.VMEM]
    A = [pl.ANY]
    axes = ("ctx", "fsdp")

    def via(move):
        perm = permutation(ctx, fsdp, move)
        return lambda x: lax.ppermute(x, axes, perm)

    via_first = via(lambda c, f: (c ^ (1 + f % 2), f))
    via_second = via(lambda c, f: (c ^ (2 - f % 2), f))
    via_diagonal = via(lambda c, f: (c ^ 3, f))
    via_core = via(lambda c, f: (c, f ^ 1))
    via_z = [None] + [via(lambda c, f, k=k: (c, f ^ (2 * k))) for k in range(1, 4)]

    def exchange_ctx(own, a, b, d):
        return (own, via_first(a), via_second(b), via_diagonal(d))

    def spread_ctx(x):
        return (x, via_first(x), via_second(x), via_diagonal(x))

    def reduce_z(x):
        return lax.psum_scatter(x, "fsdp", scatter_dimension=0, tiled=True, axis_index_groups=zgroups)

    def exchange_z(own, *others):
        return (own,) + tuple(via_z[k + 1](x) for k, x in enumerate(others))

    def gather_ctx(x):
        a, b = via_first(x), via_second(x)
        return (x, a, b, via_second(a))

    heads = HEADS // ctx
    hw = heads * HEAD_DIM
    rows = activations.shape[1]
    tokens = rows * ctx
    cut = WIDTH // fsdp
    c = lax.axis_index("ctx").astype(jnp.int32)
    shard = lax.axis_index("fsdp").astype(jnp.int32)
    core = shard % 2
    zgroups = [[2 * z + k for z in range(fsdp // 2)] for k in range(2)]

    hidden = activations[0]
    gathered = gather_ctx(hidden)
    small = (attend_bias, first_gain, first_shift, reduce_bias, second_gain, second_shift, query_bias, value_bias)
    sent = call(
        prep_kernel,
        [((3 * cut, WIDTH), BF)] * 4,
        (expand_proj, reduce_proj, attend_in, attend_out, expand_bias) + small,
        V * 13,
        [],
        "prep",
        0,
        8 * 1024 * 1024,
    )

    def gather_ffn(x):
        x = lax.all_gather(x, "fsdp", axis=0, tiled=True)
        return x.reshape(fsdp // 2, 2, 3, cut, WIDTH)

    ranks = jnp.arange(ctx, dtype=jnp.int32)
    inv = jnp.sum(jnp.where(deal[None, :] == ranks[:, None], ranks[None, :], 0), axis=1).astype(jnp.int32)
    starts = lax.all_gather(doc_start[0], "ctx", axis=0, tiled=True)
    by_rank = starts.reshape(ctx, 2, BLK)
    chosen = inv[:, None, None, None] == ranks[None, :, None, None]
    by_block = jnp.sum(jnp.where(chosen, by_rank[None], 0), axis=1)
    logical = jnp.concatenate([by_block[:, 0], by_block[::-1, 1]], axis=0).reshape(-1)
    qrow = jnp.broadcast_to(logical[None, :], (8, tokens))
    kcol = jnp.broadcast_to(logical[:, None], (tokens, 128))
    jmin = jnp.min(logical.reshape(tokens // QB, QB), axis=1) // QB

    m1 = 1 + core
    mask = inv ^ c
    jmap = jnp.where((core == 1) & (mask > 0) & (mask < 3), 3 - mask, mask)
    meta = jnp.concatenate(
        [jnp.stack([core, shard, c, c ^ m1, c ^ (3 - m1), c ^ 3]), jmap, inv, jmin]
    ).astype(jnp.int32)

    kept = []
    earlier = ()
    wide = [gather_ffn(sent[0]), gather_ffn(sent[1]), None, None]
    wide[0] = after((wide[0],), starts, *gathered[1:])[0]
    wide[2] = gather_ffn(*after(sent[2:3], wide[0]))
    pieces = []
    for layer in range(LAYERS):
        t, d = wide[2 * layer : 2 * layer + 2]
        mine = half_of(meta, t, *gathered[1:])
        a, b = via_first(mine), via_second(mine)
        qkv, *ctx_own, lse = call(
            functools.partial(attn_fwd_kernel, heads=heads, tokens=tokens),
            [((ctx, rows, 3 * hw), BF)] + [((BLK, 2 * hw), BF)] * 4 + [((8, tokens), F32)],
            (meta,) + gathered + (qrow, kcol, t, mine) + earlier,
            S + V * 6 + A * (2 + len(earlier)),
            attn_fwd_scratch(heads, tokens),
            "attn_fwd",
            2 * tokens * WIDTH * 3 * hw * 4,
            10 * 1024 * 1024,
        )
        cx = exchange_ctx(*ctx_own)
        if layer + 1 < LAYERS:
            wide[3] = gather_ffn(*after(sent[3:4], *cx[1:]))
        pieces.append((t, a, b, d, via_core(pack(a, b, lse))))
        kinds = {
            "xhat": ((rows, WIDTH), F32), "rstd": ((rows, 1), F32), "gp": ((rows, 4 * WIDTH), BF),
            "left": ((rows, 3 * WIDTH), BF), "low": ((rows, WIDTH), BF),
        }
        norms = [kinds[name] for name in ("xhat", "rstd", "gp", "xhat", "rstd")]
        lows = [kinds[name] for name in ("left", "left", "low")]
        back_outs = [((rows, WIDTH), F32), ((rows + 16, 6 * WIDTH), BF), ((ctx, BLK, 2 * hw), BF)]
        if layer + 1 < LAYERS:
            xhat1, rstd1, gp, xhat2, rstd2, l_mine, l_other, hlow, hidden_next = call_writing(
                mlp_fwd_kernel,
                norms + lows + [kinds["xhat"]],
                (meta,) + cx + (hidden,) + pieces[layer],
                S + V * 5 + A * 5,
                mlp_fwd_scratch(rows, hw),
                "mlp_fwd",
                24,
            )
        else:
            xhat1 = rstd1 = gp = xhat2 = rstd2 = None
            l_mine, l_other, hlow, *last_back = call_writing(
                last_kernel,
                lows + back_outs,
                (meta,) + cx + (hidden, cotangent[0]) + pieces[layer],
                S + V * 6 + A * 5,
                [pltpu.VMEM(*kind) for kind in norms] + mlp_fwd_scratch(rows, hw) + [pltpu.VMEM((8, WIDTH), F32)],
                "last",
                36,
            )
        l_other = via_core(l_other)
        earlier = (l_other,)
        kept.append((gathered, qkv, ctx_own, lse, xhat1, rstd1, gp, xhat2, rstd2, l_mine, l_other))
        if layer + 1 < LAYERS:
            hidden = hidden_next
            gathered = gather_ctx(hlow)
    out_act = hlow[None]

    for layer in reversed(range(LAYERS)):
        gathered, qkv, ctx_own, lse, xhat1, rstd1, gp, xhat2, rstd2, l_mine, l_other = kept[layer]
        if layer + 1 == LAYERS:
            gfs, dgg, gctx = last_back
        else:
            gfs, dgg, gctx = call_writing(
                mlp_bwd_kernel,
                back_outs,
                (meta, xhat1, rstd1, xhat2, rstd2, gp) + grads + pieces[layer] + order,
                S + V * (5 + len(grads)) + A * (5 + len(order)),
                mlp_bwd_scratch(),
                "mlp_bwd",
                12,
                parts=len(grads),
            )
        gcx = lax.all_to_all(gctx, "ctx", 0, 0, tiled=True)
        piece = ((4, 2, cut, WIDTH), BF)

        def weight_grads(*before):
            return call_writing(
                wgrad_kernel,
                [piece] * 3 + [((4, cut + 16, WIDTH), BF), piece],
                (meta, l_mine, l_other, dgg, via_core(dgg)) + before,
                S + A * (4 + len(before)),
                wgrad_scratch(),
                "wgrad",
                5,
            )

        def attention_grads(*before):
            return call(
                functools.partial(attn_bwd_kernel, heads=heads, tokens=tokens),
                [
                    ((rows, WIDTH), F32), ((rows, WIDTH), BF), ((rows, WIDTH), BF), ((rows, WIDTH), BF),
                    ((4, cut + 16, 3 * hw), BF), ((4, cut + 16, 3 * hw), BF),
                ],
                (meta,) + gathered + (qrow, kcol, qkv) + tuple(ctx_own) + (gcx, lse, wide[2 * layer]) + before,
                S + V * 13 + A * (1 + len(before)),
                attn_bwd_scratch(heads, tokens),
                "attn_bwd",
                2 * tokens * WIDTH * 3 * hw * 8,
                10 * 1024 * 1024,
            )

        def attention_shards(dwo, dw, crossed, *others):
            shape = (4, cut + 16, WIDTH + 3 * hw)
            (merged,) = call(
                merge_kernel, [(shape, BF)], (dwo, dw, crossed) + others, V * 3 + A * len(others), [], "merge", 0, 0
            )
            return merged, reduce_z(merged).reshape(shape[1:])

        if layer > 0:
            g_own, g_a, g_b, g_d, dw, dw_other = attention_grads(l_other)
            (over,) = sums([[(g_a, via_second(g_d))]])
            t, a, b, dwo, d = weight_grads(over)
            d1 = reduce_z(d)
            over = via_first(over)
            merged, att1 = attention_shards(dwo, dw, via_core(dw_other))
            back = via_second(g_b)
            grads = (gfs, g_own, back, over)
            a, b = after((a, b), over, back)
            order = (merged, a, b)
            parts1 = (t, via_first(a), via_second(b))
        else:
            (t1,) = sums([[parts1]], gcx, weight=WEIGHT)
            t, a, b, dwo, d = weight_grads(gcx, att1, t1)
            t1 = reduce_z(t1)
            from_b, from_d = via_second(b), via_second(d)
            g_own, g_a, g_b, g_d, dw, dw_other = attention_grads(t)

    def shards(x):
        return x.reshape(2, cut, WIDTH)

    a0, t0 = sums([[(a, from_d)], [(t, from_b)]], g_d, weight=WEIGHT)
    from_a = via_first(a0)
    merged, att0 = attention_shards(dwo, dw, via_core(dw_other), a0)
    back = via_second(g_d), via_second(g_b)
    shape = (2 * cut + 16, 2 * WIDTH)
    (joined,) = call(
        join_kernel, [(shape, BF)], (att1, shards(t1), shards(via_diagonal(d1)), merged), V * 3 + A, [], "join", WEIGHT, 0
    )
    (over,) = sums([[(g_a, back[0])]], joined)
    joined = spread_ctx(joined)
    (t0,) = sums([[(t0, from_a)]], over, weight=WEIGHT)
    over = via_first(over)
    ffn0 = shards(reduce_z(t0))

    small_out = None
    placed = []
    for layer in reversed(range(LAYERS)):
        if layer == 0:
            sent = spread_ctx(ffn0) + spread_ctx(att0)
            waits = ()
        else:
            sent = joined
            waits = (t0,)
        last = layer == 0
        big = [
            ((LAYERS, cut, 4 * WIDTH), F32), ((LAYERS, 4 * cut, WIDTH), F32),
            ((LAYERS, cut, 3 * WIDTH), F32), ((LAYERS, cut, WIDTH), F32),
        ]
        if last:
            smalls = [((LAYERS, cut), F32)] * 8 + [((LAYERS, 4 * cut), F32)]
        else:
            smalls = [((16, cut), F32)]
        args = (meta,) + sent + ((small_out,) + tuple(placed) if last else waits)
        spaces = S + V * len(sent) + (V + A * 4 if last else A)
        outs = pl.pallas_call(
            functools.partial(place_kernel, layer=layer, last=last),
            out_shape=[jax.ShapeDtypeStruct(shape, dtype) for shape, dtype in big + smalls],
            in_specs=[pl.BlockSpec(memory_space=space) for space in spaces],
            out_specs=[pl.BlockSpec(memory_space=space) for space in A * 4 + V * len(smalls)],
            scratch_shapes=[
                pltpu.VMEM((ctx, cut, WIDTH), F32), pltpu.VMEM((ctx, cut, 3 * hw), F32),
                pltpu.VMEM((ctx, 16, 3 * hw), F32),
                pltpu.VMEM((cut, 4 * WIDTH), F32), pltpu.VMEM((4 * cut, WIDTH), F32),
                pltpu.VMEM((cut, 3 * WIDTH), F32), pltpu.VMEM((cut, WIDTH), F32),
                pltpu.VMEM((16, 128), F32), pltpu.VMEM((8, 128), F32),
                pltpu.SemaphoreType.DMA((4,)),
            ],
            input_output_aliases={10 + n: n for n in range(4)} if last else {},
            compiler_params=pltpu.CompilerParams(vmem_limit_bytes=VMEM_LIMIT),
            cost_estimate=pl.CostEstimate(flops=0, bytes_accessed=10 * 1024 * 1024, transcendentals=0),
            name="place",
        )(*args)
        placed = outs[:4]
        small_out = outs[4]
        vectors = outs[4:]
    in_grad = add(gfs, g_own, back[1], over)[None]
    e_out, r_out, i_out, o_out = placed
    ab, fg, fs, rb, sg, ss, qb, vb, xb = vectors
    return (out_act, in_grad, i_out, qb, vb, o_out, ab, fg, fs, e_out, xb, r_out, rb, sg, ss)


def on_device(*args, ctx, fsdp):
    if ctx == 4 and fsdp == 8 and args[0].shape[1] == 2 * BLK:
        return on_device_fast(*args, ctx=ctx, fsdp=fsdp)
    return on_device_plain(*args)


def solution(mesh):
    placed = (
        P("fsdp", "ctx", None),
        P("fsdp", "ctx", None),
        P("fsdp", "ctx"),
        P(),
        P(None, "fsdp", None),
        P(None, "fsdp"),
        P(None, "fsdp"),
        P(None, "fsdp", None),
        P(None, "fsdp"),
        P(None, "fsdp"),
        P(None, "fsdp"),
        P(None, "fsdp", None),
        P(None, "fsdp"),
        P(None, "fsdp", None),
        P(None, "fsdp"),
        P(None, "fsdp"),
        P(None, "fsdp"),
    )
    return jax.shard_map(
        functools.partial(on_device, ctx=mesh.shape["ctx"], fsdp=mesh.shape["fsdp"]),
        mesh=mesh,
        in_specs=placed,
        out_specs=(
            P("fsdp", "ctx", None),
            P("fsdp", "ctx", None),
            P(None, "fsdp", None),
            P(None, "fsdp"),
            P(None, "fsdp"),
            P(None, "fsdp", None),
            P(None, "fsdp"),
            P(None, "fsdp"),
            P(None, "fsdp"),
            P(None, "fsdp", None),
            P(None, "fsdp"),
            P(None, "fsdp", None),
            P(None, "fsdp"),
            P(None, "fsdp"),
            P(None, "fsdp"),
        ),
        check_vma=False,
    )
```

profile of v0, /device:TPU:1, one launch (start us, length us, event | category | flops | bytes accessed | tf_op | source)
XLA Modules:
  0.0 472.7 jit_solution(1930355976170147817)
XLA Ops:
  7.3 3.8 prep.1
  14.7 16.6 %all-gather = s32[1,1536]{1,0:T(1,128)S(1)} all-gather(s32[1,384]{1,0:T(1,128)S(1)} %copy-done.34), channel_id=2, replica_groups=mesh['ctx'=4,'fsdp'=8] {'ctx'}, dimensions={1}, use_global_device_ids=true | all-gather | bytes 7680 | tf_op jit(solution)/shard_map/all_gather | solution.py:1339
  32.8 8.1 %collective-permute-done.2.refs_4_.rest_2_.h3 = bf16[384,768]{1,0:T(8,128)(2,1)S(1)} collective-permute-done((bf16[384,768]{1,0:T(8,128)(2,1)S(1)}, bf16[384,768]{1,0:T(8,128)(2,1)S(1)}, u32[]{:S(2)}, u32[]{:S(2)}) %collective-permute-start.2) | collective-permute-done | bytes 589856 | tf_op jit(solution)/shard_map/ppermute | solution.py:1285
  40.8 14.4 %all-gather.6.cloned.1.call-done = bf16[2304,768]{1,0:T(8,128)(2,1)} async-done(((bf16[288,768]{1,0:T(8,128)(2,1)}), bf16[2304,768]{1,0:T(8,128)(2,1)}) %all-gather.6.cloned.1.call-update) | async-done | bytes 3538960 | tf_op jit(solution)/shard_map/all_gather | solution.py:1334
  62.2 14.9 %attn_fwd.2 = (bf16[4,384,576]{2,1,0:T(8,128)(2,1)}, bf16[192,384]{1,0:T(8,128)(2,1)}, bf16[192,384]{1,0:T(8,128)(2,1)}, bf16[192,384]{1,0:T(8,128)(2,1)}, bf16[192,384]{1,0:T(8,128)(2,1)}, /*index=5*/f32[8,1536]{1,0:T(8,128)}) custom-call(s32[20]{0:T(128)} %concatenate.7.meta.refs_0_, bf16[384,768]{1,0:T(8,128)(2,1)} %bitcast.31, ...), custom_call_target="tpu_custom_call" | custom-call | tf_op jit(solution)/shard_map/attn_fwd/pallas_call | solution.py:447
  80.0 4.1 collective-permute-done.7.b.refs_8_.refs_12_
  93.4 4.6 all-gather.8.cloned.1.call-done
  99.3 13.7 %mlp_fwd.1 = (f32[384,768]{1,0:T(8,128)}, f32[384,1]{1,0:T(8,128)}, bf16[384,3072]{1,0:T(8,128)(2,1)}, f32[384,768]{1,0:T(8,128)}, f32[384,1]{1,0:T(8,128)}, /*i...) custom-call(s32[20]{0:T(128)} %concatenate.7.meta.refs_0_, ...), custom_call_target="tpu_custom_call" | custom-call | tf_op jit(solution)/shard_map/mlp_fwd/pallas_call | solution.py:528
  115.4 11.0 %collective-permute-done.9.rest_0_.h1 = bf16[384,768]{1,0:T(8,128)(2,1)S(1)} collective-permute-done((bf16[384,768]{1,0:T(8,128)(2,1)}, bf16[384,768]{1,0:T(8,128)(2,1)S(1)}, u32[]{:S(2)}, u32[]{:S(2)}) %collective-permute-start.9) | collective-permute-done | bytes 589856 | tf_op jit(solution)/shard_map/ppermute | solution.py:1285
  130.8 5.5 %collective-permute-done.11.rest_2_.h3 = bf16[384,768]{1,0:T(8,128)(2,1)S(1)} collective-permute-done((bf16[384,768]{1,0:T(8,128)(2,1)S(1)}, bf16[384,768]{1,0:T(8,128)(2,1)S(1)}, u32[]{:S(2)}, u32[]{:S(2)}) %collective-permute-start.11) | collective-permute-done | bytes 589856 | tf_op jit(solution)/shard_map/ppermute | solution.py:1285
  136.3 3.7 all-gather.10.cloned.1.call-done
  146.4 15.3 %attn_fwd.3 = (bf16[4,384,576]{2,1,0:T(8,128)(2,1)}, bf16[192,384]{1,0:T(8,128)(2,1)}, bf16[192,384]{1,0:T(8,128)(2,1)}, bf16[192,384]{1,0:T(8,128)(2,1)}, bf16[192,384]{1,0:T(8,128)(2,1)}, /*index=5*/f32[8,1536]{1,0:T(8,128)}) custom-call(s32[20]{0:T(128)} %concatenate.7.meta.refs_0_, bf16[384,768]{1,0:T(8,128)(2,1)} %get-tuple-element.100.h0, ...), custom_call_target="tpu_custom_call" | custom-call | tf_op jit(solution)/shard_map/attn_fwd/pallas_call | solution.py:447
  161.7 7.1 %collective-permute-done.17.b.refs_9_ = bf16[4,2,96,768]{3,2,1,0:T(8,128)(2,1)S(1)} collective-permute-done((bf16[4,2,96,768]{3,2,1,0:T(8,128)(2,1)}, bf16[4,2,96,768]{3,2,1,0:T(8,128)(2,1)S(1)}, u32[]{:S(2)}, u32[]{:S(2)}) %collective-permute-start.17) | collective-permute-done | bytes 1179680 | tf_op jit(solution)/shard_map/ppermute | solution.py:1285
  177.9 4.0 all-gather.12.cloned.1.call-done
  186.9 19.2 %last.1 = (bf16[384,2304]{1,0:T(8,128)(2,1)}, bf16[384,2304]{1,0:T(8,128)(2,1)}, bf16[384,768]{1,0:T(8,128)(2,1)}, f32[384,768]{1,0:T(8,128)}, bf16[400,4608]{1,0:T(8,128)(2,1)}, /*index=5*/bf16[4,192,384]{2,1,0:T(8,128)(2,1)}) custom-call(s32[20]{0:T(128)} %concatenate.7.meta.refs_0_, bf16[192,384]{1,0:T(8,128)(2,1)} %get-tuple-element.103.refs_1_.c0, ...), custom_call_target="tpu_custom_call" | custom-call | tf_op jit(solution)/shard_map/last/pallas_call | solution.py:528
  206.9 12.8 %all_to_all.10.gctx = bf16[4,192,384]{2,1,0:T(8,128)(2,1)} all-to-all(bf16[4,192,384]{2,1,0:T(8,128)(2,1)} %get-tuple-element.118), channel_id=1, replica_groups=mesh['ctx'=4,'fsdp'=8] {'ctx'}, dimensions={0} | all-to-all | bytes 1179648 | tf_op jit(solution)/shard_map/all_to_all | solution.py:1430
  221.0 23.2 %attn_bwd.2 = (f32[384,768]{1,0:T(8,128)}, bf16[384,768]{1,0:T(8,128)(2,1)}, bf16[384,768]{1,0:T(8,128)(2,1)}, bf16[384,768]{1,0:T(8,128)(2,1)}, bf16[4,112,576]...) custom-call(s32[20]{0:T(128)} %concatenate.7.meta.refs_0_, bf16[384,768]{1,0:T(8,128)(2,1)} %get-tuple-element.100.h0, ...), custom_call_target="tpu_custom_call" | custom-call | tf_op jit(solution)/shard_map/attn_bwd/pallas_call | solution.py:447
  245.8 7.8 %collective-permute-done.21.refs_1_ = bf16[384,768]{1,0:T(8,128)(2,1)S(1)} collective-permute-done((bf16[384,768]{1,0:T(8,128)(2,1)}, bf16[384,768]{1,0:T(8,128)(2,1)S(1)}, u32[]{:S(2)}, u32[]{:S(2)}) %collective-permute-start.21) | collective-permute-done | bytes 589856 | tf_op jit(solution)/shard_map/ppermute | solution.py:1285
  257.5 5.0 %collective-permute-start.24 = (bf16[4,112,576]{2,1,0:T(8,128)(2,1)S(1)}, bf16[4,112,576]{2,1,0:T(8,128)(2,1)S(1)}, u32[]{:S(2)}, u32[]{:S(2)}) collective-permute-start(bf16[4,112,576]{2,1,0:T(8,128)(2,1)S(1)} %copy-done.40), channel_id=1, source_target_pairs={{0,1},{1,0},{2,3},{3,2},{4,5},{5,4},{6,7},{7,6},{8,9},{9,8},{10,11... | collective-permute-start | bytes 1548296 | tf_op jit(solution)/shard_map/ppermute | solution.py:1285
  262.5 10.8 %wgrad.2 = (bf16[4,2,96,768]{3,2,1,0:T(8,128)(2,1)}, bf16[4,2,96,768]{3,2,1,0:T(8,128)(2,1)}, bf16[4,2,96,768]{3,2,1,0:T(8,128)(2,1)}, bf16[4,112,768]{2,1,0:T(8,128)(2,1)}, bf16[4,2,96,768]{3,2,1,0:T(8,128)(2,1)}) custom-call(s32[20]{0:T(128)} %concatenate.7.meta.refs_0_, bf16[384,2304]{1,0:T(8,128)(2,1)} %get-tuple-element.124.refs_1_, ...), custom_call_target="tpu_custom_call" | custom-call | tf_op jit(solution)/shard_map/wgrad/pallas_call | solution.py:528
  279.3 16.0 %mlp_bwd.1 = (f32[384,768]{1,0:T(8,128)}, bf16[400,4608]{1,0:T(8,128)(2,1)}, bf16[4,192,384]{2,1,0:T(8,128)(2,1)}) custom-call(s32[20]{0:T(128)} %concatenate.7.meta.refs_0_, f32[384,768]{1,0:T(8,128)} %get-tuple-element.111.refs_1_, f32[384,1]{1,0:T(8,128)} %get-tuple-element.112.refs_2_, f32[384,768]{1,0:T(8,128)} %get-tuple-element.113.refs_3_, ...), custom_call_target="tpu_custom_call" | custom-call | tf_op jit(solution)/shard_map/mlp_bwd/pallas_call | solution.py:528
  299.6 13.0 %all-to-all-done.1.refs_3_.refs_5_.gctx = bf16[4,192,384]{2,1,0:T(8,128)(2,1)S(1)} async-done(((bf16[4,192,384]{2,1,0:T(8,128)(2,1)}), bf16[4,192,384]{2,1,0:T(8,128)(2,1)S(1)}, u32[]{:S(2)}, u32[]{:S(2)}) %all-to-all-start.1) | async-done | bytes 589856 | tf_op jit(solution)/shard_map/all_to_all | solution.py:1430
  317.6 10.6 %wgrad.3 = (bf16[4,2,96,768]{3,2,1,0:T(8,128)(2,1)}, bf16[4,2,96,768]{3,2,1,0:T(8,128)(2,1)}, bf16[4,2,96,768]{3,2,1,0:T(8,128)(2,1)}, bf16[4,112,768]{2,1,0:T(8,128)(2,1)}, bf16[4,2,96,768]{3,2,1,0:T(8,128)(2,1)}) custom-call(s32[20]{0:T(128)} %concatenate.7.meta.refs_0_, bf16[384,2304]{1,0:T(8,128)(2,1)} %get-tuple-element.136.refs_1_, ...), custom_call_target="tpu_custom_call" | custom-call | tf_op jit(solution)/shard_map/wgrad/pallas_call | solution.py:528
  330.1 5.1 %reduce-scatter.10.cloned.1.call-done = bf16[1,2,96,768]{3,2,1,0:T(8,128)(2,1)} async-done(((bf16[4,2,96,768]{3,2,1,0:T(8,128)(2,1)}), bf16[1,2,96,768]{3,2,1,0:T(8,128)(2,1)}) %reduce-scatter.10.cloned.1.call-update) | async-done | bytes 294928 | tf_op jit(solution)/shard_map/reduce_scatter | solution.py:1300
  337.3 23.0 %attn_bwd.3 = (f32[384,768]{1,0:T(8,128)}, bf16[384,768]{1,0:T(8,128)(2,1)}, bf16[384,768]{1,0:T(8,128)(2,1)}, bf16[384,768]{1,0:T(8,128)(2,1)}, bf16[4,112,576]...) custom-call(s32[20]{0:T(128)} %concatenate.7.meta.refs_0_, bf16[384,768]{1,0:T(8,128)(2,1)} %bitcast.33, ...), custom_call_target="tpu_custom_call" | custom-call | tf_op jit(solution)/shard_map/attn_bwd/pallas_call | solution.py:447
  360.4 3.8 collective-permute-start.31
  365.8 4.0 sums.7
  378.7 8.0 %collective-permute-done.35.refs_1_ = bf16[4,2,96,768]{3,2,1,0:T(8,128)(2,1)S(1)} collective-permute-done((bf16[4,2,96,768]{3,2,1,0:T(8,128)(2,1)}, bf16[4,2,96,768]{3,2,1,0:T(8,128)(2,1)S(1)}, u32[]{:S(2)}, u32[]{:S(2)}) %collective-permute-start.35) | collective-permute-done | bytes 1179680 | tf_op jit(solution)/shard_map/ppermute | solution.py:1285
  394.8 9.6 %collective-permute-done.28 = bf16[384,768]{1,0:T(8,128)(2,1)} collective-permute-done((bf16[384,768]{1,0:T(8,128)(2,1)}, bf16[384,768]{1,0:T(8,128)(2,1)}, u32[]{:S(2)}, u32[]{:S(2)}) %collective-permute-start.28) | collective-permute-done | bytes 589856 | tf_op jit(solution)/shard_map/ppermute | solution.py:1285
  405.0 36.3 %collective-permute-done.34 = bf16[384,768]{1,0:T(8,128)(2,1)} collective-permute-done((bf16[384,768]{1,0:T(8,128)(2,1)}, bf16[384,768]{1,0:T(8,128)(2,1)}, u32[]{:S(2)}, u32[]{:S(2)}) %collective-permute-start.34) | collective-permute-done | bytes 589856 | tf_op jit(solution)/shard_map/ppermute | solution.py:1285
  447.9 4.9 %place.2 = (f32[2,96,3072]{2,1,0:T(8,128)}, f32[2,384,768]{2,1,0:T(8,128)}, f32[2,96,2304]{2,1,0:T(8,128)}, f32[2,96,768]{2,1,0:T(8,128)}, f32[16,96]{1,0:T(8,128)}) custom-call(s32[20]{0:T(128)} %concatenate.7.meta.refs_0_, bf16[208,1536]{1,0:T(8,128)(2,1)} %join.1.refs_2_.rest_0_, bf16[208,1536]{1,0:T(8,128)(2,1)} %collective-permute-done.42.rest_1_, ...), custom_call_target="tpu_custom_call" | custom-call | bytes 10485760 | tf_op jit(solution)/shard_map/place/pallas_call | solution.py:1522
  460.9 4.9 %place.3 = (f32[2,96,3072]{2,1,0:T(8,128)}, f32[2,384,768]{2,1,0:T(8,128)}, f32[2,96,2304]{2,1,0:T(8,128)}, f32[2,96,768]{2,1,0:T(8,128)}, f32[2,96]{1,0:T(2,128...) custom-call(s32[20]{0:T(128)} %concatenate.7.meta.refs_0_, ...), custom_call_target="tpu_custom_call", output_to_operand_aliasing={{0}: (10, {}), {1}: (11, {}), {2}: (12, {}), {3}: (13, {})} | custom-call | bytes 10485760 | tf_op jit(solution)/shard_map/place/pallas_call | solution.py:1522
  (222 shorter events, 113.2 us)
Async XLA Ops:
  7.2 48.0 %all-gather.6.cloned.1.call-start = ((), (), s32[]{:S(2)}) async-start(), calls=%async_computation.7 | async-start | bytes 3981312 | tf_op jit(solution)/shard_map/all_gather | solution.py:1334
  11.1 86.8 %all-gather.8.cloned.1.call-start = ((), (), s32[]{:S(2)}) async-start(), calls=%async_computation.8 | async-start | bytes 3981312 | tf_op jit(solution)/shard_map/all_gather | solution.py:1334
  11.1 21.6 %collective-permute-start.1 = (bf16[384,768]{1,0:T(8,128)(2,1)S(1)}, bf16[384,768]{1,0:T(8,128)(2,1)S(1)}, u32[]{:S(2)}, u32[]{:S(2)}) collective-permute-start(bf16[384,768]{1,0:T(8,128)(2,1)S(1)} %bitcast.34), channel_id=1, source_target_pairs={{0,16},{1,9},{2,18},{3,11},{4,20},{5,13},{6,22},{7,15},{8,24},{9,1... | collective-permute-start | bytes 1769480 | tf_op jit(solution)/shard_map/ppermute | solution.py:1285
  13.4 18.2 %collective-permute-start = (bf16[384,768]{1,0:T(8,128)(2,1)S(1)}, bf16[384,768]{1,0:T(8,128)(2,1)S(1)}, u32[]{:S(2)}, u32[]{:S(2)}) collective-permute-start(bf16[384,768]{1,0:T(8,128)(2,1)S(1)} %bitcast.35), channel_id=1, source_target_pairs={{0,8},{1,17},{2,10},{3,19},{4,12},{5,21},{6,14},{7,23},{8,0},{9,25... | collective-permute-start | bytes 1769480 | tf_op jit(solution)/shard_map/ppermute | solution.py:1285
  14.5 125.5 %all-gather.10.cloned.1.call-start = ((), (), s32[]{:S(2)}) async-start(), calls=%async_computation.9 | async-start | bytes 3981312 | tf_op jit(solution)/shard_map/all_gather | solution.py:1334
  58.0 26.1 %collective-permute-start.7 = (bf16[4,2,96,768]{3,2,1,0:T(8,128)(2,1)}, bf16[4,2,96,768]{3,2,1,0:T(8,128)(2,1)S(1)}, u32[]{:S(2)}, u32[]{:S(2)}) collective-permute-start(bf16[4,2,96,768]{3,2,1,0:T(8,128)(2,1)} %half.2.rest_0_), channel_id=1, source_target_pairs={{0,16},{1,9},{2,18},{3,11},{4,20},{5,13},{6,22},{7,15},{8,24},{9,1... | collective-permute-start | bytes 3538952 | tf_op jit(solution)/shard_map/ppermute | solution.py:1285
  59.3 28.2 %collective-permute-start.6 = (bf16[4,2,96,768]{3,2,1,0:T(8,128)(2,1)}, bf16[4,2,96,768]{3,2,1,0:T(8,128)(2,1)S(1)}, u32[]{:S(2)}, u32[]{:S(2)}) collective-permute-start(bf16[4,2,96,768]{3,2,1,0:T(8,128)(2,1)} %half.2.rest_0_), channel_id=1, source_target_pairs={{0,8},{1,17},{2,10},{3,19},{4,12},{5,21},{6,14},{7,23},{8,0},{9,25... | collective-permute-start | bytes 3538952 | tf_op jit(solution)/shard_map/ppermute | solution.py:1285
  79.9 102.0 %all-gather.12.cloned.1.call-start = ((), (), s32[]{:S(2)}) async-start(), calls=%async_computation.10 | async-start | bytes 3981312 | tf_op jit(solution)/shard_map/all_gather | solution.py:1334
  93.3 224.3 %reduce-scatter.6.cloned.1.call-start = ((), (), s32[]{:S(2)}) async-start(), calls=%async_computation.11 | async-start | bytes 1576960 | tf_op jit(solution)/shard_map/reduce_scatter | solution.py:1300
  128.6 16.6 %collective-permute-start.12 = (bf16[384,2304]{1,0:T(8,128)(2,1)}, bf16[384,2304]{1,0:T(8,128)(2,1)S(1)}, u32[]{:S(2)}, u32[]{:S(2)}) collective-permute-start(bf16[384,2304]{1,0:T(8,128)(2,1)} %get-tuple-element.102), channel_id=1, source_target_pairs={{0,1},{1,0},{2,3},{3,2},{4,5},{5,4},{6,7},{7,6},{8,9},{9,8},{10,11... | collective-permute-start | bytes 5308424 | tf_op jit(solution)/shard_map/ppermute | solution.py:1285
  142.7 26.1 %collective-permute-start.17 = (bf16[4,2,96,768]{3,2,1,0:T(8,128)(2,1)}, bf16[4,2,96,768]{3,2,1,0:T(8,128)(2,1)S(1)}, u32[]{:S(2)}, u32[]{:S(2)}) collective-permute-start(bf16[4,2,96,768]{3,2,1,0:T(8,128)(2,1)} %half.3.rest_0_), channel_id=1, source_target_pairs={{0,16},{1,9},{2,18},{3,11},{4,20},{5,13},{6,22},{7,15},{8,24},{9,1... | collective-permute-start | bytes 3538952 | tf_op jit(solution)/shard_map/ppermute | solution.py:1285
  144.0 27.8 %collective-permute-start.16 = (bf16[4,2,96,768]{3,2,1,0:T(8,128)(2,1)}, bf16[4,2,96,768]{3,2,1,0:T(8,128)(2,1)}, u32[]{:S(2)}, u32[]{:S(2)}) collective-permute-start(bf16[4,2,96,768]{3,2,1,0:T(8,128)(2,1)} %half.3.rest_0_), channel_id=1, source_target_pairs={{0,8},{1,17},{2,10},{3,19},{4,12},{5,21},{6,14},{7,23},{8,0},{9,25... | collective-permute-start | bytes 3538952 | tf_op jit(solution)/shard_map/ppermute | solution.py:1285
  206.1 56.4 %collective-permute-start.23 = (bf16[400,4608]{1,0:T(8,128)(2,1)}, bf16[400,4608]{1,0:T(8,128)(2,1)}, u32[]{:S(2)}, u32[]{:S(2)}) collective-permute-start(bf16[400,4608]{1,0:T(8,128)(2,1)} %get-tuple-element.125.refs_3_), channel_id=1, source_target_pairs={{0,1},{1,0},{2,3},{3,2},{4,5},{5,4},{6,7},{7,6},{8,9},{9,8},{10,11... | collective-permute-start | bytes 11059208 | tf_op jit(solution)/shard_map/ppermute | solution.py:1285
  244.9 31.9 %collective-permute-start.20 = (bf16[384,768]{1,0:T(8,128)(2,1)}, bf16[384,768]{1,0:T(8,128)(2,1)S(1)}, u32[]{:S(2)}, u32[]{:S(2)}) collective-permute-start(bf16[384,768]{1,0:T(8,128)(2,1)} %get-tuple-element.121), channel_id=1, source_target_pairs={{0,16},{1,9},{2,18},{3,11},{4,20},{5,13},{6,22},{7,15},{8,24},{9,1... | collective-permute-start | bytes 1769480 | tf_op jit(solution)/shard_map/ppermute | solution.py:1285
  256.6 20.3 %collective-permute-start.22 = (bf16[384,768]{1,0:T(8,128)(2,1)}, bf16[384,768]{1,0:T(8,128)(2,1)S(1)}, u32[]{:S(2)}, u32[]{:S(2)}) collective-permute-start(bf16[384,768]{1,0:T(8,128)(2,1)} %sums.5.refs_5_), channel_id=1, source_target_pairs={{0,8},{1,17},{2,10},{3,19},{4,12},{5,21},{6,14},{7,23},{8,0},{9,25... | collective-permute-start | bytes 1769480 | tf_op jit(solution)/shard_map/ppermute | solution.py:1285
  277.9 34.7 %collective-permute-start.26 = (bf16[4,2,96,768]{3,2,1,0:T(8,128)(2,1)}, bf16[4,2,96,768]{3,2,1,0:T(8,128)(2,1)S(1)}, u32[]{:S(2)}, u32[]{:S(2)}) collective-permute-start(bf16[4,2,96,768]{3,2,1,0:T(8,128)(2,1)} %get-tuple-element.131.refs_16_), channel_id=1, source_target_pairs={{0,8},{1,17},{2,10},{3,19},{4,12},{5,21},{6,14},{7,23},{8,0},{9,25... | collective-permute-start | bytes 3538952 | tf_op jit(solution)/shard_map/ppermute | solution.py:1285
  278.2 34.4 %collective-permute-start.27 = (bf16[4,2,96,768]{3,2,1,0:T(8,128)(2,1)}, bf16[4,2,96,768]{3,2,1,0:T(8,128)(2,1)S(1)}, u32[]{:S(2)}, u32[]{:S(2)}) collective-permute-start(bf16[4,2,96,768]{3,2,1,0:T(8,128)(2,1)} %get-tuple-element.132.refs_17_), channel_id=1, source_target_pairs={{0,16},{1,9},{2,18},{3,11},{4,20},{5,13},{6,22},{7,15},{8,24},{9,1... | collective-permute-start | bytes 3538952 | tf_op jit(solution)/shard_map/ppermute | solution.py:1285
  295.4 17.2 %all-to-all-start.1 = ((bf16[4,192,384]{2,1,0:T(8,128)(2,1)}), bf16[4,192,384]{2,1,0:T(8,128)(2,1)S(1)}, u32[]{:S(2)}, u32[]{:S(2)}) async-start(bf16[4,192,384]{2,1,0:T(8,128)(2,1)} %get-tuple-element.135), calls=%async_computation.1 | async-start | bytes 1179648 | tf_op jit(solution)/shard_map/all_to_all | solution.py:1430
  298.9 36.3 %reduce-scatter.10.cloned.1.call-start = ((), (), s32[]{:S(2)}) async-start(), calls=%async_computation.13 | async-start | bytes 1474560 | tf_op jit(solution)/shard_map/reduce_scatter | solution.py:1300
  298.9 18.7 %collective-permute-start.25 = (bf16[400,4608]{1,0:T(8,128)(2,1)}, bf16[400,4608]{1,0:T(8,128)(2,1)}, u32[]{:S(2)}, u32[]{:S(2)}) collective-permute-start(bf16[400,4608]{1,0:T(8,128)(2,1)} %get-tuple-element.137.refs_3_), channel_id=1, source_target_pairs={{0,1},{1,0},{2,3},{3,2},{4,5},{5,4},{6,7},{7,6},{8,9},{9,8},{10,11... | collective-permute-start | bytes 11059208 | tf_op jit(solution)/shard_map/ppermute | solution.py:1285
  299.6 74.2 %reduce-scatter.8.cloned.1.call-start = ((), (), s32[]{:S(2)}) async-start(), calls=%async_computation.12 | async-start | bytes 1474560 | tf_op jit(solution)/shard_map/reduce_scatter | solution.py:1300
  328.2 36.2 %collective-permute-start.32 = (bf16[4,2,96,768]{3,2,1,0:T(8,128)(2,1)}, bf16[4,2,96,768]{3,2,1,0:T(8,128)(2,1)S(1)}, u32[]{:S(2)}, u32[]{:S(2)}) collective-permute-start(bf16[4,2,96,768]{3,2,1,0:T(8,128)(2,1)} %get-tuple-element.149), channel_id=1, source_target_pairs={{0,16},{1,9},{2,18},{3,11},{4,20},{5,13},{6,22},{7,15},{8,24},{9,1... | collective-permute-start | bytes 3538952 | tf_op jit(solution)/shard_map/ppermute | solution.py:1285
  329.5 35.0 %collective-permute-start.33 = (bf16[4,2,96,768]{3,2,1,0:T(8,128)(2,1)}, bf16[4,2,96,768]{3,2,1,0:T(8,128)(2,1)S(1)}, u32[]{:S(2)}, u32[]{:S(2)}) collective-permute-start(bf16[4,2,96,768]{3,2,1,0:T(8,128)(2,1)} %get-tuple-element.150), channel_id=1, source_target_pairs={{0,16},{1,9},{2,18},{3,11},{4,20},{5,13},{6,22},{7,15},{8,24},{9,1... | collective-permute-start | bytes 3538952 | tf_op jit(solution)/shard_map/ppermute | solution.py:1285
  329.8 74.5 %reduce-scatter.14.cloned.1.call-start = ((), (), s32[]{:S(2)}) async-start(), calls=%async_computation.15 | async-start | bytes 1576960 | tf_op jit(solution)/shard_map/reduce_scatter | solution.py:1300
  335.2 38.5 %collective-permute-start.30 = (bf16[1,2,96,768]{3,2,1,0:T(8,128)(2,1)}, bf16[1,2,96,768]{3,2,1,0:T(8,128)(2,1)S(1)}, u32[]{:S(2)}, u32[]{:S(2)}) collective-permute-start(bf16[1,2,96,768]{3,2,1,0:T(8,128)(2,1)} %reduce-scatter.10.cloned.1.call-done), channel_id=1, source_target_pairs={{0,24},{1,25},{2,26},{3,27},{4,28},{5,29},{6,30},{7,31},{8,16},{9,... | collective-permute-start | bytes 884744 | tf_op jit(solution)/shard_map/ppermute | solution.py:1285
  369.8 16.8 %collective-permute-start.35 = (bf16[4,2,96,768]{3,2,1,0:T(8,128)(2,1)}, bf16[4,2,96,768]{3,2,1,0:T(8,128)(2,1)S(1)}, u32[]{:S(2)}, u32[]{:S(2)}) collective-permute-start(bf16[4,2,96,768]{3,2,1,0:T(8,128)(2,1)} %get-tuple-element.151.rest_0_), channel_id=1, source_target_pairs={{0,8},{1,17},{2,10},{3,19},{4,12},{5,21},{6,14},{7,23},{8,0},{9,25... | collective-permute-start | bytes 3538952 | tf_op jit(solution)/shard_map/ppermute | solution.py:1285
  373.6 69.1 %reduce-scatter.12.cloned.1.call-start = ((), (), s32[]{:S(2)}) async-start(), calls=%async_computation.14 | async-start | bytes 1474560 | tf_op jit(solution)/shard_map/reduce_scatter | solution.py:1300
  391.9 49.7 %collective-permute-start.44 = (bf16[208,1536]{1,0:T(8,128)(2,1)S(1)}, bf16[208,1536]{1,0:T(8,128)(2,1)}, u32[]{:S(2)}, u32[]{:S(2)}) collective-permute-start(bf16[208,1536]{1,0:T(8,128)(2,1)S(1)} %copy-done.14), channel_id=1, source_target_pairs={{0,24},{1,25},{2,26},{3,27},{4,28},{5,29},{6,30},{7,31},{8,16},{9,... | collective-permute-start | bytes 1916936 | tf_op jit(solution)/shard_map/ppermute | solution.py:1285
  392.3 50.4 %collective-permute-start.43 = (bf16[208,1536]{1,0:T(8,128)(2,1)S(1)}, bf16[208,1536]{1,0:T(8,128)(2,1)}, u32[]{:S(2)}, u32[]{:S(2)}) collective-permute-start(bf16[208,1536]{1,0:T(8,128)(2,1)S(1)} %copy-done.14), channel_id=1, source_target_pairs={{0,16},{1,9},{2,18},{3,11},{4,20},{5,13},{6,22},{7,15},{8,24},{9,1... | collective-permute-start | bytes 1916936 | tf_op jit(solution)/shard_map/ppermute | solution.py:1285
  393.3 50.6 %collective-permute-start.42 = (bf16[208,1536]{1,0:T(8,128)(2,1)S(1)}, bf16[208,1536]{1,0:T(8,128)(2,1)}, u32[]{:S(2)}, u32[]{:S(2)}) collective-permute-start(bf16[208,1536]{1,0:T(8,128)(2,1)S(1)} %copy-done.14), channel_id=1, source_target_pairs={{0,8},{1,17},{2,10},{3,19},{4,12},{5,21},{6,14},{7,23},{8,0},{9,25... | collective-permute-start | bytes 1916936 | tf_op jit(solution)/shard_map/ppermute | solution.py:1285
  394.5 46.8 %collective-permute-start.34 = (bf16[384,768]{1,0:T(8,128)(2,1)}, bf16[384,768]{1,0:T(8,128)(2,1)}, u32[]{:S(2)}, u32[]{:S(2)}) collective-permute-start(bf16[384,768]{1,0:T(8,128)(2,1)} %sums.8.refs_2_), channel_id=1, source_target_pairs={{0,8},{1,17},{2,10},{3,19},{4,12},{5,21},{6,14},{7,23},{8,0},{9,25... | collective-permute-start | bytes 1769480 | tf_op jit(solution)/shard_map/ppermute | solution.py:1285
  404.3 39.9 %collective-permute-start.41 = (bf16[112,1344]{1,0:T(8,128)(2,1)}, bf16[112,1344]{1,0:T(8,128)(2,1)S(1)}, u32[]{:S(2)}, u32[]{:S(2)}) collective-permute-start(bf16[112,1344]{1,0:T(8,128)(2,1)} %bitcast.40), channel_id=1, source_target_pairs={{0,24},{1,25},{2,26},{3,27},{4,28},{5,29},{6,30},{7,31},{8,16},{9,... | collective-permute-start | bytes 903176 | tf_op jit(solution)/shard_map/ppermute | solution.py:1285
  (66 other events, 581.0 us)
Sparse Core Ops, SparseCore 0:
  11.2 44.0 all-gather.5
  57.5 40.4 all-gather.7
  99.6 40.3 all-gather.9
  141.5 40.3 all-gather.11
  277.0 27.9 reduce-scatter.5
  307.2 27.9 reduce-scatter.9
  338.2 27.8 reduce-scatter.7
  373.7 29.1 reduce-scatter.13
  405.2 27.9 reduce-scatter.11
where the time goes:
time: 481 us; the launch traced here: 473 us
  Pallas kernels  193 us (40%)
  waiting for transfers between devices  160 us (33%)
  starting transfers between devices  53.4 us (11%)
  blocking collectives  29.4 us (6%)
  local copies, waits for them, and re-layouts  19.5 us (4%)
  between operations  14.8 us (3%)
    ppermute x45, waiting for transfers between devices, via(): return lambda x: lax.ppermute(x, axes, perm)  115 us
    pallas_call x13, Pallas kernels, call(): pl.pallas_call(kernel, out_shape=[jax.ShapeDtypeStruct(shape, dtype) for...  103 us
    pallas_call x5, Pallas kernels, call_writing(): pl.pallas_call(functools.partial(run, scratch=len(scratch), **keys), out_...  70.3 us
    ppermute x45, starting transfers between devices, via(): return lambda x: lax.ppermute(x, axes, perm)  49.4 us
    all_gather x4, waiting for transfers between devices, gather_ffn(): x = lax.all_gather(x, 'fsdp', axis=0, tiled=True)  26.7 us
    unnamed x86, local copies, waits for them, and re-layouts  16.8 us
    all_gather x1, blocking collectives, on_device_fast(): starts = lax.all_gather(doc_start[0], 'ctx', axis=0, tiled=True)  16.6 us
    all_to_all x1, waiting for transfers between devices, on_device_fast(): gcx = lax.all_to_all(gctx, 'ctx', 0, 0, tiled=True)  13 us
  transfers between devices with their start and end apart: 55, of which 21 were waited for; matrix products, arithmetic and copies ran while one was open for 1% of the time, Pallas kernels for 35%

commit v1 on v0

--- a/solution.py
+++ b/solution.py
@@ -831,17 +831,21 @@
             allowed = jnp.concatenate([col, col], axis=1) == starts_q
             if diagonal:
                 allowed = allowed & causal
-            dqs = []
+            keys = pl.ds(at, QB)
+            cols = slice(lo, lo + QB)
+            ss = [mm_nt(k_s[h, keys, :], q_s[h, cols, :]) for h in range(heads)]
+            dps = [mm_nt(v_s[h, keys, :], do_s[h, cols, :]) for h in range(heads)]
+            ps = [
+                jnp.exp2(jnp.where(allowed, s * SCORE_SCALE, NEG) - lse[h : h + 1, cols]) for h, s in enumerate(ss)
+            ]
+            dss = [
+                (p * (dp - delta_s[h : h + 1, cols])).astype(BF) for h, (p, dp) in enumerate(zip(ps, dps))
+            ]
             for h in range(heads):
-                q, do = q_s[h, lo : lo + QB, :], do_s[h, lo : lo + QB, :]
-                s = mm_nt(k_s[h, pl.ds(at, QB), :], q) * SCORE_SCALE
-                p = jnp.exp2(jnp.where(allowed, s, NEG) - lse[h : h + 1, lo : lo + QB])
-                dp = mm_nt(v_s[h, pl.ds(at, QB), :], do)
-                ds = (p * (dp - delta_s[h : h + 1, lo : lo + QB])).astype(BF)
-                dv_s[h, pl.ds(at, QB), :] += mm_nn(p.astype(BF), do)
-                dk_s[h, pl.ds(at, QB), :] += mm_nn(ds, q)
-                dqs.append(mm_nn(kt_s[head_rows[h], pl.ds(at, QB)], ds))
-            return dqs
+                dv_s[h, keys, :] += mm_nn(ps[h].astype(BF), do_s[h, cols, :])
+            for h in range(heads):
+                dk_s[h, keys, :] += mm_nn(dss[h], q_s[h, cols, :])
+            return [mm_nn(kt_s[head_rows[h], keys], dss[h]) for h in range(heads)]
 
         dqs = block(lo, True)
         if i > 0:

time: 481 us -> 477 us (level)
  Pallas kernels: 193 us -> 188 us
    reduce_scatter x5, waiting for transfers between devices: 5.14 us -> 11.8 us  [reduce_z(): lax.psum_scatter(x, 'fsdp', scatter_dimension=0, tiled=True, axis_index_g...]
    pallas_call x13, Pallas kernels: 103 us -> 97.7 us  [call(): pl.pallas_call(kernel, out_shape=[jax.ShapeDtypeStruct(shape, dtype) for...]
  transfers between devices with their start and end apart: 55 -> 55, of which waited for: 21 -> 22; matrix products, arithmetic and copies ran while one was open for 1% -> 1% of each run, Pallas kernels for 35% -> 34%
where the time goes in v1:
time: 477 us; the launch traced here: 467 us
  Pallas kernels  188 us (39%)
  waiting for transfers between devices  163 us (34%)
  starting transfers between devices  49.7 us (10%)
  blocking collectives  29.4 us (6%)
  local copies, waits for them, and re-layouts  19.2 us (4%)
  between operations  14.8 us (3%)
    ppermute x45, waiting for transfers between devices, via(): return lambda x: lax.ppermute(x, axes, perm)  112 us
    pallas_call x13, Pallas kernels, call(): pl.pallas_call(kernel, out_shape=[jax.ShapeDtypeStruct(shape, dtype) for...  97.7 us
    pallas_call x5, Pallas kernels, call_writing(): pl.pallas_call(functools.partial(run, scratch=len(scratch), **keys), out_...  70 us
    ppermute x45, starting transfers between devices, via(): return lambda x: lax.ppermute(x, axes, perm)  45.7 us
    all_gather x4, waiting for transfers between devices, gather_ffn(): x = lax.all_gather(x, 'fsdp', axis=0, tiled=True)  26.7 us
    all_gather x1, blocking collectives, on_device_fast(): starts = lax.all_gather(doc_start[0], 'ctx', axis=0, tiled=True)  16.6 us
    unnamed x86, local copies, waits for them, and re-layouts  16.5 us
    all_to_all x1, waiting for transfers between devices, on_device_fast(): gcx = lax.all_to_all(gctx, 'ctx', 0, 0, tiled=True)  13.1 us
  transfers between devices with their start and end apart: 55, of which 22 were waited for; matrix products, arithmetic and copies ran while one was open for 1% of the time, Pallas kernels for 34%

profile of v1, /device:TPU:1, one launch (start us, length us, event | category | flops | bytes accessed | tf_op | source)
XLA Modules:
  0.0 467.3 jit_solution(1053970946008938856)
XLA Ops:
  7.3 3.8 prep.1
  14.7 16.6 %all-gather = s32[1,1536]{1,0:T(1,128)S(1)} all-gather(s32[1,384]{1,0:T(1,128)S(1)} %copy-done.34), channel_id=2, replica_groups=mesh['ctx'=4,'fsdp'=8] {'ctx'}, dimensions={1}, use_global_device_ids=true | all-gather | bytes 7680 | tf_op jit(solution)/shard_map/all_gather | solution.py:1343
  32.8 8.1 %collective-permute-done.2.refs_4_.rest_2_.h3 = bf16[384,768]{1,0:T(8,128)(2,1)S(1)} collective-permute-done((bf16[384,768]{1,0:T(8,128)(2,1)S(1)}, bf16[384,768]{1,0:T(8,128)(2,1)S(1)}, u32[]{:S(2)}, u32[]{:S(2)}) %collective-permute-start.2) | collective-permute-done | bytes 589856 | tf_op jit(solution)/shard_map/ppermute | solution.py:1289
  40.8 14.4 %all-gather.6.cloned.1.call-done = bf16[2304,768]{1,0:T(8,128)(2,1)} async-done(((bf16[288,768]{1,0:T(8,128)(2,1)}), bf16[2304,768]{1,0:T(8,128)(2,1)}) %all-gather.6.cloned.1.call-update) | async-done | bytes 3538960 | tf_op jit(solution)/shard_map/all_gather | solution.py:1338
  62.2 14.9 %attn_fwd.2 = (bf16[4,384,576]{2,1,0:T(8,128)(2,1)}, bf16[192,384]{1,0:T(8,128)(2,1)}, bf16[192,384]{1,0:T(8,128)(2,1)}, bf16[192,384]{1,0:T(8,128)(2,1)}, bf16[192,384]{1,0:T(8,128)(2,1)}, /*index=5*/f32[8,1536]{1,0:T(8,128)}) custom-call(s32[20]{0:T(128)} %concatenate.7.meta.refs_0_, bf16[384,768]{1,0:T(8,128)(2,1)} %bitcast.31, ...), custom_call_target="tpu_custom_call" | custom-call | tf_op jit(solution)/shard_map/attn_fwd/pallas_call | solution.py:447
  80.0 4.1 collective-permute-done.7.b.refs_8_.refs_12_
  93.4 4.6 all-gather.8.cloned.1.call-done
  99.3 13.7 %mlp_fwd.1 = (f32[384,768]{1,0:T(8,128)}, f32[384,1]{1,0:T(8,128)}, bf16[384,3072]{1,0:T(8,128)(2,1)}, f32[384,768]{1,0:T(8,128)}, f32[384,1]{1,0:T(8,128)}, /*i...) custom-call(s32[20]{0:T(128)} %concatenate.7.meta.refs_0_, ...), custom_call_target="tpu_custom_call" | custom-call | tf_op jit(solution)/shard_map/mlp_fwd/pallas_call | solution.py:528
  115.4 11.0 %collective-permute-done.9.rest_0_.h1 = bf16[384,768]{1,0:T(8,128)(2,1)S(1)} collective-permute-done((bf16[384,768]{1,0:T(8,128)(2,1)}, bf16[384,768]{1,0:T(8,128)(2,1)S(1)}, u32[]{:S(2)}, u32[]{:S(2)}) %collective-permute-start.9) | collective-permute-done | bytes 589856 | tf_op jit(solution)/shard_map/ppermute | solution.py:1289
  130.8 5.5 %collective-permute-done.11.rest_2_.h3 = bf16[384,768]{1,0:T(8,128)(2,1)S(1)} collective-permute-done((bf16[384,768]{1,0:T(8,128)(2,1)S(1)}, bf16[384,768]{1,0:T(8,128)(2,1)S(1)}, u32[]{:S(2)}, u32[]{:S(2)}) %collective-permute-start.11) | collective-permute-done | bytes 589856 | tf_op jit(solution)/shard_map/ppermute | solution.py:1289
  136.3 3.7 all-gather.10.cloned.1.call-done
  146.4 15.3 %attn_fwd.3 = (bf16[4,384,576]{2,1,0:T(8,128)(2,1)}, bf16[192,384]{1,0:T(8,128)(2,1)}, bf16[192,384]{1,0:T(8,128)(2,1)}, bf16[192,384]{1,0:T(8,128)(2,1)}, bf16[192,384]{1,0:T(8,128)(2,1)}, /*index=5*/f32[8,1536]{1,0:T(8,128)}) custom-call(s32[20]{0:T(128)} %concatenate.7.meta.refs_0_, bf16[384,768]{1,0:T(8,128)(2,1)} %get-tuple-element.100.h0, ...), custom_call_target="tpu_custom_call" | custom-call | tf_op jit(solution)/shard_map/attn_fwd/pallas_call | solution.py:447
  161.7 7.1 %collective-permute-done.17.b.refs_9_ = bf16[4,2,96,768]{3,2,1,0:T(8,128)(2,1)S(1)} collective-permute-done((bf16[4,2,96,768]{3,2,1,0:T(8,128)(2,1)}, bf16[4,2,96,768]{3,2,1,0:T(8,128)(2,1)S(1)}, u32[]{:S(2)}, u32[]{:S(2)}) %collective-permute-start.17) | collective-permute-done | bytes 1179680 | tf_op jit(solution)/shard_map/ppermute | solution.py:1289
  177.9 4.0 all-gather.12.cloned.1.call-done
  186.9 19.2 %last.1 = (bf16[384,2304]{1,0:T(8,128)(2,1)}, bf16[384,2304]{1,0:T(8,128)(2,1)}, bf16[384,768]{1,0:T(8,128)(2,1)}, f32[384,768]{1,0:T(8,128)}, bf16[400,4608]{1,0:T(8,128)(2,1)}, /*index=5*/bf16[4,192,384]{2,1,0:T(8,128)(2,1)}) custom-call(s32[20]{0:T(128)} %concatenate.7.meta.refs_0_, bf16[192,384]{1,0:T(8,128)(2,1)} %get-tuple-element.103.refs_1_.c0, ...), custom_call_target="tpu_custom_call" | custom-call | tf_op jit(solution)/shard_map/last/pallas_call | solution.py:528
  206.9 12.8 %all_to_all.10.gctx = bf16[4,192,384]{2,1,0:T(8,128)(2,1)} all-to-all(bf16[4,192,384]{2,1,0:T(8,128)(2,1)} %get-tuple-element.118), channel_id=1, replica_groups=mesh['ctx'=4,'fsdp'=8] {'ctx'}, dimensions={0} | all-to-all | bytes 1179648 | tf_op jit(solution)/shard_map/all_to_all | solution.py:1434
  221.0 20.7 %attn_bwd.2 = (f32[384,768]{1,0:T(8,128)}, bf16[384,768]{1,0:T(8,128)(2,1)}, bf16[384,768]{1,0:T(8,128)(2,1)}, bf16[384,768]{1,0:T(8,128)(2,1)}, bf16[4,112,576]...) custom-call(s32[20]{0:T(128)} %concatenate.7.meta.refs_0_, bf16[384,768]{1,0:T(8,128)(2,1)} %get-tuple-element.100.h0, ...), custom_call_target="tpu_custom_call" | custom-call | tf_op jit(solution)/shard_map/attn_bwd/pallas_call | solution.py:447
  243.2 7.8 %collective-permute-done.21.refs_1_ = bf16[384,768]{1,0:T(8,128)(2,1)S(1)} collective-permute-done((bf16[384,768]{1,0:T(8,128)(2,1)}, bf16[384,768]{1,0:T(8,128)(2,1)S(1)}, u32[]{:S(2)}, u32[]{:S(2)}) %collective-permute-start.21) | collective-permute-done | bytes 589856 | tf_op jit(solution)/shard_map/ppermute | solution.py:1289
  257.4 10.8 %wgrad.2 = (bf16[4,2,96,768]{3,2,1,0:T(8,128)(2,1)}, bf16[4,2,96,768]{3,2,1,0:T(8,128)(2,1)}, bf16[4,2,96,768]{3,2,1,0:T(8,128)(2,1)}, bf16[4,112,768]{2,1,0:T(8,128)(2,1)}, bf16[4,2,96,768]{3,2,1,0:T(8,128)(2,1)}) custom-call(s32[20]{0:T(128)} %concatenate.7.meta.refs_0_, bf16[384,2304]{1,0:T(8,128)(2,1)} %get-tuple-element.124.refs_1_, ...), custom_call_target="tpu_custom_call" | custom-call | tf_op jit(solution)/shard_map/wgrad/pallas_call | solution.py:528
  274.2 15.8 %mlp_bwd.1 = (f32[384,768]{1,0:T(8,128)}, bf16[400,4608]{1,0:T(8,128)(2,1)}, bf16[4,192,384]{2,1,0:T(8,128)(2,1)}) custom-call(s32[20]{0:T(128)} %concatenate.7.meta.refs_0_, f32[384,768]{1,0:T(8,128)} %get-tuple-element.111.refs_1_, f32[384,1]{1,0:T(8,128)} %get-tuple-element.112.refs_2_, f32[384,768]{1,0:T(8,128)} %get-tuple-element.113.refs_3_, ...), custom_call_target="tpu_custom_call" | custom-call | tf_op jit(solution)/shard_map/mlp_bwd/pallas_call | solution.py:528
  294.3 13.1 %all-to-all-done.1.refs_3_.refs_5_.gctx = bf16[4,192,384]{2,1,0:T(8,128)(2,1)S(1)} async-done(((bf16[4,192,384]{2,1,0:T(8,128)(2,1)}), bf16[4,192,384]{2,1,0:T(8,128)(2,1)S(1)}, u32[]{:S(2)}, u32[]{:S(2)}) %all-to-all-start.1) | async-done | bytes 589856 | tf_op jit(solution)/shard_map/all_to_all | solution.py:1434
  312.6 10.6 %wgrad.3 = (bf16[4,2,96,768]{3,2,1,0:T(8,128)(2,1)}, bf16[4,2,96,768]{3,2,1,0:T(8,128)(2,1)}, bf16[4,2,96,768]{3,2,1,0:T(8,128)(2,1)}, bf16[4,112,768]{2,1,0:T(8,128)(2,1)}, bf16[4,2,96,768]{3,2,1,0:T(8,128)(2,1)}) custom-call(s32[20]{0:T(128)} %concatenate.7.meta.refs_0_, bf16[384,2304]{1,0:T(8,128)(2,1)} %get-tuple-element.136.refs_1_, ...), custom_call_target="tpu_custom_call" | custom-call | tf_op jit(solution)/shard_map/wgrad/pallas_call | solution.py:528
  325.0 7.2 %reduce-scatter.10.cloned.1.call-done = bf16[1,2,96,768]{3,2,1,0:T(8,128)(2,1)} async-done(((bf16[4,2,96,768]{3,2,1,0:T(8,128)(2,1)}), bf16[1,2,96,768]{3,2,1,0:T(8,128)(2,1)}) %reduce-scatter.10.cloned.1.call-update) | async-done | bytes 294928 | tf_op jit(solution)/shard_map/reduce_scatter | solution.py:1304
  334.3 20.5 %attn_bwd.3 = (f32[384,768]{1,0:T(8,128)}, bf16[384,768]{1,0:T(8,128)(2,1)}, bf16[384,768]{1,0:T(8,128)(2,1)}, bf16[384,768]{1,0:T(8,128)(2,1)}, bf16[4,112,576]...) custom-call(s32[20]{0:T(128)} %concatenate.7.meta.refs_0_, bf16[384,768]{1,0:T(8,128)(2,1)} %bitcast.33, ...), custom_call_target="tpu_custom_call" | custom-call | tf_op jit(solution)/shard_map/attn_bwd/pallas_call | solution.py:447
  357.7 4.0 sums.7
  370.6 8.0 %collective-permute-done.35.refs_1_ = bf16[4,2,96,768]{3,2,1,0:T(8,128)(2,1)S(1)} collective-permute-done((bf16[4,2,96,768]{3,2,1,0:T(8,128)(2,1)}, bf16[4,2,96,768]{3,2,1,0:T(8,128)(2,1)S(1)}, u32[]{:S(2)}, u32[]{:S(2)}) %collective-permute-start.35) | collective-permute-done | bytes 1179680 | tf_op jit(solution)/shard_map/ppermute | solution.py:1289
  387.0 7.6 %collective-permute-done.28 = bf16[384,768]{1,0:T(8,128)(2,1)} collective-permute-done((bf16[384,768]{1,0:T(8,128)(2,1)}, bf16[384,768]{1,0:T(8,128)(2,1)}, u32[]{:S(2)}, u32[]{:S(2)}) %collective-permute-start.28) | collective-permute-done | bytes 589856 | tf_op jit(solution)/shard_map/ppermute | solution.py:1289
  394.7 4.5 reduce-scatter.14.cloned.1.call-done
  401.3 33.9 %collective-permute-done.34 = bf16[384,768]{1,0:T(8,128)(2,1)} collective-permute-done((bf16[384,768]{1,0:T(8,128)(2,1)}, bf16[384,768]{1,0:T(8,128)(2,1)}, u32[]{:S(2)}, u32[]{:S(2)}) %collective-permute-start.34) | collective-permute-done | bytes 589856 | tf_op jit(solution)/shard_map/ppermute | solution.py:1289
  441.4 4.9 %place.2 = (f32[2,96,3072]{2,1,0:T(8,128)}, f32[2,384,768]{2,1,0:T(8,128)}, f32[2,96,2304]{2,1,0:T(8,128)}, f32[2,96,768]{2,1,0:T(8,128)}, f32[16,96]{1,0:T(8,128)}) custom-call(s32[20]{0:T(128)} %concatenate.7.meta.refs_0_, bf16[208,1536]{1,0:T(8,128)(2,1)} %join.1.refs_2_.rest_0_, bf16[208,1536]{1,0:T(8,128)(2,1)} %collective-permute-done.42.rest_1_, ...), custom_call_target="tpu_custom_call" | custom-call | bytes 10485760 | tf_op jit(solution)/shard_map/place/pallas_call | solution.py:1526
  446.2 4.9 %collective-permute-done.39.rest_5_ = bf16[112,1344]{1,0:T(8,128)(2,1)} collective-permute-done((bf16[112,1344]{1,0:T(8,128)(2,1)}, bf16[112,1344]{1,0:T(8,128)(2,1)}, u32[]{:S(2)}, u32[]{:S(2)}) %collective-permute-start.39) | collective-permute-done | bytes 301088 | tf_op jit(solution)/shard_map/ppermute | solution.py:1289
  455.5 4.9 %place.3 = (f32[2,96,3072]{2,1,0:T(8,128)}, f32[2,384,768]{2,1,0:T(8,128)}, f32[2,96,2304]{2,1,0:T(8,128)}, f32[2,96,768]{2,1,0:T(8,128)}, f32[2,96]{1,0:T(2,128...) custom-call(s32[20]{0:T(128)} %concatenate.7.meta.refs_0_, ...), custom_call_target="tpu_custom_call", output_to_operand_aliasing={{0}: (10, {}), {1}: (11, {}), {2}: (12, {}), {3}: (13, {})} | custom-call | bytes 10485760 | tf_op jit(solution)/shard_map/place/pallas_call | solution.py:1526
  (222 shorter events, 114.5 us)
Async XLA Ops:
  7.2 48.0 %all-gather.6.cloned.1.call-start = ((), (), s32[]{:S(2)}) async-start(), calls=%async_computation.7 | async-start | bytes 3981312 | tf_op jit(solution)/shard_map/all_gather | solution.py:1338
  11.1 86.8 %all-gather.8.cloned.1.call-start = ((), (), s32[]{:S(2)}) async-start(), calls=%async_computation.8 | async-start | bytes 3981312 | tf_op jit(solution)/shard_map/all_gather | solution.py:1338
  11.1 21.6 %collective-permute-start.1 = (bf16[384,768]{1,0:T(8,128)(2,1)S(1)}, bf16[384,768]{1,0:T(8,128)(2,1)S(1)}, u32[]{:S(2)}, u32[]{:S(2)}) collective-permute-start(bf16[384,768]{1,0:T(8,128)(2,1)S(1)} %bitcast.34), channel_id=1, source_target_pairs={{0,16},{1,9},{2,18},{3,11},{4,20},{5,13},{6,22},{7,15},{8,24},{9,1... | collective-permute-start | bytes 1769480 | tf_op jit(solution)/shard_map/ppermute | solution.py:1289
  13.4 18.2 %collective-permute-start = (bf16[384,768]{1,0:T(8,128)(2,1)S(1)}, bf16[384,768]{1,0:T(8,128)(2,1)S(1)}, u32[]{:S(2)}, u32[]{:S(2)}) collective-permute-start(bf16[384,768]{1,0:T(8,128)(2,1)S(1)} %bitcast.35), channel_id=1, source_target_pairs={{0,8},{1,17},{2,10},{3,19},{4,12},{5,21},{6,14},{7,23},{8,0},{9,25... | collective-permute-start | bytes 1769480 | tf_op jit(solution)/shard_map/ppermute | solution.py:1289
  14.5 125.5 %all-gather.10.cloned.1.call-start = ((), (), s32[]{:S(2)}) async-start(), calls=%async_computation.9 | async-start | bytes 3981312 | tf_op jit(solution)/shard_map/all_gather | solution.py:1338
  58.0 26.1 %collective-permute-start.7 = (bf16[4,2,96,768]{3,2,1,0:T(8,128)(2,1)}, bf16[4,2,96,768]{3,2,1,0:T(8,128)(2,1)S(1)}, u32[]{:S(2)}, u32[]{:S(2)}) collective-permute-start(bf16[4,2,96,768]{3,2,1,0:T(8,128)(2,1)} %half.2.rest_0_), channel_id=1, source_target_pairs={{0,16},{1,9},{2,18},{3,11},{4,20},{5,13},{6,22},{7,15},{8,24},{9,1... | collective-permute-start | bytes 3538952 | tf_op jit(solution)/shard_map/ppermute | solution.py:1289
  59.3 28.2 %collective-permute-start.6 = (bf16[4,2,96,768]{3,2,1,0:T(8,128)(2,1)}, bf16[4,2,96,768]{3,2,1,0:T(8,128)(2,1)S(1)}, u32[]{:S(2)}, u32[]{:S(2)}) collective-permute-start(bf16[4,2,96,768]{3,2,1,0:T(8,128)(2,1)} %half.2.rest_0_), channel_id=1, source_target_pairs={{0,8},{1,17},{2,10},{3,19},{4,12},{5,21},{6,14},{7,23},{8,0},{9,25... | collective-permute-start | bytes 3538952 | tf_op jit(solution)/shard_map/ppermute | solution.py:1289
  79.9 102.0 %all-gather.12.cloned.1.call-start = ((), (), s32[]{:S(2)}) async-start(), calls=%async_computation.10 | async-start | bytes 3981312 | tf_op jit(solution)/shard_map/all_gather | solution.py:1338
  93.3 219.3 %reduce-scatter.6.cloned.1.call-start = ((), (), s32[]{:S(2)}) async-start(), calls=%async_computation.11 | async-start | bytes 1576960 | tf_op jit(solution)/shard_map/reduce_scatter | solution.py:1304
  128.6 16.6 %collective-permute-start.12 = (bf16[384,2304]{1,0:T(8,128)(2,1)}, bf16[384,2304]{1,0:T(8,128)(2,1)S(1)}, u32[]{:S(2)}, u32[]{:S(2)}) collective-permute-start(bf16[384,2304]{1,0:T(8,128)(2,1)} %get-tuple-element.102), channel_id=1, source_target_pairs={{0,1},{1,0},{2,3},{3,2},{4,5},{5,4},{6,7},{7,6},{8,9},{9,8},{10,11... | collective-permute-start | bytes 5308424 | tf_op jit(solution)/shard_map/ppermute | solution.py:1289
  142.7 26.1 %collective-permute-start.17 = (bf16[4,2,96,768]{3,2,1,0:T(8,128)(2,1)}, bf16[4,2,96,768]{3,2,1,0:T(8,128)(2,1)S(1)}, u32[]{:S(2)}, u32[]{:S(2)}) collective-permute-start(bf16[4,2,96,768]{3,2,1,0:T(8,128)(2,1)} %half.3.rest_0_), channel_id=1, source_target_pairs={{0,16},{1,9},{2,18},{3,11},{4,20},{5,13},{6,22},{7,15},{8,24},{9,1... | collective-permute-start | bytes 3538952 | tf_op jit(solution)/shard_map/ppermute | solution.py:1289
  144.0 27.8 %collective-permute-start.16 = (bf16[4,2,96,768]{3,2,1,0:T(8,128)(2,1)}, bf16[4,2,96,768]{3,2,1,0:T(8,128)(2,1)}, u32[]{:S(2)}, u32[]{:S(2)}) collective-permute-start(bf16[4,2,96,768]{3,2,1,0:T(8,128)(2,1)} %half.3.rest_0_), channel_id=1, source_target_pairs={{0,8},{1,17},{2,10},{3,19},{4,12},{5,21},{6,14},{7,23},{8,0},{9,25... | collective-permute-start | bytes 3538952 | tf_op jit(solution)/shard_map/ppermute | solution.py:1289
  206.1 51.3 %collective-permute-start.23 = (bf16[400,4608]{1,0:T(8,128)(2,1)}, bf16[400,4608]{1,0:T(8,128)(2,1)}, u32[]{:S(2)}, u32[]{:S(2)}) collective-permute-start(bf16[400,4608]{1,0:T(8,128)(2,1)} %get-tuple-element.125.refs_3_), channel_id=1, source_target_pairs={{0,1},{1,0},{2,3},{3,2},{4,5},{5,4},{6,7},{7,6},{8,9},{9,8},{10,11... | collective-permute-start | bytes 11059208 | tf_op jit(solution)/shard_map/ppermute | solution.py:1289
  242.4 29.3 %collective-permute-start.20 = (bf16[384,768]{1,0:T(8,128)(2,1)}, bf16[384,768]{1,0:T(8,128)(2,1)S(1)}, u32[]{:S(2)}, u32[]{:S(2)}) collective-permute-start(bf16[384,768]{1,0:T(8,128)(2,1)} %get-tuple-element.121), channel_id=1, source_target_pairs={{0,16},{1,9},{2,18},{3,11},{4,20},{5,13},{6,22},{7,15},{8,24},{9,1... | collective-permute-start | bytes 1769480 | tf_op jit(solution)/shard_map/ppermute | solution.py:1289
  254.0 17.7 %collective-permute-start.22 = (bf16[384,768]{1,0:T(8,128)(2,1)}, bf16[384,768]{1,0:T(8,128)(2,1)S(1)}, u32[]{:S(2)}, u32[]{:S(2)}) collective-permute-start(bf16[384,768]{1,0:T(8,128)(2,1)} %sums.5.refs_5_), channel_id=1, source_target_pairs={{0,8},{1,17},{2,10},{3,19},{4,12},{5,21},{6,14},{7,23},{8,0},{9,25... | collective-permute-start | bytes 1769480 | tf_op jit(solution)/shard_map/ppermute | solution.py:1289
  272.8 34.7 %collective-permute-start.26 = (bf16[4,2,96,768]{3,2,1,0:T(8,128)(2,1)}, bf16[4,2,96,768]{3,2,1,0:T(8,128)(2,1)S(1)}, u32[]{:S(2)}, u32[]{:S(2)}) collective-permute-start(bf16[4,2,96,768]{3,2,1,0:T(8,128)(2,1)} %get-tuple-element.131.refs_16_), channel_id=1, source_target_pairs={{0,8},{1,17},{2,10},{3,19},{4,12},{5,21},{6,14},{7,23},{8,0},{9,25... | collective-permute-start | bytes 3538952 | tf_op jit(solution)/shard_map/ppermute | solution.py:1289
  273.1 34.4 %collective-permute-start.27 = (bf16[4,2,96,768]{3,2,1,0:T(8,128)(2,1)}, bf16[4,2,96,768]{3,2,1,0:T(8,128)(2,1)S(1)}, u32[]{:S(2)}, u32[]{:S(2)}) collective-permute-start(bf16[4,2,96,768]{3,2,1,0:T(8,128)(2,1)} %get-tuple-element.132.refs_17_), channel_id=1, source_target_pairs={{0,16},{1,9},{2,18},{3,11},{4,20},{5,13},{6,22},{7,15},{8,24},{9,1... | collective-permute-start | bytes 3538952 | tf_op jit(solution)/shard_map/ppermute | solution.py:1289
  290.0 17.4 %all-to-all-start.1 = ((bf16[4,192,384]{2,1,0:T(8,128)(2,1)}), bf16[4,192,384]{2,1,0:T(8,128)(2,1)S(1)}, u32[]{:S(2)}, u32[]{:S(2)}) async-start(bf16[4,192,384]{2,1,0:T(8,128)(2,1)} %get-tuple-element.135), calls=%async_computation.1 | async-start | bytes 1179648 | tf_op jit(solution)/shard_map/all_to_all | solution.py:1434
  293.5 38.7 %reduce-scatter.10.cloned.1.call-start = ((), (), s32[]{:S(2)}) async-start(), calls=%async_computation.13 | async-start | bytes 1474560 | tf_op jit(solution)/shard_map/reduce_scatter | solution.py:1304
  293.6 19.0 %collective-permute-start.25 = (bf16[400,4608]{1,0:T(8,128)(2,1)}, bf16[400,4608]{1,0:T(8,128)(2,1)}, u32[]{:S(2)}, u32[]{:S(2)}) collective-permute-start(bf16[400,4608]{1,0:T(8,128)(2,1)} %get-tuple-element.137.refs_3_), channel_id=1, source_target_pairs={{0,1},{1,0},{2,3},{3,2},{4,5},{5,4},{6,7},{7,6},{8,9},{9,8},{10,11... | collective-permute-start | bytes 11059208 | tf_op jit(solution)/shard_map/ppermute | solution.py:1289
  294.3 71.4 %reduce-scatter.8.cloned.1.call-start = ((), (), s32[]{:S(2)}) async-start(), calls=%async_computation.12 | async-start | bytes 1474560 | tf_op jit(solution)/shard_map/reduce_scatter | solution.py:1304
  323.2 33.1 %collective-permute-start.32 = (bf16[4,2,96,768]{3,2,1,0:T(8,128)(2,1)}, bf16[4,2,96,768]{3,2,1,0:T(8,128)(2,1)S(1)}, u32[]{:S(2)}, u32[]{:S(2)}) collective-permute-start(bf16[4,2,96,768]{3,2,1,0:T(8,128)(2,1)} %get-tuple-element.149), channel_id=1, source_target_pairs={{0,16},{1,9},{2,18},{3,11},{4,20},{5,13},{6,22},{7,15},{8,24},{9,1... | collective-permute-start | bytes 3538952 | tf_op jit(solution)/shard_map/ppermute | solution.py:1289
  324.5 31.8 %collective-permute-start.33 = (bf16[4,2,96,768]{3,2,1,0:T(8,128)(2,1)}, bf16[4,2,96,768]{3,2,1,0:T(8,128)(2,1)S(1)}, u32[]{:S(2)}, u32[]{:S(2)}) collective-permute-start(bf16[4,2,96,768]{3,2,1,0:T(8,128)(2,1)} %get-tuple-element.150), channel_id=1, source_target_pairs={{0,16},{1,9},{2,18},{3,11},{4,20},{5,13},{6,22},{7,15},{8,24},{9,1... | collective-permute-start | bytes 3538952 | tf_op jit(solution)/shard_map/ppermute | solution.py:1289
  324.8 74.4 %reduce-scatter.14.cloned.1.call-start = ((), (), s32[]{:S(2)}) async-start(), calls=%async_computation.15 | async-start | bytes 1576960 | tf_op jit(solution)/shard_map/reduce_scatter | solution.py:1304
  332.2 33.4 %collective-permute-start.30 = (bf16[1,2,96,768]{3,2,1,0:T(8,128)(2,1)}, bf16[1,2,96,768]{3,2,1,0:T(8,128)(2,1)S(1)}, u32[]{:S(2)}, u32[]{:S(2)}) collective-permute-start(bf16[1,2,96,768]{3,2,1,0:T(8,128)(2,1)} %reduce-scatter.10.cloned.1.call-done), channel_id=1, source_target_pairs={{0,24},{1,25},{2,26},{3,27},{4,28},{5,29},{6,30},{7,31},{8,16},{9,... | collective-permute-start | bytes 884744 | tf_op jit(solution)/shard_map/ppermute | solution.py:1289
  361.8 16.8 %collective-permute-start.35 = (bf16[4,2,96,768]{3,2,1,0:T(8,128)(2,1)}, bf16[4,2,96,768]{3,2,1,0:T(8,128)(2,1)S(1)}, u32[]{:S(2)}, u32[]{:S(2)}) collective-permute-start(bf16[4,2,96,768]{3,2,1,0:T(8,128)(2,1)} %get-tuple-element.151.rest_0_), channel_id=1, source_target_pairs={{0,8},{1,17},{2,10},{3,19},{4,12},{5,21},{6,14},{7,23},{8,0},{9,25... | collective-permute-start | bytes 3538952 | tf_op jit(solution)/shard_map/ppermute | solution.py:1289
  365.5 70.6 %reduce-scatter.12.cloned.1.call-start = ((), (), s32[]{:S(2)}) async-start(), calls=%async_computation.14 | async-start | bytes 1474560 | tf_op jit(solution)/shard_map/reduce_scatter | solution.py:1304
  383.8 52.3 %collective-permute-start.44 = (bf16[208,1536]{1,0:T(8,128)(2,1)S(1)}, bf16[208,1536]{1,0:T(8,128)(2,1)}, u32[]{:S(2)}, u32[]{:S(2)}) collective-permute-start(bf16[208,1536]{1,0:T(8,128)(2,1)S(1)} %copy-done.14), channel_id=1, source_target_pairs={{0,24},{1,25},{2,26},{3,27},{4,28},{5,29},{6,30},{7,31},{8,16},{9,... | collective-permute-start | bytes 1916936 | tf_op jit(solution)/shard_map/ppermute | solution.py:1289
  385.1 51.0 %collective-permute-start.43 = (bf16[208,1536]{1,0:T(8,128)(2,1)S(1)}, bf16[208,1536]{1,0:T(8,128)(2,1)}, u32[]{:S(2)}, u32[]{:S(2)}) collective-permute-start(bf16[208,1536]{1,0:T(8,128)(2,1)S(1)} %copy-done.14), channel_id=1, source_target_pairs={{0,16},{1,9},{2,18},{3,11},{4,20},{5,13},{6,22},{7,15},{8,24},{9,1... | collective-permute-start | bytes 1916936 | tf_op jit(solution)/shard_map/ppermute | solution.py:1289
  385.6 52.3 %collective-permute-start.42 = (bf16[208,1536]{1,0:T(8,128)(2,1)S(1)}, bf16[208,1536]{1,0:T(8,128)(2,1)}, u32[]{:S(2)}, u32[]{:S(2)}) collective-permute-start(bf16[208,1536]{1,0:T(8,128)(2,1)S(1)} %copy-done.14), channel_id=1, source_target_pairs={{0,8},{1,17},{2,10},{3,19},{4,12},{5,21},{6,14},{7,23},{8,0},{9,25... | collective-permute-start | bytes 1916936 | tf_op jit(solution)/shard_map/ppermute | solution.py:1289
  386.4 48.7 %collective-permute-start.34 = (bf16[384,768]{1,0:T(8,128)(2,1)}, bf16[384,768]{1,0:T(8,128)(2,1)}, u32[]{:S(2)}, u32[]{:S(2)}) collective-permute-start(bf16[384,768]{1,0:T(8,128)(2,1)} %sums.8.refs_2_), channel_id=1, source_target_pairs={{0,8},{1,17},{2,10},{3,19},{4,12},{5,21},{6,14},{7,23},{8,0},{9,25... | collective-permute-start | bytes 1769480 | tf_op jit(solution)/shard_map/ppermute | solution.py:1289
  399.2 39.5 %collective-permute-start.41 = (bf16[112,1344]{1,0:T(8,128)(2,1)}, bf16[112,1344]{1,0:T(8,128)(2,1)S(1)}, u32[]{:S(2)}, u32[]{:S(2)}) collective-permute-start(bf16[112,1344]{1,0:T(8,128)(2,1)} %bitcast.40), channel_id=1, source_target_pairs={{0,24},{1,25},{2,26},{3,27},{4,28},{5,29},{6,30},{7,31},{8,16},{9,... | collective-permute-start | bytes 903176 | tf_op jit(solution)/shard_map/ppermute | solution.py:1289
  (66 other events, 577.7 us)
Sparse Core Ops, SparseCore 0:
  11.2 44.0 all-gather.5
  57.5 40.4 all-gather.7
  99.6 40.3 all-gather.9
  141.5 40.3 all-gather.11
  271.8 30.0 reduce-scatter.5
  304.2 27.9 reduce-scatter.9
  335.2 27.8 reduce-scatter.7
  366.1 33.0 reduce-scatter.13
  401.5 27.9 reduce-scatter.11

commit v2 on v1

--- a/solution.py
+++ b/solution.py
@@ -785,11 +785,16 @@
 
 
 def attn_bwd_kernel(
-    meta, h0, h1, h2, h3, qrow, kcol, qkv, c0, c1, c2, c3, gctx, lse, t, *rest, heads, tokens
+    meta, h0, h1, h2, h3, qrow, kcol, qkv, c0, c1, c2, c3, gctx, lse, t, *rest, heads, tokens, paired
 ):
     (
-        g_own, g_a, g_b, g_d, dw_own, dw_other, q_s, k_s, v_s, do_s, kt_s, delta_s, dk_s, dv_s, dqt_s, g_s, w_s, ctx, dw, sems,
-    ) = rest[-20:]
+        dw_own, dw_other, q_s, k_s, v_s, do_s, kt_s, delta_s, dk_s, dv_s, dqt_s, g_s, w_s, ctx, dw, sems,
+    ) = rest[-16:]
+    if paired:
+        g_own, g_a, g_bd = rest[-19:-16]
+        g_b, g_d = g_bd.at[0], g_bd.at[1]
+    else:
+        g_own, g_a, g_b, g_d = rest[-20:-16]
     blocks = tokens // BLK
     hw = heads * HEAD_DIM
     scale = HEAD_DIM ** (-0.5)
@@ -1447,9 +1452,10 @@
 
         def attention_grads(*before):
             return call(
-                functools.partial(attn_bwd_kernel, heads=heads, tokens=tokens),
-                [
-                    ((rows, WIDTH), F32), ((rows, WIDTH), BF), ((rows, WIDTH), BF), ((rows, WIDTH), BF),
+                functools.partial(attn_bwd_kernel, heads=heads, tokens=tokens, paired=layer == 0),
+                [((rows, WIDTH), F32), ((rows, WIDTH), BF)]
+                + ([((2, rows, WIDTH), BF)] if layer == 0 else [((rows, WIDTH), BF)] * 2)
+                + [
                     ((4, cut + 16, 3 * hw), BF), ((4, cut + 16, 3 * hw), BF),
                 ],
                 (meta,) + gathered + (qrow, kcol, qkv) + tuple(ctx_own) + (gcx, lse, wide[2 * layer]) + before,
@@ -1484,20 +1490,21 @@
             t, a, b, dwo, d = weight_grads(gcx, att1, t1)
             t1 = reduce_z(t1)
             from_b, from_d = via_second(b), via_second(d)
-            g_own, g_a, g_b, g_d, dw, dw_other = attention_grads(t)
+            g_own, g_a, g_bd, dw, dw_other = attention_grads(t)
 
     def shards(x):
         return x.reshape(2, cut, WIDTH)
 
-    a0, t0 = sums([[(a, from_d)], [(t, from_b)]], g_d, weight=WEIGHT)
+    a0, t0 = sums([[(a, from_d)], [(t, from_b)]], g_bd, weight=WEIGHT)
     from_a = via_first(a0)
+    (d1,) = after((d1,), a0)
     merged, att0 = attention_shards(dwo, dw, via_core(dw_other), a0)
-    back = via_second(g_d), via_second(g_b)
+    back = via_second(g_bd)
     shape = (2 * cut + 16, 2 * WIDTH)
     (joined,) = call(
         join_kernel, [(shape, BF)], (att1, shards(t1), shards(via_diagonal(d1)), merged), V * 3 + A, [], "join", WEIGHT, 0
     )
-    (over,) = sums([[(g_a, back[0])]], joined)
+    (over,) = sums([[(g_a, back[1])]], joined)
     joined = spread_ctx(joined)
     (t0,) = sums([[(t0, from_a)]], over, weight=WEIGHT)
     over = via_first(over)
@@ -1544,7 +1551,7 @@
         placed = outs[:4]
         small_out = outs[4]
         vectors = outs[4:]
-    in_grad = add(gfs, g_own, back[1], over)[None]
+    in_grad = add(gfs, g_own, back[0], over)[None]
     e_out, r_out, i_out, o_out = placed
     ab, fg, fs, rb, sg, ss, qb, vb, xb = vectors
     return (out_act, in_grad, i_out, qb, vb, o_out, ab, fg, fs, e_out, xb, r_out, rb, sg, ss)

time: 477 us -> 474 us (level)
  waiting for transfers between devices: 163 us -> 158 us
    reduce_scatter x5, waiting for transfers between devices: 11.8 us -> 2.7 us  [reduce_z(): lax.psum_scatter(x, 'fsdp', scatter_dimension=0, tiled=True, axis_index_g...]
    ppermute x45 -> x44, waiting for transfers between devices: 112 us -> 115 us  [via(): return lambda x: lax.ppermute(x, axes, perm)]
    ppermute x45 -> x44, starting transfers between devices: 45.7 us -> 47.2 us  [via(): return lambda x: lax.ppermute(x, axes, perm)]
    unnamed x86 -> x92, local copies, waits for them, and re-layouts: 16.5 us -> 16 us
  transfers between devices with their start and end apart: 55 -> 54, of which waited for: 22 -> 23; matrix products, arithmetic and copies ran while one was open for 1% -> 2% of each run, Pallas kernels for 34% -> 34%
where the time goes in v2:
time: 474 us; the launch traced here: 465 us
  Pallas kernels  188 us (40%)
  waiting for transfers between devices  158 us (33%)
  starting transfers between devices  51.3 us (11%)
  blocking collectives  29.4 us (6%)
  local copies, waits for them, and re-layouts  20.6 us (4%)
  between operations  14.8 us (3%)
    ppermute x44, waiting for transfers between devices, via(): return lambda x: lax.ppermute(x, axes, perm)  115 us
    pallas_call x13, Pallas kernels, call(): pl.pallas_call(kernel, out_shape=[jax.ShapeDtypeStruct(shape, dtype) for...  97.7 us
    pallas_call x5, Pallas kernels, call_writing(): pl.pallas_call(functools.partial(run, scratch=len(scratch), **keys), out_...  70.1 us
    ppermute x44, starting transfers between devices, via(): return lambda x: lax.ppermute(x, axes, perm)  47.2 us
    all_gather x4, waiting for transfers between devices, gather_ffn(): x = lax.all_gather(x, 'fsdp', axis=0, tiled=True)  26.6 us
    all_gather x1, blocking collectives, on_device_fast(): starts = lax.all_gather(doc_start[0], 'ctx', axis=0, tiled=True)  16.6 us
    unnamed x92, local copies, waits for them, and re-layouts  16 us
    all_to_all x1, waiting for transfers between devices, on_device_fast(): gcx = lax.all_to_all(gctx, 'ctx', 0, 0, tiled=True)  13.1 us
  transfers between devices with their start and end apart: 54, of which 23 were waited for; matrix products, arithmetic and copies ran while one was open for 2% of the time, Pallas kernels for 34%

profile of v2, /device:TPU:1, one launch (start us, length us, event | category | flops | bytes accessed | tf_op | source)
XLA Modules:
  0.0 464.8 jit_solution(16426173726383331400)
XLA Ops:
  7.3 3.8 prep.1
  14.7 16.6 %all-gather = s32[1,1536]{1,0:T(1,128)S(1)} all-gather(s32[1,384]{1,0:T(1,128)S(1)} %copy-done.37), channel_id=2, replica_groups=mesh['ctx'=4,'fsdp'=8] {'ctx'}, dimensions={1}, use_global_device_ids=true | all-gather | bytes 7680 | tf_op jit(solution)/shard_map/all_gather | solution.py:1348
  32.7 8.1 %collective-permute-done.2.refs_4_.rest_2_.h3 = bf16[384,768]{1,0:T(8,128)(2,1)S(1)} collective-permute-done((bf16[384,768]{1,0:T(8,128)(2,1)S(1)}, bf16[384,768]{1,0:T(8,128)(2,1)S(1)}, u32[]{:S(2)}, u32[]{:S(2)}) %collective-permute-start.2) | collective-permute-done | bytes 589856 | tf_op jit(solution)/shard_map/ppermute | solution.py:1294
  40.8 14.4 %all-gather.6.cloned.1.call-done = bf16[2304,768]{1,0:T(8,128)(2,1)} async-done(((bf16[288,768]{1,0:T(8,128)(2,1)}), bf16[2304,768]{1,0:T(8,128)(2,1)}) %all-gather.6.cloned.1.call-update) | async-done | bytes 3538960 | tf_op jit(solution)/shard_map/all_gather | solution.py:1343
  62.3 14.9 %attn_fwd.2 = (bf16[4,384,576]{2,1,0:T(8,128)(2,1)}, bf16[192,384]{1,0:T(8,128)(2,1)}, bf16[192,384]{1,0:T(8,128)(2,1)}, bf16[192,384]{1,0:T(8,128)(2,1)}, bf16[192,384]{1,0:T(8,128)(2,1)}, /*index=5*/f32[8,1536]{1,0:T(8,128)}) custom-call(s32[20]{0:T(128)} %concatenate.7.meta.refs_0_, bf16[384,768]{1,0:T(8,128)(2,1)} %bitcast.38, ...), custom_call_target="tpu_custom_call" | custom-call | tf_op jit(solution)/shard_map/attn_fwd/pallas_call | solution.py:447
  80.0 4.1 collective-permute-done.7.b.refs_8_.refs_12_
  93.4 4.6 all-gather.8.cloned.1.call-done
  99.3 13.7 %mlp_fwd.1 = (f32[384,768]{1,0:T(8,128)}, f32[384,1]{1,0:T(8,128)}, bf16[384,3072]{1,0:T(8,128)(2,1)}, f32[384,768]{1,0:T(8,128)}, f32[384,1]{1,0:T(8,128)}, /*i...) custom-call(s32[20]{0:T(128)} %concatenate.7.meta.refs_0_, ...), custom_call_target="tpu_custom_call" | custom-call | tf_op jit(solution)/shard_map/mlp_fwd/pallas_call | solution.py:528
  115.5 11.0 %collective-permute-done.9.rest_0_.h1 = bf16[384,768]{1,0:T(8,128)(2,1)S(1)} collective-permute-done((bf16[384,768]{1,0:T(8,128)(2,1)}, bf16[384,768]{1,0:T(8,128)(2,1)S(1)}, u32[]{:S(2)}, u32[]{:S(2)}) %collective-permute-start.9) | collective-permute-done | bytes 589856 | tf_op jit(solution)/shard_map/ppermute | solution.py:1294
  130.8 5.5 %collective-permute-done.11.rest_2_.h3 = bf16[384,768]{1,0:T(8,128)(2,1)S(1)} collective-permute-done((bf16[384,768]{1,0:T(8,128)(2,1)S(1)}, bf16[384,768]{1,0:T(8,128)(2,1)S(1)}, u32[]{:S(2)}, u32[]{:S(2)}) %collective-permute-start.11) | collective-permute-done | bytes 589856 | tf_op jit(solution)/shard_map/ppermute | solution.py:1294
  146.4 15.2 %attn_fwd.3 = (bf16[4,384,576]{2,1,0:T(8,128)(2,1)}, bf16[192,384]{1,0:T(8,128)(2,1)}, bf16[192,384]{1,0:T(8,128)(2,1)}, bf16[192,384]{1,0:T(8,128)(2,1)}, bf16[192,384]{1,0:T(8,128)(2,1)}, /*index=5*/f32[8,1536]{1,0:T(8,128)}) custom-call(s32[20]{0:T(128)} %concatenate.7.meta.refs_0_, bf16[384,768]{1,0:T(8,128)(2,1)} %get-tuple-element.99.h0, ...), custom_call_target="tpu_custom_call" | custom-call | tf_op jit(solution)/shard_map/attn_fwd/pallas_call | solution.py:447
  161.7 7.2 %collective-permute-done.17.b.refs_9_ = bf16[4,2,96,768]{3,2,1,0:T(8,128)(2,1)S(1)} collective-permute-done((bf16[4,2,96,768]{3,2,1,0:T(8,128)(2,1)}, bf16[4,2,96,768]{3,2,1,0:T(8,128)(2,1)S(1)}, u32[]{:S(2)}, u32[]{:S(2)}) %collective-permute-start.17) | collective-permute-done | bytes 1179680 | tf_op jit(solution)/shard_map/ppermute | solution.py:1294
  178.0 3.9 all-gather.12.cloned.1.call-done
  186.8 19.2 %last.1 = (bf16[384,2304]{1,0:T(8,128)(2,1)}, bf16[384,2304]{1,0:T(8,128)(2,1)}, bf16[384,768]{1,0:T(8,128)(2,1)}, f32[384,768]{1,0:T(8,128)}, bf16[400,4608]{1,0:T(8,128)(2,1)}, /*index=5*/bf16[4,192,384]{2,1,0:T(8,128)(2,1)}) custom-call(s32[20]{0:T(128)} %concatenate.7.meta.refs_0_, bf16[192,384]{1,0:T(8,128)(2,1)} %get-tuple-element.102.refs_1_.c0, ...), custom_call_target="tpu_custom_call" | custom-call | tf_op jit(solution)/shard_map/last/pallas_call | solution.py:528
  206.8 12.8 %all_to_all.10.gctx = bf16[4,192,384]{2,1,0:T(8,128)(2,1)} all-to-all(bf16[4,192,384]{2,1,0:T(8,128)(2,1)} %get-tuple-element.117), channel_id=1, replica_groups=mesh['ctx'=4,'fsdp'=8] {'ctx'}, dimensions={0} | all-to-all | bytes 1179648 | tf_op jit(solution)/shard_map/all_to_all | solution.py:1439
  220.9 20.7 %attn_bwd.2 = (f32[384,768]{1,0:T(8,128)}, bf16[384,768]{1,0:T(8,128)(2,1)}, bf16[384,768]{1,0:T(8,128)(2,1)}, bf16[384,768]{1,0:T(8,128)(2,1)}, bf16[4,112,576]...) custom-call(s32[20]{0:T(128)} %concatenate.7.meta.refs_0_, bf16[384,768]{1,0:T(8,128)(2,1)} %get-tuple-element.99.h0, ...), custom_call_target="tpu_custom_call" | custom-call | tf_op jit(solution)/shard_map/attn_bwd/pallas_call | solution.py:447
  243.1 7.8 %collective-permute-done.21.refs_1_ = bf16[384,768]{1,0:T(8,128)(2,1)S(1)} collective-permute-done((bf16[384,768]{1,0:T(8,128)(2,1)}, bf16[384,768]{1,0:T(8,128)(2,1)S(1)}, u32[]{:S(2)}, u32[]{:S(2)}) %collective-permute-start.21) | collective-permute-done | bytes 589856 | tf_op jit(solution)/shard_map/ppermute | solution.py:1294
  257.3 10.8 %wgrad.2 = (bf16[4,2,96,768]{3,2,1,0:T(8,128)(2,1)}, bf16[4,2,96,768]{3,2,1,0:T(8,128)(2,1)}, bf16[4,2,96,768]{3,2,1,0:T(8,128)(2,1)}, bf16[4,112,768]{2,1,0:T(8,128)(2,1)}, bf16[4,2,96,768]{3,2,1,0:T(8,128)(2,1)}) custom-call(s32[20]{0:T(128)} %concatenate.7.meta.refs_0_, bf16[384,2304]{1,0:T(8,128)(2,1)} %get-tuple-element.123.refs_1_, ...), custom_call_target="tpu_custom_call" | custom-call | tf_op jit(solution)/shard_map/wgrad/pallas_call | solution.py:528
  274.1 15.9 %mlp_bwd.1 = (f32[384,768]{1,0:T(8,128)}, bf16[400,4608]{1,0:T(8,128)(2,1)}, bf16[4,192,384]{2,1,0:T(8,128)(2,1)}) custom-call(s32[20]{0:T(128)} %concatenate.7.meta.refs_0_, f32[384,768]{1,0:T(8,128)} %get-tuple-element.110.refs_1_, f32[384,1]{1,0:T(8,128)} %get-tuple-element.111.refs_2_, f32[384,768]{1,0:T(8,128)} %get-tuple-element.112.refs_3_, ...), custom_call_target="tpu_custom_call" | custom-call | tf_op jit(solution)/shard_map/mlp_bwd/pallas_call | solution.py:528
  294.2 13.1 %all-to-all-done.1.refs_3_.refs_5_.gctx = bf16[4,192,384]{2,1,0:T(8,128)(2,1)S(1)} async-done(((bf16[4,192,384]{2,1,0:T(8,128)(2,1)}), bf16[4,192,384]{2,1,0:T(8,128)(2,1)S(1)}, u32[]{:S(2)}, u32[]{:S(2)}) %all-to-all-start.1) | async-done | bytes 589856 | tf_op jit(solution)/shard_map/all_to_all | solution.py:1439
  312.5 10.6 %wgrad.3 = (bf16[4,2,96,768]{3,2,1,0:T(8,128)(2,1)}, bf16[4,2,96,768]{3,2,1,0:T(8,128)(2,1)}, bf16[4,2,96,768]{3,2,1,0:T(8,128)(2,1)}, bf16[4,112,768]{2,1,0:T(8,128)(2,1)}, bf16[4,2,96,768]{3,2,1,0:T(8,128)(2,1)}) custom-call(s32[20]{0:T(128)} %concatenate.7.meta.refs_0_, bf16[384,2304]{1,0:T(8,128)(2,1)} %get-tuple-element.135.refs_1_, ...), custom_call_target="tpu_custom_call" | custom-call | tf_op jit(solution)/shard_map/wgrad/pallas_call | solution.py:528
  324.9 20.5 %attn_bwd.3 = (f32[384,768]{1,0:T(8,128)}, bf16[384,768]{1,0:T(8,128)(2,1)}, bf16[2,384,768]{2,1,0:T(8,128)(2,1)}, bf16[4,112,576]{2,1,0:T(8,128)(2,1)}, bf16[4,112,576]{2,1,0:T(8,128)(2,1)}) custom-call(s32[20]{0:T(128)} %concatenate.7.meta.refs_0_, bf16[384,768]{1,0:T(8,128)(2,1)} %bitcast.40, bf16[384,768]{1,0:T(8,128)(2,1)} %copy-done.7, ...), custom_call_target="tpu_custom_call" | custom-call | tf_op jit(solution)/shard_map/attn_bwd/pallas_call | solution.py:447
  347.5 4.0 collective-permute-done.30.refs_3_
  352.5 4.1 sums.7
  361.8 5.3 %collective-permute-done.28 = bf16[2,384,768]{2,1,0:T(8,128)(2,1)} collective-permute-done((bf16[2,384,768]{2,1,0:T(8,128)(2,1)}, bf16[2,384,768]{2,1,0:T(8,128)(2,1)}, u32[]{:S(2)}, u32[]{:S(2)}) %collective-permute-start.28) | collective-permute-done | bytes 1179680 | tf_op jit(solution)/shard_map/ppermute | solution.py:1294
  369.1 4.5 collective-permute-done.31
  378.5 5.5 %collective-permute-done.34.refs_1_ = bf16[4,2,96,768]{3,2,1,0:T(8,128)(2,1)S(1)} collective-permute-done((bf16[4,2,96,768]{3,2,1,0:T(8,128)(2,1)S(1)}, bf16[4,2,96,768]{3,2,1,0:T(8,128)(2,1)S(1)}, u32[]{:S(2)}, u32[]{:S(2)}) %collective-permute-start.34) | collective-permute-done | bytes 1179680 | tf_op jit(solution)/shard_map/ppermute | solution.py:1294
  397.5 31.8 %collective-permute-done.33 = bf16[384,768]{1,0:T(8,128)(2,1)S(1)} collective-permute-done((bf16[384,768]{1,0:T(8,128)(2,1)}, bf16[384,768]{1,0:T(8,128)(2,1)S(1)}, u32[]{:S(2)}, u32[]{:S(2)}) %collective-permute-start.33) | collective-permute-done | bytes 589856 | tf_op jit(solution)/shard_map/ppermute | solution.py:1294
  436.7 4.9 %place.2 = (f32[2,96,3072]{2,1,0:T(8,128)}, f32[2,384,768]{2,1,0:T(8,128)}, f32[2,96,2304]{2,1,0:T(8,128)}, f32[2,96,768]{2,1,0:T(8,128)}, f32[16,96]{1,0:T(8,128)}) custom-call(s32[20]{0:T(128)} %concatenate.7.meta.refs_0_, bf16[208,1536]{1,0:T(8,128)(2,1)} %join.1.refs_2_.rest_0_, bf16[208,1536]{1,0:T(8,128)(2,1)} %collective-permute-done.41.rest_1_, ...), custom_call_target="tpu_custom_call" | custom-call | bytes 10485760 | tf_op jit(solution)/shard_map/place/pallas_call | solution.py:1533
  441.6 4.3 collective-permute-done.38.rest_5_
  445.9 5.1 %collective-permute-done.36.rest_2_ = bf16[2,96,768]{2,1,0:T(8,128)(2,1)S(1)} collective-permute-done((bf16[2,96,768]{2,1,0:T(8,128)(2,1)}, bf16[2,96,768]{2,1,0:T(8,128)(2,1)S(1)}, u32[]{:S(2)}, u32[]{:S(2)}) %collective-permute-start.36) | collective-permute-done | bytes 294944 | tf_op jit(solution)/shard_map/ppermute | solution.py:1294
  452.9 4.9 %place.3 = (f32[2,96,3072]{2,1,0:T(8,128)}, f32[2,384,768]{2,1,0:T(8,128)}, f32[2,96,2304]{2,1,0:T(8,128)}, f32[2,96,768]{2,1,0:T(8,128)}, f32[2,96]{1,0:T(2,128...) custom-call(s32[20]{0:T(128)} %concatenate.7.meta.refs_0_, ...), custom_call_target="tpu_custom_call", output_to_operand_aliasing={{0}: (10, {}), {1}: (11, {}), {2}: (12, {}), {3}: (13, {})} | custom-call | bytes 10485760 | tf_op jit(solution)/shard_map/place/pallas_call | solution.py:1533
  (228 shorter events, 121.5 us)
Async XLA Ops:
  7.2 48.1 %all-gather.6.cloned.1.call-start = ((), (), s32[]{:S(2)}) async-start(), calls=%async_computation.7 | async-start | bytes 3981312 | tf_op jit(solution)/shard_map/all_gather | solution.py:1343
  11.1 86.8 %all-gather.8.cloned.1.call-start = ((), (), s32[]{:S(2)}) async-start(), calls=%async_computation.8 | async-start | bytes 3981312 | tf_op jit(solution)/shard_map/all_gather | solution.py:1343
  11.1 21.6 %collective-permute-start.1 = (bf16[384,768]{1,0:T(8,128)(2,1)S(1)}, bf16[384,768]{1,0:T(8,128)(2,1)S(1)}, u32[]{:S(2)}, u32[]{:S(2)}) collective-permute-start(bf16[384,768]{1,0:T(8,128)(2,1)S(1)} %bitcast.41), channel_id=1, source_target_pairs={{0,16},{1,9},{2,18},{3,11},{4,20},{5,13},{6,22},{7,15},{8,24},{9,1... | collective-permute-start | bytes 1769480 | tf_op jit(solution)/shard_map/ppermute | solution.py:1294
  13.4 18.2 %collective-permute-start = (bf16[384,768]{1,0:T(8,128)(2,1)S(1)}, bf16[384,768]{1,0:T(8,128)(2,1)S(1)}, u32[]{:S(2)}, u32[]{:S(2)}) collective-permute-start(bf16[384,768]{1,0:T(8,128)(2,1)S(1)} %bitcast.42), channel_id=1, source_target_pairs={{0,8},{1,17},{2,10},{3,19},{4,12},{5,21},{6,14},{7,23},{8,0},{9,25... | collective-permute-start | bytes 1769480 | tf_op jit(solution)/shard_map/ppermute | solution.py:1294
  14.5 125.5 %all-gather.10.cloned.1.call-start = ((), (), s32[]{:S(2)}) async-start(), calls=%async_computation.9 | async-start | bytes 3981312 | tf_op jit(solution)/shard_map/all_gather | solution.py:1343
  58.0 26.1 %collective-permute-start.7 = (bf16[4,2,96,768]{3,2,1,0:T(8,128)(2,1)}, bf16[4,2,96,768]{3,2,1,0:T(8,128)(2,1)S(1)}, u32[]{:S(2)}, u32[]{:S(2)}) collective-permute-start(bf16[4,2,96,768]{3,2,1,0:T(8,128)(2,1)} %half.2.rest_0_), channel_id=1, source_target_pairs={{0,16},{1,9},{2,18},{3,11},{4,20},{5,13},{6,22},{7,15},{8,24},{9,1... | collective-permute-start | bytes 3538952 | tf_op jit(solution)/shard_map/ppermute | solution.py:1294
  59.3 28.2 %collective-permute-start.6 = (bf16[4,2,96,768]{3,2,1,0:T(8,128)(2,1)}, bf16[4,2,96,768]{3,2,1,0:T(8,128)(2,1)S(1)}, u32[]{:S(2)}, u32[]{:S(2)}) collective-permute-start(bf16[4,2,96,768]{3,2,1,0:T(8,128)(2,1)} %half.2.rest_0_), channel_id=1, source_target_pairs={{0,8},{1,17},{2,10},{3,19},{4,12},{5,21},{6,14},{7,23},{8,0},{9,25... | collective-permute-start | bytes 3538952 | tf_op jit(solution)/shard_map/ppermute | solution.py:1294
  79.9 102.0 %all-gather.12.cloned.1.call-start = ((), (), s32[]{:S(2)}) async-start(), calls=%async_computation.10 | async-start | bytes 3981312 | tf_op jit(solution)/shard_map/all_gather | solution.py:1343
  93.3 219.2 %reduce-scatter.6.cloned.1.call-start = ((), (), s32[]{:S(2)}) async-start(), calls=%async_computation.11 | async-start | bytes 1576960 | tf_op jit(solution)/shard_map/reduce_scatter | solution.py:1309
  142.7 26.1 %collective-permute-start.17 = (bf16[4,2,96,768]{3,2,1,0:T(8,128)(2,1)}, bf16[4,2,96,768]{3,2,1,0:T(8,128)(2,1)S(1)}, u32[]{:S(2)}, u32[]{:S(2)}) collective-permute-start(bf16[4,2,96,768]{3,2,1,0:T(8,128)(2,1)} %half.3.rest_0_), channel_id=1, source_target_pairs={{0,16},{1,9},{2,18},{3,11},{4,20},{5,13},{6,22},{7,15},{8,24},{9,1... | collective-permute-start | bytes 3538952 | tf_op jit(solution)/shard_map/ppermute | solution.py:1294
  144.0 27.8 %collective-permute-start.16 = (bf16[4,2,96,768]{3,2,1,0:T(8,128)(2,1)}, bf16[4,2,96,768]{3,2,1,0:T(8,128)(2,1)}, u32[]{:S(2)}, u32[]{:S(2)}) collective-permute-start(bf16[4,2,96,768]{3,2,1,0:T(8,128)(2,1)} %half.3.rest_0_), channel_id=1, source_target_pairs={{0,8},{1,17},{2,10},{3,19},{4,12},{5,21},{6,14},{7,23},{8,0},{9,25... | collective-permute-start | bytes 3538952 | tf_op jit(solution)/shard_map/ppermute | solution.py:1294
  206.0 51.3 %collective-permute-start.23 = (bf16[400,4608]{1,0:T(8,128)(2,1)}, bf16[400,4608]{1,0:T(8,128)(2,1)}, u32[]{:S(2)}, u32[]{:S(2)}) collective-permute-start(bf16[400,4608]{1,0:T(8,128)(2,1)} %get-tuple-element.124.refs_3_), channel_id=1, source_target_pairs={{0,1},{1,0},{2,3},{3,2},{4,5},{5,4},{6,7},{7,6},{8,9},{9,8},{10,11... | collective-permute-start | bytes 11059208 | tf_op jit(solution)/shard_map/ppermute | solution.py:1294
  242.3 29.3 %collective-permute-start.20 = (bf16[384,768]{1,0:T(8,128)(2,1)}, bf16[384,768]{1,0:T(8,128)(2,1)S(1)}, u32[]{:S(2)}, u32[]{:S(2)}) collective-permute-start(bf16[384,768]{1,0:T(8,128)(2,1)} %get-tuple-element.120), channel_id=1, source_target_pairs={{0,16},{1,9},{2,18},{3,11},{4,20},{5,13},{6,22},{7,15},{8,24},{9,1... | collective-permute-start | bytes 1769480 | tf_op jit(solution)/shard_map/ppermute | solution.py:1294
  253.9 17.7 %collective-permute-start.22 = (bf16[384,768]{1,0:T(8,128)(2,1)}, bf16[384,768]{1,0:T(8,128)(2,1)S(1)}, u32[]{:S(2)}, u32[]{:S(2)}) collective-permute-start(bf16[384,768]{1,0:T(8,128)(2,1)} %sums.5.refs_5_), channel_id=1, source_target_pairs={{0,8},{1,17},{2,10},{3,19},{4,12},{5,21},{6,14},{7,23},{8,0},{9,25... | collective-permute-start | bytes 1769480 | tf_op jit(solution)/shard_map/ppermute | solution.py:1294
  272.7 34.7 %collective-permute-start.26 = (bf16[4,2,96,768]{3,2,1,0:T(8,128)(2,1)}, bf16[4,2,96,768]{3,2,1,0:T(8,128)(2,1)S(1)}, u32[]{:S(2)}, u32[]{:S(2)}) collective-permute-start(bf16[4,2,96,768]{3,2,1,0:T(8,128)(2,1)} %get-tuple-element.130.refs_16_), channel_id=1, source_target_pairs={{0,8},{1,17},{2,10},{3,19},{4,12},{5,21},{6,14},{7,23},{8,0},{9,25... | collective-permute-start | bytes 3538952 | tf_op jit(solution)/shard_map/ppermute | solution.py:1294
  272.9 34.4 %collective-permute-start.27 = (bf16[4,2,96,768]{3,2,1,0:T(8,128)(2,1)}, bf16[4,2,96,768]{3,2,1,0:T(8,128)(2,1)S(1)}, u32[]{:S(2)}, u32[]{:S(2)}) collective-permute-start(bf16[4,2,96,768]{3,2,1,0:T(8,128)(2,1)} %get-tuple-element.131.refs_17_), channel_id=1, source_target_pairs={{0,16},{1,9},{2,18},{3,11},{4,20},{5,13},{6,22},{7,15},{8,24},{9,1... | collective-permute-start | bytes 3538952 | tf_op jit(solution)/shard_map/ppermute | solution.py:1294
  293.5 63.1 %reduce-scatter.10.cloned.1.call-start = ((), (), s32[]{:S(2)}) async-start(), calls=%async_computation.13 | async-start | bytes 1474560 | tf_op jit(solution)/shard_map/reduce_scatter | solution.py:1309
  293.5 18.9 %collective-permute-start.25 = (bf16[400,4608]{1,0:T(8,128)(2,1)}, bf16[400,4608]{1,0:T(8,128)(2,1)}, u32[]{:S(2)}, u32[]{:S(2)}) collective-permute-start(bf16[400,4608]{1,0:T(8,128)(2,1)} %get-tuple-element.136.refs_3_), channel_id=1, source_target_pairs={{0,1},{1,0},{2,3},{3,2},{4,5},{5,4},{6,7},{7,6},{8,9},{9,8},{10,11... | collective-permute-start | bytes 11059208 | tf_op jit(solution)/shard_map/ppermute | solution.py:1294
  294.2 74.9 %reduce-scatter.8.cloned.1.call-start = ((), (), s32[]{:S(2)}) async-start(), calls=%async_computation.12 | async-start | bytes 1474560 | tf_op jit(solution)/shard_map/reduce_scatter | solution.py:1309
  323.1 24.4 %collective-permute-start.29 = (bf16[4,2,96,768]{3,2,1,0:T(8,128)(2,1)}, bf16[4,2,96,768]{3,2,1,0:T(8,128)(2,1)S(1)}, u32[]{:S(2)}, u32[]{:S(2)}) collective-permute-start(bf16[4,2,96,768]{3,2,1,0:T(8,128)(2,1)} %get-tuple-element.144), channel_id=1, source_target_pairs={{0,16},{1,9},{2,18},{3,11},{4,20},{5,13},{6,22},{7,15},{8,24},{9,1... | collective-permute-start | bytes 3538952 | tf_op jit(solution)/shard_map/ppermute | solution.py:1294
  324.4 27.0 %collective-permute-start.30 = (bf16[4,2,96,768]{3,2,1,0:T(8,128)(2,1)}, bf16[4,2,96,768]{3,2,1,0:T(8,128)(2,1)S(1)}, u32[]{:S(2)}, u32[]{:S(2)}) collective-permute-start(bf16[4,2,96,768]{3,2,1,0:T(8,128)(2,1)} %get-tuple-element.145), channel_id=1, source_target_pairs={{0,16},{1,9},{2,18},{3,11},{4,20},{5,13},{6,22},{7,15},{8,24},{9,1... | collective-permute-start | bytes 3538952 | tf_op jit(solution)/shard_map/ppermute | solution.py:1294
  324.7 70.8 %reduce-scatter.14.cloned.1.call-start = ((), (), s32[]{:S(2)}) async-start(), calls=%async_computation.15 | async-start | bytes 1576960 | tf_op jit(solution)/shard_map/reduce_scatter | solution.py:1309
  346.5 20.6 %collective-permute-start.28 = (bf16[2,384,768]{2,1,0:T(8,128)(2,1)}, bf16[2,384,768]{2,1,0:T(8,128)(2,1)}, u32[]{:S(2)}, u32[]{:S(2)}) collective-permute-start(bf16[2,384,768]{2,1,0:T(8,128)(2,1)} %get-tuple-element.140.refs_4_), channel_id=1, source_target_pairs={{0,16},{1,9},{2,18},{3,11},{4,20},{5,13},{6,22},{7,15},{8,24},{9,1... | collective-permute-start | bytes 3538952 | tf_op jit(solution)/shard_map/ppermute | solution.py:1294
  358.9 25.1 %collective-permute-start.34 = (bf16[4,2,96,768]{3,2,1,0:T(8,128)(2,1)S(1)}, bf16[4,2,96,768]{3,2,1,0:T(8,128)(2,1)S(1)}, u32[]{:S(2)}, u32[]{:S(2)}) collective-permute-start(bf16[4,2,96,768]{3,2,1,0:T(8,128)(2,1)S(1)} %copy-done.17), channel_id=1, source_target_pairs={{0,8},{1,17},{2,10},{3,19},{4,12},{5,21},{6,14},{7,23},{8,0},{9,25... | collective-permute-start | bytes 3538952 | tf_op jit(solution)/shard_map/ppermute | solution.py:1294
  361.8 69.6 %reduce-scatter.12.cloned.1.call-start = ((), (), s32[]{:S(2)}) async-start(), calls=%async_computation.14 | async-start | bytes 1474560 | tf_op jit(solution)/shard_map/reduce_scatter | solution.py:1309
  389.1 41.7 %collective-permute-start.43 = (bf16[208,1536]{1,0:T(8,128)(2,1)S(1)}, bf16[208,1536]{1,0:T(8,128)(2,1)S(1)}, u32[]{:S(2)}, u32[]{:S(2)}) collective-permute-start(bf16[208,1536]{1,0:T(8,128)(2,1)S(1)} %copy-done.14), channel_id=1, source_target_pairs={{0,24},{1,25},{2,26},{3,27},{4,28},{5,29},{6,30},{7,31},{8,16},{9,... | collective-permute-start | bytes 1916936 | tf_op jit(solution)/shard_map/ppermute | solution.py:1294
  391.2 40.1 %collective-permute-start.42 = (bf16[208,1536]{1,0:T(8,128)(2,1)S(1)}, bf16[208,1536]{1,0:T(8,128)(2,1)}, u32[]{:S(2)}, u32[]{:S(2)}) collective-permute-start(bf16[208,1536]{1,0:T(8,128)(2,1)S(1)} %copy-done.14), channel_id=1, source_target_pairs={{0,16},{1,9},{2,18},{3,11},{4,20},{5,13},{6,22},{7,15},{8,24},{9,1... | collective-permute-start | bytes 1916936 | tf_op jit(solution)/shard_map/ppermute | solution.py:1294
  391.2 40.8 %collective-permute-start.41 = (bf16[208,1536]{1,0:T(8,128)(2,1)S(1)}, bf16[208,1536]{1,0:T(8,128)(2,1)}, u32[]{:S(2)}, u32[]{:S(2)}) collective-permute-start(bf16[208,1536]{1,0:T(8,128)(2,1)S(1)} %copy-done.14), channel_id=1, source_target_pairs={{0,8},{1,17},{2,10},{3,19},{4,12},{5,21},{6,14},{7,23},{8,0},{9,25... | collective-permute-start | bytes 1916936 | tf_op jit(solution)/shard_map/ppermute | solution.py:1294
  391.8 37.6 %collective-permute-start.33 = (bf16[384,768]{1,0:T(8,128)(2,1)}, bf16[384,768]{1,0:T(8,128)(2,1)S(1)}, u32[]{:S(2)}, u32[]{:S(2)}) collective-permute-start(bf16[384,768]{1,0:T(8,128)(2,1)} %sums.8.refs_2_), channel_id=1, source_target_pairs={{0,8},{1,17},{2,10},{3,19},{4,12},{5,21},{6,14},{7,23},{8,0},{9,25... | collective-permute-start | bytes 1769480 | tf_op jit(solution)/shard_map/ppermute | solution.py:1294
  395.4 38.1 %collective-permute-start.40 = (bf16[112,1344]{1,0:T(8,128)(2,1)}, bf16[112,1344]{1,0:T(8,128)(2,1)S(1)}, u32[]{:S(2)}, u32[]{:S(2)}) collective-permute-start(bf16[112,1344]{1,0:T(8,128)(2,1)} %bitcast.47), channel_id=1, source_target_pairs={{0,24},{1,25},{2,26},{3,27},{4,28},{5,29},{6,30},{7,31},{8,16},{9,... | collective-permute-start | bytes 903176 | tf_op jit(solution)/shard_map/ppermute | solution.py:1294
  432.1 18.9 %collective-permute-start.36 = (bf16[2,96,768]{2,1,0:T(8,128)(2,1)}, bf16[2,96,768]{2,1,0:T(8,128)(2,1)S(1)}, u32[]{:S(2)}, u32[]{:S(2)}) collective-permute-start(bf16[2,96,768]{2,1,0:T(8,128)(2,1)} %bitcast.52), channel_id=1, source_target_pairs={{0,16},{1,9},{2,18},{3,11},{4,20},{5,13},{6,22},{7,15},{8,24},{9,1... | collective-permute-start | bytes 884744 | tf_op jit(solution)/shard_map/ppermute | solution.py:1294
  433.5 18.7 %collective-permute-start.35 = (bf16[2,96,768]{2,1,0:T(8,128)(2,1)}, bf16[2,96,768]{2,1,0:T(8,128)(2,1)S(1)}, u32[]{:S(2)}, u32[]{:S(2)}) collective-permute-start(bf16[2,96,768]{2,1,0:T(8,128)(2,1)} %bitcast.53), channel_id=1, source_target_pairs={{0,8},{1,17},{2,10},{3,19},{4,12},{5,21},{6,14},{7,23},{8,0},{9,25... | collective-permute-start | bytes 884744 | tf_op jit(solution)/shard_map/ppermute | solution.py:1294
  (68 other events, 537.0 us)
Sparse Core Ops, SparseCore 0:
  11.2 44.0 all-gather.5
  57.5 40.4 all-gather.7
  99.6 40.3 all-gather.9
  141.5 40.3 all-gather.11
  271.7 30.0 reduce-scatter.5
  304.1 27.9 reduce-scatter.9
  335.1 27.8 reduce-scatter.7
  366.1 29.3 reduce-scatter.13
  397.7 27.9 reduce-scatter.11

commit v3 on v1

--- a/solution.py
+++ b/solution.py
@@ -659,6 +659,10 @@
             break
 
 
+def parts_kernel(*refs, layout, count, skip):
+    sums_kernel(*refs[:count], *refs[count + skip :], layout=layout, count=count, split=0)
+
+
 def sums(outputs, *others, split=0, weight=0):
     args = tuple(x for groups in outputs for group in groups for x in group)
     layout = tuple(tuple(len(group) for group in groups) for groups in outputs)
@@ -669,6 +673,18 @@
         shapes = [
             (groups[0][0].shape[:-1] + (sum(group[0].shape[-1] for group in groups),), BF) for groups in outputs
         ]
+    if not split and args[0].ndim == 4:
+        part = pl.BlockSpec((1,) + args[0].shape[1:], lambda n: (n, 0, 0, 0))
+        return pl.pallas_call(
+            functools.partial(parts_kernel, layout=layout, count=len(args), skip=len(others)),
+            grid=(args[0].shape[0],),
+            out_shape=[jax.ShapeDtypeStruct(shape, dtype) for shape, dtype in shapes],
+            in_specs=[part] * len(args) + [pl.BlockSpec(memory_space=pl.ANY)] * len(others),
+            out_specs=[part] * len(shapes),
+            compiler_params=pltpu.CompilerParams(vmem_limit_bytes=VMEM_LIMIT),
+            cost_estimate=pl.CostEstimate(flops=weight, bytes_accessed=0, transcendentals=0),
+            name="sums",
+        )(*args, *others)
     return call(
         functools.partial(sums_kernel, layout=layout, count=len(args), split=split),
         shapes, args + others, [pltpu.VMEM] * len(args) + [pl.ANY] * len(others), [], "sums", weight, 0,

time: 477 us -> 479 us (level)
  Pallas kernels: 188 us -> 197 us
  waiting for transfers between devices: 163 us -> 156 us
    pallas_call x0 -> x3, Pallas kernels: none -> 12.2 us  [sums(): pl.pallas_call(functools.partial(parts_kernel, layout=layout, count=len(a...]
    reduce_scatter x5, waiting for transfers between devices: 11.8 us -> 6.92 us  [reduce_z(): lax.psum_scatter(x, 'fsdp', scatter_dimension=0, tiled=True, axis_index_g...]
    pallas_call x13 -> x10, Pallas kernels: 97.7 us -> 94.5 us  [call(): pl.pallas_call(kernel, out_shape=[jax.ShapeDtypeStruct(shape, dtype) for...]
  transfers between devices with their start and end apart: 55 -> 55, of which waited for: 22 -> 22; matrix products, arithmetic and copies ran while one was open for 1% -> 1% of each run, Pallas kernels for 34% -> 36%
where the time goes in v3:
time: 479 us; the launch traced here: 471 us
  Pallas kernels  197 us (41%)
  waiting for transfers between devices  156 us (33%)
  starting transfers between devices  51.3 us (11%)
  blocking collectives  29.4 us (6%)
  local copies, waits for them, and re-layouts  18.7 us (4%)
  between operations  14.8 us (3%)
    ppermute x45, waiting for transfers between devices, via(): return lambda x: lax.ppermute(x, axes, perm)  109 us
    pallas_call x10, Pallas kernels, call(): pl.pallas_call(kernel, out_shape=[jax.ShapeDtypeStruct(shape, dtype) for...  94.5 us
    pallas_call x5, Pallas kernels, call_writing(): pl.pallas_call(functools.partial(run, scratch=len(scratch), **keys), out_...  70.2 us
    ppermute x45, starting transfers between devices, via(): return lambda x: lax.ppermute(x, axes, perm)  47.3 us
    all_gather x4, waiting for transfers between devices, gather_ffn(): x = lax.all_gather(x, 'fsdp', axis=0, tiled=True)  26.7 us
    all_gather x1, blocking collectives, on_device_fast(): starts = lax.all_gather(doc_start[0], 'ctx', axis=0, tiled=True)  16.6 us
    unnamed x86, local copies, waits for them, and re-layouts  16 us
    all_to_all x1, waiting for transfers between devices, on_device_fast(): gcx = lax.all_to_all(gctx, 'ctx', 0, 0, tiled=True)  13.1 us
  transfers between devices with their start and end apart: 55, of which 22 were waited for; matrix products, arithmetic and copies ran while one was open for 1% of the time, Pallas kernels for 36%

profile of v3, /device:TPU:1, one launch (start us, length us, event | category | flops | bytes accessed | tf_op | source)
XLA Modules:
  0.0 470.6 jit_solution(5660034486383410676)
XLA Ops:
  7.3 3.8 prep.1
  14.7 16.6 %all-gather = s32[1,1536]{1,0:T(1,128)S(1)} all-gather(s32[1,384]{1,0:T(1,128)S(1)} %copy-done.34), channel_id=2, replica_groups=mesh['ctx'=4,'fsdp'=8] {'ctx'}, dimensions={1}, use_global_device_ids=true | all-gather | bytes 7680 | tf_op jit(solution)/shard_map/all_gather | solution.py:1359
  32.8 8.1 %collective-permute-done.2.refs_4_.rest_2_.h3 = bf16[384,768]{1,0:T(8,128)(2,1)S(1)} collective-permute-done((bf16[384,768]{1,0:T(8,128)(2,1)S(1)}, bf16[384,768]{1,0:T(8,128)(2,1)S(1)}, u32[]{:S(2)}, u32[]{:S(2)}) %collective-permute-start.2) | collective-permute-done | bytes 589856 | tf_op jit(solution)/shard_map/ppermute | solution.py:1305
  40.8 14.4 %all-gather.6.cloned.1.call-done = bf16[2304,768]{1,0:T(8,128)(2,1)} async-done(((bf16[288,768]{1,0:T(8,128)(2,1)}), bf16[2304,768]{1,0:T(8,128)(2,1)}) %all-gather.6.cloned.1.call-update) | async-done | bytes 3538960 | tf_op jit(solution)/shard_map/all_gather | solution.py:1354
  62.2 16.6 %attn_fwd.2 = (bf16[4,384,576]{2,1,0:T(8,128)(2,1)}, bf16[192,384]{1,0:T(8,128)(2,1)}, bf16[192,384]{1,0:T(8,128)(2,1)}, bf16[192,384]{1,0:T(8,128)(2,1)}, bf16[192,384]{1,0:T(8,128)(2,1)}, /*index=5*/f32[8,1536]{1,0:T(8,128)}) custom-call(s32[20]{0:T(128)} %concatenate.7.meta.refs_0_, bf16[384,768]{1,0:T(8,128)(2,1)} %bitcast.31, ...), custom_call_target="tpu_custom_call" | custom-call | tf_op jit(solution)/shard_map/attn_fwd/pallas_call | solution.py:447
  93.4 4.6 all-gather.8.cloned.1.call-done
  99.3 13.7 %mlp_fwd.1 = (f32[384,768]{1,0:T(8,128)}, f32[384,1]{1,0:T(8,128)}, bf16[384,3072]{1,0:T(8,128)(2,1)}, f32[384,768]{1,0:T(8,128)}, f32[384,1]{1,0:T(8,128)}, /*i...) custom-call(s32[20]{0:T(128)} %concatenate.7.meta.refs_0_, ...), custom_call_target="tpu_custom_call" | custom-call | tf_op jit(solution)/shard_map/mlp_fwd/pallas_call | solution.py:528
  115.4 11.0 %collective-permute-done.9.rest_0_.h1 = bf16[384,768]{1,0:T(8,128)(2,1)S(1)} collective-permute-done((bf16[384,768]{1,0:T(8,128)(2,1)}, bf16[384,768]{1,0:T(8,128)(2,1)S(1)}, u32[]{:S(2)}, u32[]{:S(2)}) %collective-permute-start.9) | collective-permute-done | bytes 589856 | tf_op jit(solution)/shard_map/ppermute | solution.py:1305
  130.8 5.5 %collective-permute-done.11.rest_2_.h3 = bf16[384,768]{1,0:T(8,128)(2,1)S(1)} collective-permute-done((bf16[384,768]{1,0:T(8,128)(2,1)S(1)}, bf16[384,768]{1,0:T(8,128)(2,1)S(1)}, u32[]{:S(2)}, u32[]{:S(2)}) %collective-permute-start.11) | collective-permute-done | bytes 589856 | tf_op jit(solution)/shard_map/ppermute | solution.py:1305
  136.3 3.7 all-gather.10.cloned.1.call-done
  146.4 17.0 %attn_fwd.3 = (bf16[4,384,576]{2,1,0:T(8,128)(2,1)}, bf16[192,384]{1,0:T(8,128)(2,1)}, bf16[192,384]{1,0:T(8,128)(2,1)}, bf16[192,384]{1,0:T(8,128)(2,1)}, bf16[192,384]{1,0:T(8,128)(2,1)}, /*index=5*/f32[8,1536]{1,0:T(8,128)}) custom-call(s32[20]{0:T(128)} %concatenate.7.meta.refs_0_, bf16[384,768]{1,0:T(8,128)(2,1)} %get-tuple-element.100.h0, ...), custom_call_target="tpu_custom_call" | custom-call | tf_op jit(solution)/shard_map/attn_fwd/pallas_call | solution.py:447
  163.4 5.4 %collective-permute-done.17.b.refs_9_ = bf16[4,2,96,768]{3,2,1,0:T(8,128)(2,1)S(1)} collective-permute-done((bf16[4,2,96,768]{3,2,1,0:T(8,128)(2,1)}, bf16[4,2,96,768]{3,2,1,0:T(8,128)(2,1)S(1)}, u32[]{:S(2)}, u32[]{:S(2)}) %collective-permute-start.17) | collective-permute-done | bytes 1179680 | tf_op jit(solution)/shard_map/ppermute | solution.py:1305
  177.9 4.0 all-gather.12.cloned.1.call-done
  186.9 19.2 %last.1 = (bf16[384,2304]{1,0:T(8,128)(2,1)}, bf16[384,2304]{1,0:T(8,128)(2,1)}, bf16[384,768]{1,0:T(8,128)(2,1)}, f32[384,768]{1,0:T(8,128)}, bf16[400,4608]{1,0:T(8,128)(2,1)}, /*index=5*/bf16[4,192,384]{2,1,0:T(8,128)(2,1)}) custom-call(s32[20]{0:T(128)} %concatenate.7.meta.refs_0_, bf16[192,384]{1,0:T(8,128)(2,1)} %get-tuple-element.103.refs_1_.c0, ...), custom_call_target="tpu_custom_call" | custom-call | tf_op jit(solution)/shard_map/last/pallas_call | solution.py:528
  206.9 12.8 %all_to_all.10.gctx = bf16[4,192,384]{2,1,0:T(8,128)(2,1)} all-to-all(bf16[4,192,384]{2,1,0:T(8,128)(2,1)} %get-tuple-element.118), channel_id=1, replica_groups=mesh['ctx'=4,'fsdp'=8] {'ctx'}, dimensions={0} | all-to-all | bytes 1179648 | tf_op jit(solution)/shard_map/all_to_all | solution.py:1450
  221.0 22.7 %attn_bwd.2 = (f32[384,768]{1,0:T(8,128)}, bf16[384,768]{1,0:T(8,128)(2,1)}, bf16[384,768]{1,0:T(8,128)(2,1)}, bf16[384,768]{1,0:T(8,128)(2,1)}, bf16[4,112,576]...) custom-call(s32[20]{0:T(128)} %concatenate.7.meta.refs_0_, bf16[384,768]{1,0:T(8,128)(2,1)} %get-tuple-element.100.h0, ...), custom_call_target="tpu_custom_call" | custom-call | tf_op jit(solution)/shard_map/attn_bwd/pallas_call | solution.py:447
  245.3 7.8 %collective-permute-done.21.refs_1_ = bf16[384,768]{1,0:T(8,128)(2,1)S(1)} collective-permute-done((bf16[384,768]{1,0:T(8,128)(2,1)}, bf16[384,768]{1,0:T(8,128)(2,1)S(1)}, u32[]{:S(2)}, u32[]{:S(2)}) %collective-permute-start.21) | collective-permute-done | bytes 589856 | tf_op jit(solution)/shard_map/ppermute | solution.py:1305
  259.4 10.8 %wgrad.2 = (bf16[4,2,96,768]{3,2,1,0:T(8,128)(2,1)}, bf16[4,2,96,768]{3,2,1,0:T(8,128)(2,1)}, bf16[4,2,96,768]{3,2,1,0:T(8,128)(2,1)}, bf16[4,112,768]{2,1,0:T(8,128)(2,1)}, bf16[4,2,96,768]{3,2,1,0:T(8,128)(2,1)}) custom-call(s32[20]{0:T(128)} %concatenate.7.meta.refs_0_, bf16[384,2304]{1,0:T(8,128)(2,1)} %get-tuple-element.124.refs_1_, ...), custom_call_target="tpu_custom_call" | custom-call | tf_op jit(solution)/shard_map/wgrad/pallas_call | solution.py:528
  276.2 16.0 %mlp_bwd.1 = (f32[384,768]{1,0:T(8,128)}, bf16[400,4608]{1,0:T(8,128)(2,1)}, bf16[4,192,384]{2,1,0:T(8,128)(2,1)}) custom-call(s32[20]{0:T(128)} %concatenate.7.meta.refs_0_, f32[384,768]{1,0:T(8,128)} %get-tuple-element.111.refs_1_, f32[384,1]{1,0:T(8,128)} %get-tuple-element.112.refs_2_, f32[384,768]{1,0:T(8,128)} %get-tuple-element.113.refs_3_, ...), custom_call_target="tpu_custom_call" | custom-call | tf_op jit(solution)/shard_map/mlp_bwd/pallas_call | solution.py:528
  296.3 13.1 %all-to-all-done.1.refs_3_.refs_5_.gctx = bf16[4,192,384]{2,1,0:T(8,128)(2,1)S(1)} async-done(((bf16[4,192,384]{2,1,0:T(8,128)(2,1)}), bf16[4,192,384]{2,1,0:T(8,128)(2,1)S(1)}, u32[]{:S(2)}, u32[]{:S(2)}) %all-to-all-start.1) | async-done | bytes 589856 | tf_op jit(solution)/shard_map/all_to_all | solution.py:1450
  311.0 4.0 sums.6.refs_7_
  315.0 10.6 %wgrad.3 = (bf16[4,2,96,768]{3,2,1,0:T(8,128)(2,1)}, bf16[4,2,96,768]{3,2,1,0:T(8,128)(2,1)}, bf16[4,2,96,768]{3,2,1,0:T(8,128)(2,1)}, bf16[4,112,768]{2,1,0:T(8,128)(2,1)}, bf16[4,2,96,768]{3,2,1,0:T(8,128)(2,1)}) custom-call(s32[20]{0:T(128)} %concatenate.7.meta.refs_0_, bf16[384,2304]{1,0:T(8,128)(2,1)} %get-tuple-element.136.refs_1_, ...), custom_call_target="tpu_custom_call" | custom-call | tf_op jit(solution)/shard_map/wgrad/pallas_call | solution.py:528
  327.5 3.8 reduce-scatter.10.cloned.1.call-done
  333.4 22.6 %attn_bwd.3 = (f32[384,768]{1,0:T(8,128)}, bf16[384,768]{1,0:T(8,128)(2,1)}, bf16[384,768]{1,0:T(8,128)(2,1)}, bf16[384,768]{1,0:T(8,128)(2,1)}, bf16[4,112,576]...) custom-call(s32[20]{0:T(128)} %concatenate.7.meta.refs_0_, bf16[384,768]{1,0:T(8,128)(2,1)} %bitcast.33, ...), custom_call_target="tpu_custom_call" | custom-call | tf_op jit(solution)/shard_map/attn_bwd/pallas_call | solution.py:447
  358.8 4.4 sums.7
  372.2 8.1 %collective-permute-done.35.refs_1_ = bf16[4,2,96,768]{3,2,1,0:T(8,128)(2,1)S(1)} collective-permute-done((bf16[4,2,96,768]{3,2,1,0:T(8,128)(2,1)}, bf16[4,2,96,768]{3,2,1,0:T(8,128)(2,1)S(1)}, u32[]{:S(2)}, u32[]{:S(2)}) %collective-permute-start.35) | collective-permute-done | bytes 1179680 | tf_op jit(solution)/shard_map/ppermute | solution.py:1305
  381.4 3.9 sums.9.rest_4_
  390.3 5.8 %collective-permute-done.28 = bf16[384,768]{1,0:T(8,128)(2,1)} collective-permute-done((bf16[384,768]{1,0:T(8,128)(2,1)}, bf16[384,768]{1,0:T(8,128)(2,1)}, u32[]{:S(2)}, u32[]{:S(2)}) %collective-permute-start.28) | collective-permute-done | bytes 589856 | tf_op jit(solution)/shard_map/ppermute | solution.py:1305
  401.2 36.9 %collective-permute-done.34 = bf16[384,768]{1,0:T(8,128)(2,1)} collective-permute-done((bf16[384,768]{1,0:T(8,128)(2,1)}, bf16[384,768]{1,0:T(8,128)(2,1)}, u32[]{:S(2)}, u32[]{:S(2)}) %collective-permute-start.34) | collective-permute-done | bytes 589856 | tf_op jit(solution)/shard_map/ppermute | solution.py:1305
  444.7 4.9 %place.2 = (f32[2,96,3072]{2,1,0:T(8,128)}, f32[2,384,768]{2,1,0:T(8,128)}, f32[2,96,2304]{2,1,0:T(8,128)}, f32[2,96,768]{2,1,0:T(8,128)}, f32[16,96]{1,0:T(8,128)}) custom-call(s32[20]{0:T(128)} %concatenate.7.meta.refs_0_, bf16[208,1536]{1,0:T(8,128)(2,1)} %join.1.refs_2_.rest_0_, bf16[208,1536]{1,0:T(8,128)(2,1)} %collective-permute-done.42.rest_1_, ...), custom_call_target="tpu_custom_call" | custom-call | bytes 10485760 | tf_op jit(solution)/shard_map/place/pallas_call | solution.py:1542
  449.6 4.8 %collective-permute-done.39.rest_5_ = bf16[112,1344]{1,0:T(8,128)(2,1)} collective-permute-done((bf16[112,1344]{1,0:T(8,128)(2,1)}, bf16[112,1344]{1,0:T(8,128)(2,1)}, u32[]{:S(2)}, u32[]{:S(2)}) %collective-permute-start.39) | collective-permute-done | bytes 301088 | tf_op jit(solution)/shard_map/ppermute | solution.py:1305
  458.8 4.9 %place.3 = (f32[2,96,3072]{2,1,0:T(8,128)}, f32[2,384,768]{2,1,0:T(8,128)}, f32[2,96,2304]{2,1,0:T(8,128)}, f32[2,96,768]{2,1,0:T(8,128)}, f32[2,96]{1,0:T(2,128...) custom-call(s32[20]{0:T(128)} %concatenate.7.meta.refs_0_, ...), custom_call_target="tpu_custom_call", output_to_operand_aliasing={{0}: (10, {}), {1}: (11, {}), {2}: (12, {}), {3}: (13, {})} | custom-call | bytes 10485760 | tf_op jit(solution)/shard_map/place/pallas_call | solution.py:1542
  (222 shorter events, 114.6 us)
Async XLA Ops:
  7.2 48.0 %all-gather.6.cloned.1.call-start = ((), (), s32[]{:S(2)}) async-start(), calls=%async_computation.7 | async-start | bytes 3981312 | tf_op jit(solution)/shard_map/all_gather | solution.py:1354
  11.1 86.8 %all-gather.8.cloned.1.call-start = ((), (), s32[]{:S(2)}) async-start(), calls=%async_computation.8 | async-start | bytes 3981312 | tf_op jit(solution)/shard_map/all_gather | solution.py:1354
  11.1 21.6 %collective-permute-start.1 = (bf16[384,768]{1,0:T(8,128)(2,1)S(1)}, bf16[384,768]{1,0:T(8,128)(2,1)S(1)}, u32[]{:S(2)}, u32[]{:S(2)}) collective-permute-start(bf16[384,768]{1,0:T(8,128)(2,1)S(1)} %bitcast.34), channel_id=1, source_target_pairs={{0,16},{1,9},{2,18},{3,11},{4,20},{5,13},{6,22},{7,15},{8,24},{9,1... | collective-permute-start | bytes 1769480 | tf_op jit(solution)/shard_map/ppermute | solution.py:1305
  13.4 18.2 %collective-permute-start = (bf16[384,768]{1,0:T(8,128)(2,1)S(1)}, bf16[384,768]{1,0:T(8,128)(2,1)S(1)}, u32[]{:S(2)}, u32[]{:S(2)}) collective-permute-start(bf16[384,768]{1,0:T(8,128)(2,1)S(1)} %bitcast.35), channel_id=1, source_target_pairs={{0,8},{1,17},{2,10},{3,19},{4,12},{5,21},{6,14},{7,23},{8,0},{9,25... | collective-permute-start | bytes 1769480 | tf_op jit(solution)/shard_map/ppermute | solution.py:1305
  14.5 125.5 %all-gather.10.cloned.1.call-start = ((), (), s32[]{:S(2)}) async-start(), calls=%async_computation.9 | async-start | bytes 3981312 | tf_op jit(solution)/shard_map/all_gather | solution.py:1354
  58.0 26.1 %collective-permute-start.7 = (bf16[4,2,96,768]{3,2,1,0:T(8,128)(2,1)}, bf16[4,2,96,768]{3,2,1,0:T(8,128)(2,1)S(1)}, u32[]{:S(2)}, u32[]{:S(2)}) collective-permute-start(bf16[4,2,96,768]{3,2,1,0:T(8,128)(2,1)} %half.2.rest_0_), channel_id=1, source_target_pairs={{0,16},{1,9},{2,18},{3,11},{4,20},{5,13},{6,22},{7,15},{8,24},{9,1... | collective-permute-start | bytes 3538952 | tf_op jit(solution)/shard_map/ppermute | solution.py:1305
  59.3 28.2 %collective-permute-start.6 = (bf16[4,2,96,768]{3,2,1,0:T(8,128)(2,1)}, bf16[4,2,96,768]{3,2,1,0:T(8,128)(2,1)S(1)}, u32[]{:S(2)}, u32[]{:S(2)}) collective-permute-start(bf16[4,2,96,768]{3,2,1,0:T(8,128)(2,1)} %half.2.rest_0_), channel_id=1, source_target_pairs={{0,8},{1,17},{2,10},{3,19},{4,12},{5,21},{6,14},{7,23},{8,0},{9,25... | collective-permute-start | bytes 3538952 | tf_op jit(solution)/shard_map/ppermute | solution.py:1305
  81.6 100.3 %all-gather.12.cloned.1.call-start = ((), (), s32[]{:S(2)}) async-start(), calls=%async_computation.10 | async-start | bytes 3981312 | tf_op jit(solution)/shard_map/all_gather | solution.py:1354
  93.3 221.7 %reduce-scatter.6.cloned.1.call-start = ((), (), s32[]{:S(2)}) async-start(), calls=%async_computation.11 | async-start | bytes 1576960 | tf_op jit(solution)/shard_map/reduce_scatter | solution.py:1320
  128.6 16.6 %collective-permute-start.12 = (bf16[384,2304]{1,0:T(8,128)(2,1)}, bf16[384,2304]{1,0:T(8,128)(2,1)S(1)}, u32[]{:S(2)}, u32[]{:S(2)}) collective-permute-start(bf16[384,2304]{1,0:T(8,128)(2,1)} %get-tuple-element.102), channel_id=1, source_target_pairs={{0,1},{1,0},{2,3},{3,2},{4,5},{5,4},{6,7},{7,6},{8,9},{9,8},{10,11... | collective-permute-start | bytes 5308424 | tf_op jit(solution)/shard_map/ppermute | solution.py:1305
  142.7 26.1 %collective-permute-start.17 = (bf16[4,2,96,768]{3,2,1,0:T(8,128)(2,1)}, bf16[4,2,96,768]{3,2,1,0:T(8,128)(2,1)S(1)}, u32[]{:S(2)}, u32[]{:S(2)}) collective-permute-start(bf16[4,2,96,768]{3,2,1,0:T(8,128)(2,1)} %half.3.rest_0_), channel_id=1, source_target_pairs={{0,16},{1,9},{2,18},{3,11},{4,20},{5,13},{6,22},{7,15},{8,24},{9,1... | collective-permute-start | bytes 3538952 | tf_op jit(solution)/shard_map/ppermute | solution.py:1305
  144.0 27.8 %collective-permute-start.16 = (bf16[4,2,96,768]{3,2,1,0:T(8,128)(2,1)}, bf16[4,2,96,768]{3,2,1,0:T(8,128)(2,1)}, u32[]{:S(2)}, u32[]{:S(2)}) collective-permute-start(bf16[4,2,96,768]{3,2,1,0:T(8,128)(2,1)} %half.3.rest_0_), channel_id=1, source_target_pairs={{0,8},{1,17},{2,10},{3,19},{4,12},{5,21},{6,14},{7,23},{8,0},{9,25... | collective-permute-start | bytes 3538952 | tf_op jit(solution)/shard_map/ppermute | solution.py:1305
  206.1 53.3 %collective-permute-start.23 = (bf16[400,4608]{1,0:T(8,128)(2,1)}, bf16[400,4608]{1,0:T(8,128)(2,1)}, u32[]{:S(2)}, u32[]{:S(2)}) collective-permute-start(bf16[400,4608]{1,0:T(8,128)(2,1)} %get-tuple-element.125.refs_3_), channel_id=1, source_target_pairs={{0,1},{1,0},{2,3},{3,2},{4,5},{5,4},{6,7},{7,6},{8,9},{9,8},{10,11... | collective-permute-start | bytes 11059208 | tf_op jit(solution)/shard_map/ppermute | solution.py:1305
  244.4 29.3 %collective-permute-start.20 = (bf16[384,768]{1,0:T(8,128)(2,1)}, bf16[384,768]{1,0:T(8,128)(2,1)S(1)}, u32[]{:S(2)}, u32[]{:S(2)}) collective-permute-start(bf16[384,768]{1,0:T(8,128)(2,1)} %get-tuple-element.121), channel_id=1, source_target_pairs={{0,16},{1,9},{2,18},{3,11},{4,20},{5,13},{6,22},{7,15},{8,24},{9,1... | collective-permute-start | bytes 1769480 | tf_op jit(solution)/shard_map/ppermute | solution.py:1305
  256.1 17.7 %collective-permute-start.22 = (bf16[384,768]{1,0:T(8,128)(2,1)}, bf16[384,768]{1,0:T(8,128)(2,1)S(1)}, u32[]{:S(2)}, u32[]{:S(2)}) collective-permute-start(bf16[384,768]{1,0:T(8,128)(2,1)} %sums.5.refs_5_), channel_id=1, source_target_pairs={{0,8},{1,17},{2,10},{3,19},{4,12},{5,21},{6,14},{7,23},{8,0},{9,25... | collective-permute-start | bytes 1769480 | tf_op jit(solution)/shard_map/ppermute | solution.py:1305
  274.8 34.7 %collective-permute-start.26 = (bf16[4,2,96,768]{3,2,1,0:T(8,128)(2,1)}, bf16[4,2,96,768]{3,2,1,0:T(8,128)(2,1)S(1)}, u32[]{:S(2)}, u32[]{:S(2)}) collective-permute-start(bf16[4,2,96,768]{3,2,1,0:T(8,128)(2,1)} %get-tuple-element.131.refs_16_), channel_id=1, source_target_pairs={{0,8},{1,17},{2,10},{3,19},{4,12},{5,21},{6,14},{7,23},{8,0},{9,25... | collective-permute-start | bytes 3538952 | tf_op jit(solution)/shard_map/ppermute | solution.py:1305
  275.1 34.4 %collective-permute-start.27 = (bf16[4,2,96,768]{3,2,1,0:T(8,128)(2,1)}, bf16[4,2,96,768]{3,2,1,0:T(8,128)(2,1)S(1)}, u32[]{:S(2)}, u32[]{:S(2)}) collective-permute-start(bf16[4,2,96,768]{3,2,1,0:T(8,128)(2,1)} %get-tuple-element.132.refs_17_), channel_id=1, source_target_pairs={{0,16},{1,9},{2,18},{3,11},{4,20},{5,13},{6,22},{7,15},{8,24},{9,1... | collective-permute-start | bytes 3538952 | tf_op jit(solution)/shard_map/ppermute | solution.py:1305
  292.2 17.2 %all-to-all-start.1 = ((bf16[4,192,384]{2,1,0:T(8,128)(2,1)}), bf16[4,192,384]{2,1,0:T(8,128)(2,1)S(1)}, u32[]{:S(2)}, u32[]{:S(2)}) async-start(bf16[4,192,384]{2,1,0:T(8,128)(2,1)} %get-tuple-element.135), calls=%async_computation.1 | async-start | bytes 1179648 | tf_op jit(solution)/shard_map/all_to_all | solution.py:1450
  295.7 35.6 %reduce-scatter.10.cloned.1.call-start = ((), (), s32[]{:S(2)}) async-start(), calls=%async_computation.13 | async-start | bytes 1474560 | tf_op jit(solution)/shard_map/reduce_scatter | solution.py:1320
  295.8 19.3 %collective-permute-start.25 = (bf16[400,4608]{1,0:T(8,128)(2,1)}, bf16[400,4608]{1,0:T(8,128)(2,1)}, u32[]{:S(2)}, u32[]{:S(2)}) collective-permute-start(bf16[400,4608]{1,0:T(8,128)(2,1)} %get-tuple-element.137.refs_3_), channel_id=1, source_target_pairs={{0,1},{1,0},{2,3},{3,2},{4,5},{5,4},{6,7},{7,6},{8,9},{9,8},{10,11... | collective-permute-start | bytes 11059208 | tf_op jit(solution)/shard_map/ppermute | solution.py:1305
  296.3 71.0 %reduce-scatter.8.cloned.1.call-start = ((), (), s32[]{:S(2)}) async-start(), calls=%async_computation.12 | async-start | bytes 1474560 | tf_op jit(solution)/shard_map/reduce_scatter | solution.py:1320
  325.7 31.8 %collective-permute-start.32 = (bf16[4,2,96,768]{3,2,1,0:T(8,128)(2,1)}, bf16[4,2,96,768]{3,2,1,0:T(8,128)(2,1)S(1)}, u32[]{:S(2)}, u32[]{:S(2)}) collective-permute-start(bf16[4,2,96,768]{3,2,1,0:T(8,128)(2,1)} %get-tuple-element.149), channel_id=1, source_target_pairs={{0,16},{1,9},{2,18},{3,11},{4,20},{5,13},{6,22},{7,15},{8,24},{9,1... | collective-permute-start | bytes 3538952 | tf_op jit(solution)/shard_map/ppermute | solution.py:1305
  326.9 30.5 %collective-permute-start.33 = (bf16[4,2,96,768]{3,2,1,0:T(8,128)(2,1)}, bf16[4,2,96,768]{3,2,1,0:T(8,128)(2,1)S(1)}, u32[]{:S(2)}, u32[]{:S(2)}) collective-permute-start(bf16[4,2,96,768]{3,2,1,0:T(8,128)(2,1)} %get-tuple-element.150), channel_id=1, source_target_pairs={{0,16},{1,9},{2,18},{3,11},{4,20},{5,13},{6,22},{7,15},{8,24},{9,1... | collective-permute-start | bytes 3538952 | tf_op jit(solution)/shard_map/ppermute | solution.py:1305
  327.2 71.9 %reduce-scatter.14.cloned.1.call-start = ((), (), s32[]{:S(2)}) async-start(), calls=%async_computation.15 | async-start | bytes 1576960 | tf_op jit(solution)/shard_map/reduce_scatter | solution.py:1320
  331.3 35.9 %collective-permute-start.30 = (bf16[1,2,96,768]{3,2,1,0:T(8,128)(2,1)}, bf16[1,2,96,768]{3,2,1,0:T(8,128)(2,1)S(1)}, u32[]{:S(2)}, u32[]{:S(2)}) collective-permute-start(bf16[1,2,96,768]{3,2,1,0:T(8,128)(2,1)} %reduce-scatter.10.cloned.1.call-done), channel_id=1, source_target_pairs={{0,24},{1,25},{2,26},{3,27},{4,28},{5,29},{6,30},{7,31},{8,16},{9,... | collective-permute-start | bytes 884744 | tf_op jit(solution)/shard_map/ppermute | solution.py:1305
  363.2 17.1 %collective-permute-start.35 = (bf16[4,2,96,768]{3,2,1,0:T(8,128)(2,1)}, bf16[4,2,96,768]{3,2,1,0:T(8,128)(2,1)S(1)}, u32[]{:S(2)}, u32[]{:S(2)}) collective-permute-start(bf16[4,2,96,768]{3,2,1,0:T(8,128)(2,1)} %get-tuple-element.151.rest_0_), channel_id=1, source_target_pairs={{0,8},{1,17},{2,10},{3,19},{4,12},{5,21},{6,14},{7,23},{8,0},{9,25... | collective-permute-start | bytes 3538952 | tf_op jit(solution)/shard_map/ppermute | solution.py:1305
  367.2 72.3 %reduce-scatter.12.cloned.1.call-start = ((), (), s32[]{:S(2)}) async-start(), calls=%async_computation.14 | async-start | bytes 1474560 | tf_op jit(solution)/shard_map/reduce_scatter | solution.py:1320
  386.5 52.9 %collective-permute-start.44 = (bf16[208,1536]{1,0:T(8,128)(2,1)S(1)}, bf16[208,1536]{1,0:T(8,128)(2,1)}, u32[]{:S(2)}, u32[]{:S(2)}) collective-permute-start(bf16[208,1536]{1,0:T(8,128)(2,1)S(1)} %copy-done.14), channel_id=1, source_target_pairs={{0,24},{1,25},{2,26},{3,27},{4,28},{5,29},{6,30},{7,31},{8,16},{9,... | collective-permute-start | bytes 1916936 | tf_op jit(solution)/shard_map/ppermute | solution.py:1305
  388.4 51.1 %collective-permute-start.43 = (bf16[208,1536]{1,0:T(8,128)(2,1)S(1)}, bf16[208,1536]{1,0:T(8,128)(2,1)}, u32[]{:S(2)}, u32[]{:S(2)}) collective-permute-start(bf16[208,1536]{1,0:T(8,128)(2,1)S(1)} %copy-done.14), channel_id=1, source_target_pairs={{0,16},{1,9},{2,18},{3,11},{4,20},{5,13},{6,22},{7,15},{8,24},{9,1... | collective-permute-start | bytes 1916936 | tf_op jit(solution)/shard_map/ppermute | solution.py:1305
  388.8 52.0 %collective-permute-start.42 = (bf16[208,1536]{1,0:T(8,128)(2,1)S(1)}, bf16[208,1536]{1,0:T(8,128)(2,1)}, u32[]{:S(2)}, u32[]{:S(2)}) collective-permute-start(bf16[208,1536]{1,0:T(8,128)(2,1)S(1)} %copy-done.14), channel_id=1, source_target_pairs={{0,8},{1,17},{2,10},{3,19},{4,12},{5,21},{6,14},{7,23},{8,0},{9,25... | collective-permute-start | bytes 1916936 | tf_op jit(solution)/shard_map/ppermute | solution.py:1305
  389.2 48.9 %collective-permute-start.34 = (bf16[384,768]{1,0:T(8,128)(2,1)}, bf16[384,768]{1,0:T(8,128)(2,1)}, u32[]{:S(2)}, u32[]{:S(2)}) collective-permute-start(bf16[384,768]{1,0:T(8,128)(2,1)} %sums.8.refs_2_), channel_id=1, source_target_pairs={{0,8},{1,17},{2,10},{3,19},{4,12},{5,21},{6,14},{7,23},{8,0},{9,25... | collective-permute-start | bytes 1769480 | tf_op jit(solution)/shard_map/ppermute | solution.py:1305
  399.2 42.9 %collective-permute-start.41 = (bf16[112,1344]{1,0:T(8,128)(2,1)}, bf16[112,1344]{1,0:T(8,128)(2,1)S(1)}, u32[]{:S(2)}, u32[]{:S(2)}) collective-permute-start(bf16[112,1344]{1,0:T(8,128)(2,1)} %bitcast.40), channel_id=1, source_target_pairs={{0,24},{1,25},{2,26},{3,27},{4,28},{5,29},{6,30},{7,31},{8,16},{9,... | collective-permute-start | bytes 903176 | tf_op jit(solution)/shard_map/ppermute | solution.py:1305
  (66 other events, 576.6 us)
Sparse Core Ops, SparseCore 0:
  11.2 44.0 all-gather.5
  57.5 40.4 all-gather.7
  99.6 40.3 all-gather.9
  141.5 40.3 all-gather.11
  273.8 27.1 reduce-scatter.5
  303.3 27.9 reduce-scatter.9
  334.3 27.8 reduce-scatter.7
  367.3 31.8 reduce-scatter.13
  401.5 27.9 reduce-scatter.11
